TPU v7x, 32 devices: a whole 2x2x4 slice. The times are simulated.
32 devices in a mesh: seq: 4 (over y, x), head: 8 (over z, core).
Axes of the slice: x: 2, y: 2, z: 4, core: 2. Of those that a mesh axis runs over, the one named last changes fastest.
Arguments:
- x_heads: bfloat16 [2, 1024, 16384], P(None, 'seq', 'head'), may hold values from -6 to 6
- gate_z: bfloat16 [2, 1024, 16384], P(None, 'seq', 'head'), may hold values from -6 to 6
- b_proj: bfloat16 [2, 1024, 128], P(None, 'seq'), may hold values from -0.59765625 to 0.59765625
- c_proj: bfloat16 [2, 1024, 128], P(None, 'seq'), may hold values from -6 to 6
- dt_raw: float32 [2, 1024, 256], P(None, 'seq', 'head'), may hold values from -3 to 3
- dt_bias: float32 [2, 256], P(None, 'head'), may hold values from -1 to 0.5
- decay_rate: float32 [2, 256], P(None, 'head'), may hold values from 0 to 1, as said below
- skip_d: float32 [2, 256], P(None, 'head'), may hold values from 0.5 to 1.5
- norm_gain: float32 [2, 16384], P(None, 'head'), may hold values from 0.5 to 1.5
- w_out: bfloat16 [2, 16384, 8192], P(None, 'head', 'seq'), may hold values from -0.046875 to 0.046875
- seg_ids: int32 [1024], P('seq'), may hold values from 0 to 2, never falling along the last dimension, each value on 1 to 512 neighbouring positions
Outputs:
- mixed: bfloat16 [2, 1024, 8192], P(None, 'head', 'seq')
Inputs may be any that keep to these rules, and one draw needn't show every extreme that they name: `decay_rate`: Positive. `seg_ids`: document numbers start at 0, never fall along the sequence and take every value; one document has exactly 512 tokens.
All inputs are finite; a program needn't handle non-finite values.
Results may differ from a plain program's by a relative error of at most 0.019.
Values may be sent and summed in bfloat16 or wider, within the bound.
No kernel may reach another device: no remote copies, remote signals or barrier semaphores. Data moves between devices by JAX's collectives and lax.ppermute only.
A program may use at most 128 MiB of HBM per device.

v0:
```python
import functools
import jax
import jax.numpy as jnp
from jax import lax
from jax.experimental import pallas as pl
from jax.experimental.pallas import tpu as pltpu
from jax.sharding import PartitionSpec as P

F32, BF16 = jnp.float32, jnp.bfloat16
LANES = 128
EXTRA = 16
NEG = -1e30
EPS = 1e-05
IN_VMEM = pl.BlockSpec(memory_space=pltpu.VMEM)
ANYWHERE = pl.BlockSpec(memory_space=pl.ANY)
SCOPE = 16 * 1024 * 1024
HEAVY = 10**11


def dot(a, b):
    return jnp.dot(a, b, preferred_element_type=F32)


def call(kernel, name, operands, outs, far=(), after=(), carry=(), scratch=(), weight=1, **kw):
    given, idle = len(operands) + len(far), len(after) + len(carry)

    def body(*refs):
        rest = refs[given + idle :]
        return kernel(*refs[:given], *rest[: len(outs)], *rest[len(outs) + len(carry) :])

    return pl.pallas_call(
        body,
        name=name,
        in_specs=[IN_VMEM] * len(operands)
        + [ANYWHERE] * len(far)
        + [IN_VMEM] * len(after)
        + [ANYWHERE] * len(carry),
        out_specs=[IN_VMEM] * len(outs) + [ANYWHERE] * len(carry),
        out_shape=[pltpu.VMEM(shape, dtype) for shape, dtype in outs]
        + [jax.ShapeDtypeStruct(a.shape, a.dtype) for a in carry],
        scratch_shapes=list(scratch),
        input_output_aliases={given + len(after) + i: len(outs) + i for i in range(len(carry))},
        compiler_params=pltpu.CompilerParams(vmem_limit_bytes=SCOPE),
        cost_estimate=pl.CostEstimate(flops=weight, bytes_accessed=1, transcendentals=0),
        **kw,
    )(*operands, *far, *after, *carry)


def start_all(sems, pairs):
    fetches = [pltpu.make_async_copy(source, target, sems.at[i]) for i, (source, target) in enumerate(pairs)]
    for fetch in fetches:
        fetch.start()
    return fetches


def tiles(width):
    tile = min(512, width)
    return [slice(i, i + tile) for i in range(0, width, tile)]


def lane_split(head_size, shape):
    return lax.broadcasted_iota(jnp.int32, shape, 1) // head_size


def spread(values, lane_head, first):
    shape = (values.shape[0], LANES)
    out = jnp.broadcast_to(values[:, first : first + 1], shape)
    for k in range(1, lane_head[1]):
        out = jnp.where(lane_head[0] == k, values[:, first + k : first + k + 1], out)
    return out


def lane_heads(head_size):
    return (lane_split(head_size, (1, LANES)), LANES // head_size)


def column(row):
    return jnp.broadcast_to(row, (LANES, row.shape[1])).T[:, :1]


def head_column(row):
    heads = row.shape[1]
    padded = jnp.concatenate([row, jnp.zeros((1, LANES - heads), F32)], axis=1)
    return jnp.broadcast_to(padded, (LANES, LANES)).T[:heads, :1]


def turned(values):
    heads, rows = values.shape
    return jnp.concatenate([values, jnp.zeros((LANES - heads, rows), F32)], axis=0).T[:, :heads]


def prep_kernel(model, head_size, x_all, b_all, raw_all, bias_all, rate_all, skip_all, seg_all, msg_ref, run_ref, q_ref, step_ref, row_ref, *scratch):
    x_ref, b_ref, raw_ref, bias_ref, rate_ref, skip_ref, seg_ref, sems = scratch
    rows, channels = x_ref.shape[1:]
    mine = pl.ds(model, 1)
    cuts = tiles(channels)
    fetches = start_all(
        sems,
        [(raw_all.at[mine], raw_ref), (bias_all, bias_ref), (rate_all, rate_ref), (skip_all, skip_ref)]
        + [(seg_all, seg_ref), (b_all.at[mine], b_ref)]
        + [(x_all.at[mine, :, cut], x_ref.at[:, :, cut]) for cut in cuts],
    )
    for fetch in fetches[:6]:
        fetch.wait()
    heads = raw_ref.shape[1]
    state = b_ref.shape[2]
    step_t = jax.nn.softplus(raw_ref[0] + head_column(bias_ref[model : model + 1, :]))
    log_decay = -head_column(rate_ref[model : model + 1, :]) * step_t
    earlier = lax.broadcasted_iota(jnp.int32, (rows, rows), 0)
    later = lax.broadcasted_iota(jnp.int32, (rows, rows), 1)
    tri = (later >= earlier).astype(F32)
    run_t = jnp.dot(log_decay, tri, precision=lax.Precision.HIGHEST, preferred_element_type=F32)
    run, step = turned(run_t), turned(step_t)
    run_ref[:, :rows] = run_t
    run_ref[:, rows:] = jnp.broadcast_to(head_column(skip_ref[model : model + 1, :]), (heads, LANES))
    step_ref[...] = step_t
    q_ref[...] = run_t - jnp.log(step_t)
    seg_row = seg_ref[...].astype(F32)
    row_ref[...] = seg_row
    seg_col = column(seg_row)
    last = seg_row[:, rows - 1 :]
    total = run[rows - 1 :, :]
    tail = jnp.exp(total - run) * step * (seg_col == last).astype(F32)
    etot = jnp.exp(total)
    b_t = b_ref[0].astype(F32).T.astype(BF16)
    lane_head = lane_heads(head_size)
    row_id = lax.broadcasted_iota(jnp.int32, (EXTRA, LANES), 0)
    for p in range(channels // LANES):
        cols = slice(p * LANES, (p + 1) * LANES)
        first = p * lane_head[1]
        for cut, fetch in zip(cuts, fetches[6:]):
            if cut.start == cols.start:
                fetch.wait()
        xw = (x_ref[0, :, cols].astype(F32) * spread(tail, lane_head, first)).astype(BF16)
        msg_ref[:state, cols] = dot(b_t, xw).astype(BF16)
        decay = spread(etot, lane_head, first)
        high = decay.astype(BF16).astype(F32)
        extra = jnp.where(row_id == 0, high, jnp.where(row_id == 1, decay - high, jnp.where(row_id == 2, last, 0.0)))
        msg_ref[state:, cols] = extra.astype(BF16)


def prep(model, head_size, x, b, raw, bias, rate, skip, seg_row, after=()):
    _, rows, channels = x.shape
    heads, state = raw.shape[1], b.shape[2]
    far = (x, b, raw, bias, rate, skip, seg_row)
    return call(
        functools.partial(prep_kernel, model, head_size),
        f"prep_{model}",
        (),
        [((state + EXTRA, channels), BF16), ((heads, rows + LANES), F32), ((heads, rows), F32), ((heads, rows), F32), ((1, rows), F32)],
        far,
        after,
        scratch=[pltpu.VMEM((1,) + a.shape[1:] if a.ndim == 3 else a.shape, a.dtype) for a in far]
        + [pltpu.SemaphoreType.DMA((6 + len(tiles(channels)),))],
    )


def inside_kernel(model, head_size, run_ref, q_ref, step_ref, seg_ref, x_all, gate_all_, b_all, c_all, yg_ref, fg_ref, *scratch):
    x_ref, gate_ref, b_ref, c_ref, sems = scratch
    rows, channels = x_ref.shape[1:]
    mine = pl.ds(model, 1)
    cuts = tiles(channels)
    fetches = start_all(
        sems,
        [(b_all.at[mine], b_ref), (c_all.at[mine], c_ref)]
        + [pair for cut in cuts for pair in ((x_all.at[mine, :, cut], x_ref.at[:, :, cut]), (gate_all_.at[mine, :, cut], gate_ref.at[:, :, cut]))],
    )
    for fetch in fetches[:2]:
        fetch.wait()
    half = rows // 2
    lane_head = lane_heads(head_size)
    run, step, q = turned(run_ref[:, :rows]), turned(step_ref[...]), q_ref[...]
    skip = turned(run_ref[:, rows:])[:1]
    seg_row = seg_ref[...].astype(F32)
    seg_col = column(seg_row)

    products = lax.dot_general(c_ref[0], b_ref[0], (((1,), (1,)), ((), ())), preferred_element_type=F32)
    tri = lax.broadcasted_iota(jnp.int32, (half, half), 0) >= lax.broadcasted_iota(jnp.int32, (half, half), 1)
    parts = [slice(0, half), slice(half, rows)]
    masks = [tri & (seg_col[part] == seg_row[:, part]) for part in parts]
    diagonal = [products[part, part] for part in parts]
    below = jnp.where(seg_col[parts[1]] == seg_row[:, parts[0]], products[parts[1], parts[0]], 0.0).astype(BF16)
    middle = run[half - 1 : half, :]
    entry = jnp.exp(run[parts[1]] - middle)
    leave = jnp.exp(middle - run[parts[0]]) * step[parts[0]]
    factor = jnp.exp(run)
    for p in range(channels // LANES):
        cols = slice(p * LANES, (p + 1) * LANES)
        first = p * lane_head[1]
        for i, cut in enumerate(cuts):
            if cut.start == cols.start:
                fetches[2 + 2 * i].wait()
                fetches[3 + 2 * i].wait()
        x = x_ref[0, :, cols]
        xf = x.astype(F32)
        ys = []
        for part, mask, prod in zip(parts, masks, diagonal):
            y = None
            for k in range(lane_head[1]):
                h = first + k
                mixing = jnp.exp(jnp.where(mask, run[part, h : h + 1] - q[h : h + 1, part], NEG))
                term = dot((mixing * prod).astype(BF16), x[part])
                y = term if y is None else jnp.where(lane_head[0] == k, term, y)
            ys.append(y)
        sent = (xf[parts[0]] * spread(leave, lane_head, first)).astype(BF16)
        ys[1] = ys[1] + dot(below, sent) * spread(entry, lane_head, first)
        y = jnp.concatenate(ys, axis=0) + spread(skip, lane_head, first) * xf
        v = gate_ref[0, :, cols].astype(F32)
        silu = v / (1.0 + jnp.exp(-v))
        yg_ref[:, cols] = (y * silu).astype(BF16)
        fg_ref[:, cols] = (spread(factor, lane_head, first) * silu).astype(BF16)


def inside(model, head_size, x, gate, b, c, run, q, step, seg_row, after=()):
    _, rows, channels = x.shape
    far = (x, gate, b, c)
    return call(
        functools.partial(inside_kernel, model, head_size),
        f"inside_{model}",
        (run, q, step, seg_row),
        [((rows, channels), BF16)] * 2,
        far,
        after,
        scratch=[pltpu.VMEM((1,) + a.shape[1:], a.dtype) for a in far]
        + [pltpu.SemaphoreType.DMA((2 + 2 * len(tiles(channels)),))],
    )


def load_kernel(w_all, gain_all, w_ref, inverse_ref, gain_ref, sems):
    fetches = start_all(sems, [(gain_all, gain_ref)] + [(w_all.at[i], w_ref.at[i]) for i in range(w_all.shape[0])])
    fetches[0].wait()
    inverse_ref[...] = 1.0 / gain_ref[...]
    for fetch in fetches[1:]:
        fetch.wait()


def load(w, gain, after):
    return call(
        load_kernel,
        "load",
        (),
        [(w.shape, BF16), (gain.shape, F32)],
        (w, gain),
        after,
        scratch=[pltpu.VMEM(gain.shape, F32), pltpu.SemaphoreType.DMA((1 + w.shape[0],))],
    )


def join_kernel(state, own_ref, got_ref, out_ref):
    own, got = own_ref[...].astype(F32), got_ref[...].astype(F32)
    same = (own[state + 2 : state + 3] == got[state + 2 : state + 3]).astype(F32)
    decay = (own[state : state + 1] + own[state + 1 : state + 2]) * same
    out_ref[:state, :] = (own[:state] + decay * got[:state]).astype(BF16)
    out_ref[state:, :] = own_ref[state:, :]


def join(model, state, own, got, after=()):
    return call(functools.partial(join_kernel, state), f"join_{model}", (own, got), [(own.shape, BF16)], (), after)[0]


def gate_kernel(model, state, alone, near_ref, *refs):
    further = 7 if alone else 6
    far_refs, refs = refs[:-further], refs[-further:]
    c_ref, seg_ref, yg_ref, fg_ref, gain_ref, g_ref, *ss_ref = refs
    rows, channels = yg_ref.shape
    paired = True if alone else lax.axis_index("seq") % 2 == 1
    seg_col = column(seg_ref[...])
    squares = jnp.zeros((8, rows), F32)
    for cols in tiles(channels):
        near = near_ref[:, cols].astype(F32)
        far = far_refs[0][:, cols].astype(F32)
        for ref in far_refs[1:]:
            far = far + ref[:, cols].astype(F32)
        last_near, last_far = near[state + 2 : state + 3], far[state + 2 : state + 3]
        decay = (near[state : state + 1] + near[state + 1 : state + 2]) * (last_near == last_far).astype(F32)
        entering = (near[:state] + jnp.where(paired, decay, 1.0) * far[:state]).astype(BF16)
        anchor = jnp.where(paired, last_near, last_far)[:, :1]
        reached = (seg_col == anchor).astype(F32)
        gated = yg_ref[:, cols].astype(F32) + reached * fg_ref[:, cols].astype(F32) * dot(c_ref[model], entering)
        g_ref[:, cols] = (gated * gain_ref[model : model + 1, cols]).astype(BF16)
        if alone:
            ones = jnp.ones((8, cols.stop - cols.start), BF16)
            squares += lax.dot_general(
                ones, (gated * gated).astype(BF16), (((1,), (1,)), ((), ())), preferred_element_type=F32
            )
    if alone:
        ss_ref[0][...] = squares


def gate_all(model, alone, near, far, c, seg_row, yg, fg, gain, after=()):
    return call(
        functools.partial(gate_kernel, model, c.shape[2], alone),
        f"gated_{model}",
        (near, *far, c, seg_row, yg, fg, gain),
        [(yg.shape, BF16)] + [((8, yg.shape[0]), F32)] * alone,
        (),
        after,
    )


def project_kernel(model, shapes, forward, sends, *refs):
    given, (w_ref, inverse_ref, keep_ref, *refs) = refs[: sum(shapes)], refs[sum(shapes) :]
    count = len(shapes)
    half, width = keep_ref.shape[1], w_ref.shape[2]
    send_refs, (*refs, lhs) = refs[: len(sends)], refs[len(sends) :]
    first = lax.axis_index("head") % 2 == 0
    if forward:
        refs[0][...] = given[0][:half, :]
        refs[1][...] = given[1][half:, :]
    row = 0
    for ref in given:
        lhs[row : row + ref.shape[0], :] = ref[...]
        row += ref.shape[0]
    squares = jnp.zeros((row, LANES), F32)
    for part in tiles(w_ref.shape[1]):
        gated = lhs[:, part].astype(F32) * inverse_ref[model : model + 1, part]
        squares += dot((gated * gated).astype(BF16), jnp.ones((part.stop - part.start, LANES), BF16))

    def put(result, ref, blocks, start, at, size):
        for k in range(count):
            early = result[2 * k * half : (2 * k + 1) * half].astype(BF16)
            late = result[(2 * k + 1) * half : (2 * k + 2) * half].astype(BF16)
            keep_ref[k, :, pl.ds(start + at, size)] = jnp.where(first, early, late)
            which, place = (ref, blocks.index(k)) if k in blocks else (None, 0)
            if which is None:
                which, place = [(r, part.index(k)) for r, (part, *_) in zip(send_refs, sends) if k in part][0]
            which[place, :, pl.ds(at, size)] = jnp.where(first, late, early)

    tile = min(512, width)
    done = set()
    for ref, (blocks, start, stop) in zip(send_refs, sends):
        if start in done:
            continue
        done.add(start)

        def step(j, _, ref=ref, blocks=blocks, start=start):
            at = pl.multiple_of(j * tile, tile)
            put(dot(lhs[...], w_ref[model, :, pl.ds(start + at, tile)]), ref, blocks, start, at, tile)
            return 0

        lax.fori_loop(0, (min(stop, width) - start) // tile, step, 0)
        if stop > width:
            put(squares, ref, blocks, start, width - start, LANES)


def project(name, model, blocks, weights, after=(), forward=False, split=None, weight=1):
    w, inverse = weights
    flat = [a for block in blocks for a in block]
    depth, width = w.shape[1:]
    n, full = len(blocks), width + LANES
    half = sum(a.shape[0] for a in flat) // (2 * n)
    if split == "blocks":
        sends = [([k], 0, full) for k in range(n)]
    elif split == "columns":
        sends = [(list(range(n)), 0, width // 2), (list(range(n)), width // 2, full)]
    else:
        sends = [(list(range(n)), 0, full)]
    return call(
        functools.partial(project_kernel, model, [len(block) for block in blocks], forward, sends),
        name,
        (*flat, w, inverse),
        [((n, half, full), BF16)]
        + [((len(part), half, stop - start), BF16) for part, start, stop in sends]
        + [((half, depth), BF16)] * (2 * forward),
        (),
        after,
        scratch=[pltpu.VMEM((2 * half * n, depth), BF16)],
        weight=weight,
    )


def release(name, arrays, after, weight=1):
    return call(lambda *refs: None, name, (), [], (), after, carry=arrays, weight=weight)


def pair_kernel(places, counts, *refs):
    keeps, gots = refs[:2], (refs[2 : 2 + counts[0]], refs[2 + counts[0] : 2 + sum(counts)])
    first_ref, second_ref = refs[-2:]
    turned_round = (lax.axis_index("seq") // 2 + lax.axis_index("head") // 2) % 2 == 0

    def ends(pieces):
        stops = [0]
        for ref in pieces:
            stops.append(stops[-1] + ref.shape[2])
        return stops

    bounds = sorted({*ends(gots[0]), *ends(gots[1])})
    for start, stop in zip(bounds, bounds[1:]):
        sums = []
        for keep, pieces, (at, got_at) in zip(keeps, gots, places):
            stops = ends(pieces)
            piece = max(i for i, lower in enumerate(stops) if lower <= start)
            got = pieces[piece][got_at, :, start - stops[piece] : stop - stops[piece]]
            sums.append(keep[at, :, start:stop].astype(F32) + got.astype(F32))
        first_ref[:, start:stop] = jnp.where(turned_round, sums[1], sums[0]).astype(BF16)
        second_ref[:, start:stop] = jnp.where(turned_round, sums[0], sums[1]).astype(BF16)


def pair_sums(name, one, other, after=()):
    return call(
        functools.partial(pair_kernel, ((one[1], one[3]), (other[1], other[3])), (len(one[2]), len(other[2]))),
        name,
        (one[0], other[0], *one[2], *other[2]),
        [(one[0].shape[1:], BF16)] * 2,
        (),
        after,
    )


def add_kernel(own_ref, got_ref, out_ref):
    out_ref[...] = (own_ref[...].astype(F32) + got_ref[...].astype(F32)).astype(BF16)


def add(name, own, got, after=()):
    return call(add_kernel, name, (own, got), [(own.shape, BF16)], (), after)


def last_kernel(total, model, *refs):
    beside, opposite, out_ref = refs[:4], refs[4:8], refs[8]
    width = out_ref.shape[2]
    s, z = lax.axis_index("seq"), lax.axis_index("head") // 2
    straight = (s == z) | (s + z == 3)
    inner = (z == 1) | (z == 2)

    def write(refs):
        value = jnp.where(inner, refs[0][...], refs[1][...]).astype(F32)
        for ref in refs[2:]:
            value = value + ref[...].astype(F32)
        scale = lax.rsqrt(value[:, width : width + 1] / total + EPS)
        out_ref[0] = (value[:, :width] * scale).astype(BF16)

    pl.when(straight)(lambda: write(opposite))
    pl.when(~straight)(lambda: write(beside))


def last(model, total, beside, opposite, before, after=()):
    half, width = beside[0].shape[0], beside[0].shape[1] - LANES
    operands = (*beside, *opposite)
    earlier = () if before is None else (before,)
    kernel = functools.partial(last_kernel, total, model)
    return pl.pallas_call(
        lambda *refs: kernel(*refs[: len(operands)], refs[-1]),
        name=f"last_{model}",
        grid=(1,),
        in_specs=[IN_VMEM] * (len(operands) + len(after))
        + [ANYWHERE] * len(earlier),
        out_specs=pl.BlockSpec((1, half, width), lambda i: (model, 0, 0)),
        out_shape=jax.ShapeDtypeStruct((2, half, width), BF16),
        input_output_aliases={len(operands) + len(after): 0} if earlier else {},
        compiler_params=pltpu.CompilerParams(vmem_limit_bytes=SCOPE),
        cost_estimate=pl.CostEstimate(flops=1 if earlier else HEAVY, bytes_accessed=1, transcendentals=0),
    )(*operands, *after, *earlier)


def xor_pairs(n, k):
    return [(i, i ^ k) for i in range(n)]


def fast(x, gate, b, c, raw, bias, rate, skip, gain, w, seg):
    raw = jnp.swapaxes(raw, 1, 2)
    head_size = x.shape[2] // raw.shape[1]
    state = b.shape[2]
    n_seq, n_head = lax.axis_size("seq"), lax.axis_size("head")
    total = x.shape[2] * n_head
    seg_row = seg.reshape(1, -1)
    def flat(si, zi, ci):
        return si * n_head + zi * 2 + ci

    def sends(kinds, turn):
        pairs = []
        for si in range(n_seq):
            if 0 in [si ^ k for k in kinds]:
                steps = ([(1, 0), (3, 2), (2, 3), (0, 1)], [], [(2, 0), (1, 3)])[turn]
            else:
                steps = ([(0, 1), (3, 2)], [(0, 1), (3, 2)], [(1, 2), (2, 1)])[turn]
            pairs += [(flat(si, a, ci), flat(si, o, ci)) for a, o in steps for ci in range(2)]
        return pairs

    ring = [(0, 1), (2, 3)]
    across = lambda a: lax.ppermute(a, "head", xor_pairs(n_head, 1))
    beside = lambda a, k: lax.ppermute(a, "seq", xor_pairs(n_seq, k))
    ss = jnp.zeros((8, x.shape[1]), F32)

    x, gate, raw, bias, rate, skip, w = (
        pltpu.with_memory_space_constraint(a, pltpu.HBM) for a in (x, gate, raw, bias, rate, skip, w)
    )
    b_far, c_far, seg_far, gain_far = (pltpu.with_memory_space_constraint(a, pltpu.HBM) for a in (b, c, seg_row, gain))
    msg0, *scan0 = prep(0, head_size, x, b_far, raw, bias, rate, skip, seg_far)
    near0 = lax.ppermute(msg0, "seq", ring)
    msg1, *scan1 = prep(1, head_size, x, b_far, raw, bias, rate, skip, seg_far, (msg0, *scan0))
    near1 = lax.ppermute(msg1, "seq", ring)
    yg0, fg0 = inside(0, head_size, x, gate, b_far, c_far, *scan0, (msg0, msg1, *scan1))
    end0 = join(0, state, msg0, near0, (yg0, fg0, msg1, scan0[-1], *scan1))
    far0 = [lax.ppermute(end0, "seq", [(1, t)]) for t in (2, 3)]
    yg1, fg1 = inside(1, head_size, x, gate, b_far, c_far, *scan1, (end0, yg0, fg0, near0, msg1, scan0[-1]))
    end1 = join(1, state, msg1, near1, (yg0, fg0, near0, yg1, fg1, scan0[-1], scan1[-1], *far0))
    far1 = [lax.ppermute(end1, "seq", [(1, t)]) for t in (2, 3)]
    held = (near1, yg1, fg1, scan1[-1])
    w = load(w, gain_far, (end1, near0, yg0, fg0, scan0[-1], *far0, *held))
    g0, = gate_all(0, False, near0, far0, c, scan0[-1], yg0, fg0, gain, (*w, *far1, *held))
    x0, y0 = beside(g0, 1), beside(g0, 2)
    g1, = gate_all(1, False, near1, far1, c, scan1[-1], yg1, fg1, gain, (*w, g0))
    x1, y1 = beside(g1, 1), beside(g1, 2)

    def both(forwarded):
        return beside(forwarded[0], 2), beside(forwarded[1], 1)

    def turn(value, kinds, i):
        return lax.ppermute(value, ("seq", "head"), sends(kinds, i))

    xy, od = (1, 2), (0, 3)
    keep_n0, *send_n0, f0, l0 = project("next_0", 0, [(x0,), (y0,), (g0,)], w, (g1,), True, "blocks")
    got_n0 = [across(a) for a in send_n0]
    keep_o1, send_o1 = project("own_1", 1, [(g1,)], w, (keep_n0, f0, l0))
    held = (*w, keep_n0, keep_o1)
    first_n0, second_n0 = pair_sums(
        "sum_next_0", (keep_n0, 0, got_n0[:1], 0), (keep_n0, 1, got_n0[1:2], 0), (f0, l0, got_n0[2], send_o1, *held)
    )
    one_n0, two_n0 = turn(first_n0, xy, 0), turn(second_n0, xy, 1)
    got_o1 = across(send_o1)
    own0, own1 = (keep_n0, 2, got_n0[2:], 0), (keep_o1, 0, (got_o1,), 0)
    held = (*held, first_n0, got_n0[2])
    f0, l0 = release("release_0", (f0, l0), (x1, y1, second_n0, *held), HEAVY)
    d0 = both((f0, l0))
    held = (*held, second_n0)
    keep_n1, send_n1, f1, l1 = project("next_1", 1, [(x1,), (y1,)], w, (f0, *held), True)
    got_n1 = across(send_n1)
    held = (*held[:-1], keep_n1, f1, l1)
    join_n0, = add("add_next_0", second_n0, one_n0, (got_o1, *held))
    three_n0 = turn(join_n0, xy, 2)
    held = (*held[:-3], got_o1, join_n0)
    f1, l1 = release("release_1", (f1, l1), (*d0, keep_n1, *held))
    d1 = both((f1, l1))
    keep_n1, = release("gate_1", (keep_n1,), (f1, two_n0, *d0, *held), HEAVY)
    held = (*held, two_n0)
    first_n1, second_n1 = pair_sums("sum_next_1", (keep_n1, 0, (got_n1,), 0), (keep_n1, 1, (got_n1,), 1), (three_n0, *d0, *held))
    one_n1 = turn(first_n1, xy, 0)
    held = (*held, three_n0, first_n1, second_n1)
    keep_d0, *send_d0 = project("opposite_0", 0, [d0], w, held, False, "columns")
    got_d0 = [across(a) for a in send_d0]
    first_d0, second_d0 = pair_sums("sum_opposite_0", own0, (keep_d0, 0, got_d0, 0), held)
    one_d0, two_d0 = turn(first_d0, od, 0), turn(second_d0, od, 1)
    held = (keep_o1, got_o1, first_n0, join_n0, two_n0, three_n0, first_n1, second_n1, first_d0, second_d0)
    keep_d1, *send_d1 = project("opposite_1", 1, [d1], w, held, False, "columns", HEAVY)
    got_d1 = [across(a) for a in send_d1]
    first_d1, second_d1 = pair_sums("sum_opposite_1", own1, (keep_d1, 0, got_d1, 0), held)
    one_d1, two_d1 = turn(first_d1, od, 0), turn(second_d1, od, 1)
    held = (*held[2:], first_d1, second_d1)
    join_n1, = add("add_next_1", second_n1, one_n1, held)
    three_n1 = turn(join_n1, xy, 2)
    held = (*held, join_n1)
    join_d0, = add("add_opposite_0", second_d0, one_d0, held)
    three_d0 = turn(join_d0, od, 2)
    held = (*held, join_d0)
    join_d1, = add("add_opposite_1", second_d1, one_d1, (three_n1, *held))
    three_d1 = turn(join_d1, od, 2)
    second_n1, = release("release_2", (second_n1,), (join_d1, three_n1, first_n1, join_n1, first_d1))
    two_n1 = turn(second_n1, xy, 1)
    held = (first_n1, join_n1, three_n1, first_d1, join_d1)
    out = last(0, total, (first_n0, join_n0, two_n0, three_n0), (first_d0, join_d0, two_d0, three_d0), None, held)
    return last(1, total, (first_n1, join_n1, two_n1, three_n1), (first_d1, join_d1, two_d1, three_d1), out)


def plain(x, gate, b, c, raw, bias, rate, skip, gain, w, seg):
    raw = jnp.swapaxes(raw, 1, 2)
    head_size = x.shape[2] // raw.shape[1]
    state = b.shape[2]
    n_seq, n_head = lax.axis_size("seq"), lax.axis_size("head")
    total = x.shape[2] * n_head
    seg_row = seg.reshape(1, -1)
    s, h = lax.axis_index("seq"), lax.axis_index("head")
    gs, sums = [], []
    for m in range(2):
        msg, *scan = prep(m, head_size, x, b, raw, bias, rate, skip, seg_row)
        every = lax.all_gather(msg, "seq").astype(F32)
        entering, before = jnp.zeros_like(every[0]), every[0]
        for k in range(n_seq - 1):
            now = every[k]
            same = (now[state + 2] == before[state + 2]).astype(F32)
            decay = (now[state] + now[state + 1]) * same
            new = jnp.concatenate([now[:state] + decay * entering[:state], now[state:]])
            entering = jnp.where(k < s, new, entering)
            before = now
        yg, fg = inside(m, head_size, x, gate, b, c, *scan)
        near = entering.astype(BF16)
        g, ss = gate_all(m, True, near, [jnp.zeros_like(near)], c, scan[-1], yg, fg, gain)
        gs.append(g)
        sums.append(ss[0])
    g = lax.all_gather(jnp.stack(gs), "seq", axis=1, tiled=True)
    terms = jnp.einsum("mtk,mkd->mtd", g, w, preferred_element_type=F32)
    summed = lax.psum_scatter(terms.astype(BF16), "head", scatter_dimension=1, tiled=True)
    squares = lax.all_gather(lax.psum(jnp.stack(sums), "head"), "seq", axis=1, tiled=True)
    mine = lax.dynamic_slice_in_dim(squares, h * summed.shape[1], summed.shape[1], axis=1)
    return (summed.astype(F32) * lax.rsqrt(mine / total + EPS)[:, :, None]).astype(BF16)


def solution(mesh):
    placed = (
        P(None, "seq", "head"),
        P(None, "seq", "head"),
        P(None, "seq", None),
        P(None, "seq", None),
        P(None, "seq", "head"),
        P(None, "head"),
        P(None, "head"),
        P(None, "head"),
        P(None, "head"),
        P(None, "head", "seq"),
        P("seq"),
    )
    local = fast if mesh.shape["seq"] == 4 and mesh.shape["head"] == 8 else plain
    return jax.shard_map(
        local, mesh=mesh, in_specs=placed, out_specs=P(None, "head", "seq"), check_vma=False
    )
```

profile of v0, /device:TPU:0, one launch (start us, length us, event | category | flops | bytes accessed | tf_op | source)
XLA Modules:
  0.0 200.0 jit_solution(16062059979556645470)
XLA Ops:
  0.0 3.9 %prep_0.1 = (bf16[144,2048]{1,0:T(8,128)(2,1)S(1)}, f32[32,384]{1,0:T(8,128)S(1)}, f32[32,256]{1,0:T(8,128)S(1)}, f32[32,256]{1,0:T(8,128)S(1)}, f32[1,256]{1,0:T(1,128)S(1)}) custom-call(bf16[2,256,2048]{2,1,0:T(8,128)(2,1)} %refs_4_.7, bf16[2,256,128]{2,1,0:T(8,128)(2,1)} %refs_6_.3, f32[2,32,256]{2,1,0:T(8,128)} %bitcast.2, f32[2,32]{1,0:T(2,128)} %refs_3_.5, ...), custom_call_target="tpu_custom_call" | custom-call | flops 1 | bytes 1 | tf_op jit(solution)/shard_map/prep_0/pallas_call | solution.py:31
  4.0 4.9 %collective-permute-start.1 = (bf16[144,2048]{1,0:T(8,128)(2,1)S(1)}, bf16[144,2048]{1,0:T(8,128)(2,1)S(1)}, u32[]{:S(2)}, u32[]{:S(2)}) collective-permute-start(bf16[144,2048]{1,0:T(8,128)(2,1)S(1)} %get-tuple-element.51.refs_7_.refs_8_.refs_0_), channel_id=1, source_target_pairs={{0,8},{16,24},{1,9},{17,25},{2,10},{18,26},{3,11},{19,27},{4,12},{... | collective-permute-start | bytes 1769480 | tf_op jit(solution)/shard_map/ppermute | solution.py:489
  8.8 4.0 %prep_1.1 = (bf16[144,2048]{1,0:T(8,128)(2,1)S(1)}, f32[32,384]{1,0:T(8,128)S(1)}, f32[32,256]{1,0:T(8,128)S(1)}, f32[32,256]{1,0:T(8,128)S(1)}, f32[1,256]{1,0:T(1,128)S(1)}) custom-call(bf16[2,256,2048]{2,1,0:T(8,128)(2,1)} %refs_4_.7, bf16[2,256,128]{2,1,0:T(8,128)(2,1)} %refs_6_.3, f32[2,32,256]{2,1,0:T(8,128)} %bitcast.3, f32[2,32]{1,0:T(2,128)} %refs_3_.5, ...), custom_call_target="tpu_custom_call" | custom-call | flops 1 | bytes 1 | tf_op jit(solution)/shard_map/prep_1/pallas_call | solution.py:31
  12.8 1.3 collective-permute-start
  14.1 5.4 %inside_0.1 = (bf16[256,2048]{1,0:T(8,128)(2,1)S(1)}, bf16[256,2048]{1,0:T(8,128)(2,1)S(1)}) custom-call(f32[32,384]{1,0:T(8,128)S(1)} %get-tuple-element.52.refs_8_.refs_0_, f32[32,256]{1,0:T(8,128)S(1)} %get-tuple-element.53.refs_9_.refs_1_, f32[32,256]{1,0:T(8,128)S(1)} %get-tuple-element.54.refs_10_.refs_2_, ...), custom_call_target="tpu_custom_call" | custom-call | flops 1 | bytes 1 | tf_op jit(solution)/shard_map/inside_0/pallas_call | solution.py:31
  19.5 3.0 %collective-permute-done.1.refs_1_.refs_11_.refs_4_.refs_3_.refs_0_ = bf16[144,2048]{1,0:T(8,128)(2,1)S(1)} collective-permute-done((bf16[144,2048]{1,0:T(8,128)(2,1)S(1)}, bf16[144,2048]{1,0:T(8,128)(2,1)S(1)}, u32[]{:S(2)}, u32[]{:S(2)}) %collective-permute-start.1) | collective-permute-done | bytes 589856 | tf_op jit(solution)/shard_map/ppermute | solution.py:489
  22.5 0.2 join_0.1.refs_8_
  22.7 0.7 collective-permute-start.2
  23.4 0.9 collective-permute-start.3
  24.3 5.4 %inside_1.1 = (bf16[256,2048]{1,0:T(8,128)(2,1)S(1)}, bf16[256,2048]{1,0:T(8,128)(2,1)S(1)}) custom-call(f32[32,384]{1,0:T(8,128)S(1)} %get-tuple-element.57.refs_10_.refs_6_.refs_0_, f32[32,256]{1,0:T(8,128)S(1)} %get-tuple-element.58.refs_11_.refs_7_.refs_1_, f32[32,256]{1,0:T(8,128)S(1)} %get-tuple-element.59.refs_12_.refs_8_.refs_2_, ...), custom_call_target="tpu_custom_call" | custom-call | flops 1 | bytes 1 | tf_op jit(solution)/shard_map/inside_1/pallas_call | solution.py:31
  29.7 4.4 %collective-permute-done.refs_1_.refs_9_.refs_12_.refs_0_ = bf16[144,2048]{1,0:T(8,128)(2,1)S(1)} collective-permute-done((bf16[144,2048]{1,0:T(8,128)(2,1)S(1)}, bf16[144,2048]{1,0:T(8,128)(2,1)S(1)}, u32[]{:S(2)}, u32[]{:S(2)}) %collective-permute-start) | collective-permute-done | bytes 589856 | tf_op jit(solution)/shard_map/ppermute | solution.py:491
  34.0 0.2 join_1.1.refs_2_
  34.2 0.8 collective-permute-start.4
  35.1 0.7 collective-permute-start.5
  35.8 5.8 %load.1 = (bf16[2,2048,2048]{2,1,0:T(8,128)(2,1)S(1)}, f32[2,2048]{1,0:T(2,128)S(1)}) custom-call(bf16[2,2048,2048]{2,1,0:T(8,128)(2,1)} %refs_0_.5, f32[2,2048]{1,0:T(2,128)} %refs_7_.7, bf16[144,2048]{1,0:T(8,128)(2,1)S(1)} %join_1.1.refs_2_, bf16[144,2048]{1,0:T(8,128)(2,1)S(1)} %collective-permute-done.1.refs_1_.refs_11_.refs_4_.refs_3_.refs_0_, ...), custom_call_target="tpu_custom_call" | custom-call | flops 1 | bytes 1 | tf_op jit(solution)/shard_map/load/pallas_call | solution.py:31
  41.6 0.9 gated_0.1.refs_10_.refs_2_
  42.5 13.7 %collective-permute-start.8 = (bf16[256,2048]{1,0:T(8,128)(2,1)S(1)}, bf16[256,2048]{1,0:T(8,128)(2,1)S(1)}, u32[]{:S(2)}, u32[]{:S(2)}) collective-permute-start(bf16[256,2048]{1,0:T(8,128)(2,1)S(1)} %gated_0.1.refs_10_.refs_2_), channel_id=1, source_target_pairs={{0,8},{8,0},{16,24},{24,16},{1,9},{9,1},{17,25},{25,17},{2,10},{10... | collective-permute-start | bytes 3145736 | tf_op jit(solution)/shard_map/ppermute | solution.py:481
  56.2 2.5 %collective-permute-start.9 = (bf16[256,2048]{1,0:T(8,128)(2,1)S(1)}, bf16[256,2048]{1,0:T(8,128)(2,1)S(1)}, u32[]{:S(2)}, u32[]{:S(2)}) collective-permute-start(bf16[256,2048]{1,0:T(8,128)(2,1)S(1)} %gated_0.1.refs_10_.refs_2_), channel_id=1, source_target_pairs={{0,16},{8,24},{16,0},{24,8},{1,17},{9,25},{17,1},{25,9},{2,18},{10... | collective-permute-start | bytes 3145736 | tf_op jit(solution)/shard_map/ppermute | solution.py:481
  58.7 0.9 gated_1.1.refs_5_.refs_0_
  59.6 0.8 collective-permute-start.6
  60.3 20.0 %collective-permute-done.8.refs_0_ = bf16[256,2048]{1,0:T(8,128)(2,1)S(1)} collective-permute-done((bf16[256,2048]{1,0:T(8,128)(2,1)S(1)}, bf16[256,2048]{1,0:T(8,128)(2,1)S(1)}, u32[]{:S(2)}, u32[]{:S(2)}) %collective-permute-start.8) | collective-permute-done | bytes 1048608 | tf_op jit(solution)/shard_map/ppermute | solution.py:481
  80.3 2.5 %collective-permute-done.9.refs_1_ = bf16[256,2048]{1,0:T(8,128)(2,1)S(1)} collective-permute-done((bf16[256,2048]{1,0:T(8,128)(2,1)S(1)}, bf16[256,2048]{1,0:T(8,128)(2,1)S(1)}, u32[]{:S(2)}, u32[]{:S(2)}) %collective-permute-start.9) | collective-permute-done | bytes 1048608 | tf_op jit(solution)/shard_map/ppermute | solution.py:481
  82.8 8.2 %next_0.1 = (bf16[3,128,2176]{2,1,0:T(8,128)(2,1)S(1)}, bf16[1,128,2176]{2,1,0:T(8,128)(2,1)S(1)}, bf16[1,128,2176]{2,1,0:T(8,128)(2,1)S(1)}, bf16[1,128,2176]{2...) custom-call(bf16[256,2048]{1,0:T(8,128)(2,1)S(1)} %collective-permute-done.8.refs_0_, ...), custom_call_target="tpu_custom_call" | custom-call | flops 1 | bytes 1 | tf_op jit(solution)/shard_map/next_0/pallas_call | solution.py:31
  91.1 0.5 collective-permute-start.11
  91.7 3.3 %own_1.1 = (bf16[1,128,2176]{2,1,0:T(8,128)(2,1)S(1)}, bf16[1,128,2176]{2,1,0:T(8,128)(2,1)S(1)}) custom-call(bf16[256,2048]{1,0:T(8,128)(2,1)S(1)} %gated_1.1.refs_5_.refs_0_, bf16[2,2048,2048]{2,1,0:T(8,128)(2,1)S(1)} %get-tuple-element.65.refs_8_.refs_3_.refs_1_.refs_2_.refs_5_.refs_4_.refs_7_, ...), custom_call_target="tpu_custom_call" | custom-call | flops 1 | bytes 1 | tf_op jit(solution)/shard_map/own_1/pallas_call | solution.py:31
  95.0 0.5 collective-permute-start.15
  95.5 0.4 sum_next_0.1
  95.9 3.5 %collective-permute-start.16 = (bf16[128,2176]{1,0:T(8,128)(2,1)S(1)}, bf16[128,2176]{1,0:T(8,128)(2,1)S(1)}, u32[]{:S(2)}, u32[]{:S(2)}) collective-permute-start(bf16[128,2176]{1,0:T(8,128)(2,1)S(1)} %get-tuple-element.76.refs_7_.refs_9_.refs_8_.refs_11_.refs_6_.refs_2_.refs_3_.refs_0_), channel_id=1, source_target_pairs={{0,2},{1,3},{6,4},{7,5},{10,8},{11,9},{14,12},{15,13},{12,14},{13,... | collective-permute-start | bytes 1671176 | tf_op jit(solution)/shard_map/ppermute | solution.py:509
  99.4 1.5 collective-permute-start.17
  101.0 1.5 collective-permute-start.13
  102.5 1.3 collective-permute-start.14
  103.8 5.8 %next_1.1 = (bf16[2,128,2176]{2,1,0:T(8,128)(2,1)S(1)}, bf16[2,128,2176]{2,1,0:T(8,128)(2,1)S(1)}, bf16[128,2048]{1,0:T(8,128)(2,1)S(1)}, bf16[128,2048]{1,0:T(8,128)(2,1)S(1)}) custom-call(bf16[256,2048]{1,0:T(8,128)(2,1)S(1)} %collective-permute-done.6.refs_0_, bf16[256,2048]{1,0:T(8,128)(2,1)S(1)} %collective-permute-done.7.refs_1_, ...), custom_call_target="tpu_custom_call" | custom-call | flops 1 | bytes 1 | tf_op jit(solution)/shard_map/next_1/pallas_call | solution.py:31
  109.7 2.7 %collective-permute-done.16.refs_1_ = bf16[128,2176]{1,0:T(8,128)(2,1)S(1)} collective-permute-done((bf16[128,2176]{1,0:T(8,128)(2,1)S(1)}, bf16[128,2176]{1,0:T(8,128)(2,1)S(1)}, u32[]{:S(2)}, u32[]{:S(2)}) %collective-permute-start.16) | collective-permute-done | bytes 557088 | tf_op jit(solution)/shard_map/ppermute | solution.py:509
  112.4 0.1 add_next_0.1.refs_10_.refs_11_.refs_14_.refs_12_.refs_7_.refs_8_.refs_3_.refs_4_.refs_1_
  112.5 0.7 collective-permute-start.19
  113.2 1.5 collective-permute-done.13.refs_0_.refs_2_.refs_5_
  114.7 1.1 collective-permute-done.14.refs_1_.refs_3_.refs_6_
  115.8 0.6 collective-permute-start.23
  116.5 1.0 collective-permute-start.24
  117.5 5.9 %collective-permute-done.17.refs_1_.refs_15_.refs_12_.refs_13_.refs_8_.refs_9_.refs_4_.refs_5_.refs_2_ = bf16[128,2176]{1,0:T(8,128)(2,1)S(1)} collective-permute-done((bf16[128,2176]{1,0:T(8,128)(2,1)S(1)}, bf16[128,2176]{1,0:T(8,128)(2,1)S(1)}, u32[]{:S(2)}, u32[]{:S(2)}) %collective-permute-start.17) | collective-permute-done | bytes 557088 | tf_op jit(solution)/shard_map/ppermute | solution.py:509
  123.5 0.4 sum_next_1.1
  123.8 3.3 %opposite_0.1 = (bf16[1,128,2176]{2,1,0:T(8,128)(2,1)S(1)}, bf16[1,128,1024]{2,1,0:T(8,128)(2,1)S(1)}, bf16[1,128,1152]{2,1,0:T(8,128)(2,1)S(1)}) custom-call(bf16[128,2048]{1,0:T(8,128)(2,1)S(1)} %collective-permute-done.13.refs_0_.refs_2_.refs_5_, bf16[128,2048]{1,0:T(8,128)(2,1)S(1)} %collective-permute-done.14.refs_1_.refs_3_.refs_6_, ...), custom_call_target="tpu_custom_call" | custom-call | flops 1 | bytes 1 | tf_op jit(solution)/shard_map/opposite_0/pallas_call | solution.py:31
  127.3 0.5 collective-permute-start.21
  127.8 8.3 %collective-permute-start.20 = (bf16[128,2176]{1,0:T(8,128)(2,1)S(1)}, bf16[128,2176]{1,0:T(8,128)(2,1)S(1)}, u32[]{:S(2)}, u32[]{:S(2)}) collective-permute-start(bf16[128,2176]{1,0:T(8,128)(2,1)S(1)} %get-tuple-element.84.refs_14_.refs_15_.refs_10_.refs_11_.refs_6_.refs_7_.refs_2_.refs_8_.refs_0_), channel_id=1, source_target_pairs={{0,2},{1,3},{6,4},{7,5},{10,8},{11,9},{14,12},{15,13},{12,14},{13,... | collective-permute-start | bytes 1671176 | tf_op jit(solution)/shard_map/ppermute | solution.py:509
  136.1 0.4 sum_opposite_0.1
  136.4 1.9 collective-permute-start.29
  138.4 3.3 %opposite_1.1 = (bf16[1,128,2176]{2,1,0:T(8,128)(2,1)S(1)}, bf16[1,128,1024]{2,1,0:T(8,128)(2,1)S(1)}, bf16[1,128,1152]{2,1,0:T(8,128)(2,1)S(1)}) custom-call(bf16[128,2048]{1,0:T(8,128)(2,1)S(1)} %collective-permute-done.23.refs_0_, bf16[128,2048]{1,0:T(8,128)(2,1)S(1)} %collective-permute-done.24.refs_1_, ...), custom_call_target="tpu_custom_call" | custom-call | flops 99999997952 | bytes 1 | tf_op jit(solution)/shard_map/opposite_1/pallas_call | solution.py:31
  141.8 0.5 collective-permute-start.25
  142.3 1.4 collective-permute-done.25.refs_3_
  143.8 0.4 sum_opposite_1.1
  144.1 4.9 %collective-permute-done.20.refs_1_ = bf16[128,2176]{1,0:T(8,128)(2,1)S(1)} collective-permute-done((bf16[128,2176]{1,0:T(8,128)(2,1)S(1)}, bf16[128,2176]{1,0:T(8,128)(2,1)S(1)}, u32[]{:S(2)}, u32[]{:S(2)}) %collective-permute-start.20) | collective-permute-done | bytes 557088 | tf_op jit(solution)/shard_map/ppermute | solution.py:509
  149.0 0.1 add_next_1.1.refs_12_.refs_13_.refs_3_.refs_9_.refs_1_
  149.1 0.7 collective-permute-start.28
  149.8 7.2 %collective-permute-start.27 = (bf16[128,2176]{1,0:T(8,128)(2,1)S(1)}, bf16[128,2176]{1,0:T(8,128)(2,1)S(1)}, u32[]{:S(2)}, u32[]{:S(2)}) collective-permute-start(bf16[128,2176]{1,0:T(8,128)(2,1)S(1)} %get-tuple-element.95.refs_10_.refs_11_.refs_4_), channel_id=1, source_target_pairs={{2,0},{3,1},{6,4},{7,5},{4,6},{5,7},{0,2},{1,3},{8,10},{9,11},{14,... | collective-permute-start | bytes 1671176 | tf_op jit(solution)/shard_map/ppermute | solution.py:509
  157.0 0.7 collective-permute-start.33
  157.7 3.2 %collective-permute-done.29.refs_1_ = bf16[128,2176]{1,0:T(8,128)(2,1)S(1)} collective-permute-done((bf16[128,2176]{1,0:T(8,128)(2,1)S(1)}, bf16[128,2176]{1,0:T(8,128)(2,1)S(1)}, u32[]{:S(2)}, u32[]{:S(2)}) %collective-permute-start.29) | collective-permute-done | bytes 557088 | tf_op jit(solution)/shard_map/ppermute | solution.py:509
  161.1 1.3 collective-permute-start.34
  162.4 0.7 collective-permute-start.31
  163.1 22.7 %collective-permute-done.27.refs_1_ = bf16[128,2176]{1,0:T(8,128)(2,1)S(1)} collective-permute-done((bf16[128,2176]{1,0:T(8,128)(2,1)S(1)}, bf16[128,2176]{1,0:T(8,128)(2,1)S(1)}, u32[]{:S(2)}, u32[]{:S(2)}) %collective-permute-start.27) | collective-permute-done | bytes 557088 | tf_op jit(solution)/shard_map/ppermute | solution.py:509
  185.9 1.3 collective-permute-start.32
  187.2 4.5 %collective-permute-start.30 = (bf16[128,2176]{1,0:T(8,128)(2,1)S(1)}, bf16[128,2176]{1,0:T(8,128)(2,1)S(1)}, u32[]{:S(2)}, u32[]{:S(2)}) collective-permute-start(bf16[128,2176]{1,0:T(8,128)(2,1)S(1)} %release_2.1), channel_id=1, source_target_pairs={{0,2},{1,3},{6,4},{7,5},{24,26},{25,27},{30,28},{31,29}} | collective-permute-start | bytes 1671176 | tf_op jit(solution)/shard_map/ppermute | solution.py:509
  191.7 1.3 last_0.1.refs_8_
  193.0 5.7 %collective-permute-done.30.refs_2_ = bf16[128,2176]{1,0:T(8,128)(2,1)S(1)} collective-permute-done((bf16[128,2176]{1,0:T(8,128)(2,1)S(1)}, bf16[128,2176]{1,0:T(8,128)(2,1)S(1)}, u32[]{:S(2)}, u32[]{:S(2)}) %collective-permute-start.30) | collective-permute-done | bytes 557088 | tf_op jit(solution)/shard_map/ppermute | solution.py:509
  198.7 1.2 last_1.1
  (38 shorter events, 0.7 us)
Async XLA Ops:
  4.0 18.6 %collective-permute-start.1 = (bf16[144,2048]{1,0:T(8,128)(2,1)S(1)}, bf16[144,2048]{1,0:T(8,128)(2,1)S(1)}, u32[]{:S(2)}, u32[]{:S(2)}) collective-permute-start(bf16[144,2048]{1,0:T(8,128)(2,1)S(1)} %get-tuple-element.51.refs_7_.refs_8_.refs_0_), channel_id=1, source_target_pairs={{0,8},{16,24},{1,9},{17,25},{2,10},{18,26},{3,11},{19,27},{4,12},{... | collective-permute-start | bytes 1769480 | tf_op jit(solution)/shard_map/ppermute | solution.py:489
  12.8 21.2 %collective-permute-start = (bf16[144,2048]{1,0:T(8,128)(2,1)S(1)}, bf16[144,2048]{1,0:T(8,128)(2,1)S(1)}, u32[]{:S(2)}, u32[]{:S(2)}) collective-permute-start(bf16[144,2048]{1,0:T(8,128)(2,1)S(1)} %get-tuple-element.56.refs_9_.refs_4_.refs_12_.refs_0_), channel_id=1, source_target_pairs={{0,8},{16,24},{1,9},{17,25},{2,10},{18,26},{3,11},{19,27},{4,12},{... | collective-permute-start | bytes 1769480 | tf_op jit(solution)/shard_map/ppermute | solution.py:491
  22.7 11.3 %collective-permute-start.2 = (bf16[144,2048]{1,0:T(8,128)(2,1)S(1)}, bf16[144,2048]{1,0:T(8,128)(2,1)S(1)}, u32[]{:S(2)}, u32[]{:S(2)}) collective-permute-start(bf16[144,2048]{1,0:T(8,128)(2,1)S(1)} %join_0.1.refs_8_), channel_id=1, source_target_pairs={{8,16},{9,17},{10,18},{11,19},{12,20},{13,21},{14,22},{15,23}} | collective-permute-start | bytes 1769480 | tf_op jit(solution)/shard_map/ppermute | solution.py:494
  23.4 10.6 %collective-permute-start.3 = (bf16[144,2048]{1,0:T(8,128)(2,1)S(1)}, bf16[144,2048]{1,0:T(8,128)(2,1)S(1)}, u32[]{:S(2)}, u32[]{:S(2)}) collective-permute-start(bf16[144,2048]{1,0:T(8,128)(2,1)S(1)} %join_0.1.refs_8_), channel_id=1, source_target_pairs={{8,24},{9,25},{10,26},{11,27},{12,28},{13,29},{14,30},{15,31}} | collective-permute-start | bytes 1769480 | tf_op jit(solution)/shard_map/ppermute | solution.py:494
  34.2 7.4 %copy-start = (bf16[2,256,128]{2,1,0:T(8,128)(2,1)S(1)}, bf16[2,256,128]{2,1,0:T(8,128)(2,1)}, u32[]{:S(2)}) copy-start(bf16[2,256,128]{2,1,0:T(8,128)(2,1)} %refs_3_.7) | copy-start | bytes 393220
  34.2 7.4 %copy-start.1 = (f32[2,2048]{1,0:T(2,128)S(1)}, f32[2,2048]{1,0:T(2,128)}, u32[]{:S(2)}) copy-start(f32[2,2048]{1,0:T(2,128)} %refs_7_.7) | copy-start | bytes 49156
  34.2 7.4 %collective-permute-start.4 = (bf16[144,2048]{1,0:T(8,128)(2,1)S(1)}, bf16[144,2048]{1,0:T(8,128)(2,1)S(1)}, u32[]{:S(2)}, u32[]{:S(2)}) collective-permute-start(bf16[144,2048]{1,0:T(8,128)(2,1)S(1)} %join_1.1.refs_2_), channel_id=1, source_target_pairs={{8,16},{9,17},{10,18},{11,19},{12,20},{13,21},{14,22},{15,23}} | collective-permute-start | bytes 1769480 | tf_op jit(solution)/shard_map/ppermute | solution.py:497
  35.1 6.5 %collective-permute-start.5 = (bf16[144,2048]{1,0:T(8,128)(2,1)S(1)}, bf16[144,2048]{1,0:T(8,128)(2,1)S(1)}, u32[]{:S(2)}, u32[]{:S(2)}) collective-permute-start(bf16[144,2048]{1,0:T(8,128)(2,1)S(1)} %join_1.1.refs_2_), channel_id=1, source_target_pairs={{8,24},{9,25},{10,26},{11,27},{12,28},{13,29},{14,30},{15,31}} | collective-permute-start | bytes 1769480 | tf_op jit(solution)/shard_map/ppermute | solution.py:497
  42.5 37.8 %collective-permute-start.8 = (bf16[256,2048]{1,0:T(8,128)(2,1)S(1)}, bf16[256,2048]{1,0:T(8,128)(2,1)S(1)}, u32[]{:S(2)}, u32[]{:S(2)}) collective-permute-start(bf16[256,2048]{1,0:T(8,128)(2,1)S(1)} %gated_0.1.refs_10_.refs_2_), channel_id=1, source_target_pairs={{0,8},{8,0},{16,24},{24,16},{1,9},{9,1},{17,25},{25,17},{2,10},{10... | collective-permute-start | bytes 3145736 | tf_op jit(solution)/shard_map/ppermute | solution.py:481
  56.2 26.6 %collective-permute-start.9 = (bf16[256,2048]{1,0:T(8,128)(2,1)S(1)}, bf16[256,2048]{1,0:T(8,128)(2,1)S(1)}, u32[]{:S(2)}, u32[]{:S(2)}) collective-permute-start(bf16[256,2048]{1,0:T(8,128)(2,1)S(1)} %gated_0.1.refs_10_.refs_2_), channel_id=1, source_target_pairs={{0,16},{8,24},{16,0},{24,8},{1,17},{9,25},{17,1},{25,9},{2,18},{10... | collective-permute-start | bytes 3145736 | tf_op jit(solution)/shard_map/ppermute | solution.py:481
  59.6 41.4 %collective-permute-start.6 = (bf16[256,2048]{1,0:T(8,128)(2,1)S(1)}, bf16[256,2048]{1,0:T(8,128)(2,1)S(1)}, u32[]{:S(2)}, u32[]{:S(2)}) collective-permute-start(bf16[256,2048]{1,0:T(8,128)(2,1)S(1)} %gated_1.1.refs_5_.refs_0_), channel_id=1, source_target_pairs={{0,8},{8,0},{16,24},{24,16},{1,9},{9,1},{17,25},{25,17},{2,10},{10... | collective-permute-start | bytes 3145736 | tf_op jit(solution)/shard_map/ppermute | solution.py:481
  60.3 40.7 %collective-permute-start.7 = (bf16[256,2048]{1,0:T(8,128)(2,1)S(1)}, bf16[256,2048]{1,0:T(8,128)(2,1)S(1)}, u32[]{:S(2)}, u32[]{:S(2)}) collective-permute-start(bf16[256,2048]{1,0:T(8,128)(2,1)S(1)} %gated_1.1.refs_5_.refs_0_), channel_id=1, source_target_pairs={{0,16},{8,24},{16,0},{24,8},{1,17},{9,25},{17,1},{25,9},{2,18},{10... | collective-permute-start | bytes 3145736 | tf_op jit(solution)/shard_map/ppermute | solution.py:481
  91.0 4.0 %collective-permute-start.10 = (bf16[1,128,2176]{2,1,0:T(8,128)(2,1)S(1)}, bf16[1,128,2176]{2,1,0:T(8,128)(2,1)S(1)}, u32[]{:S(2)}, u32[]{:S(2)}) collective-permute-start(bf16[1,128,2176]{2,1,0:T(8,128)(2,1)S(1)} %get-tuple-element.68), channel_id=1, source_target_pairs={{0,1},{1,0},{2,3},{3,2},{4,5},{5,4},{6,7},{7,6},{8,9},{9,8},{10,11... | collective-permute-start | bytes 1671176 | tf_op jit(solution)/shard_map/ppermute | solution.py:480
  91.1 4.4 %collective-permute-start.11 = (bf16[1,128,2176]{2,1,0:T(8,128)(2,1)S(1)}, bf16[1,128,2176]{2,1,0:T(8,128)(2,1)S(1)}, u32[]{:S(2)}, u32[]{:S(2)}) collective-permute-start(bf16[1,128,2176]{2,1,0:T(8,128)(2,1)S(1)} %get-tuple-element.69), channel_id=1, source_target_pairs={{0,1},{1,0},{2,3},{3,2},{4,5},{5,4},{6,7},{7,6},{8,9},{9,8},{10,11... | collective-permute-start | bytes 1671176 | tf_op jit(solution)/shard_map/ppermute | solution.py:480
  91.6 3.9 %collective-permute-start.12 = (bf16[1,128,2176]{2,1,0:T(8,128)(2,1)S(1)}, bf16[1,128,2176]{2,1,0:T(8,128)(2,1)S(1)}, u32[]{:S(2)}, u32[]{:S(2)}) collective-permute-start(bf16[1,128,2176]{2,1,0:T(8,128)(2,1)S(1)} %get-tuple-element.72), channel_id=1, source_target_pairs={{0,1},{1,0},{2,3},{3,2},{4,5},{5,4},{6,7},{7,6},{8,9},{9,8},{10,11... | collective-permute-start | bytes 1671176 | tf_op jit(solution)/shard_map/ppermute | solution.py:480
  95.0 14.6 %collective-permute-start.15 = (bf16[1,128,2176]{2,1,0:T(8,128)(2,1)S(1)}, bf16[1,128,2176]{2,1,0:T(8,128)(2,1)S(1)}, u32[]{:S(2)}, u32[]{:S(2)}) collective-permute-start(bf16[1,128,2176]{2,1,0:T(8,128)(2,1)S(1)} %get-tuple-element.73.refs_7_), channel_id=1, source_target_pairs={{0,1},{1,0},{2,3},{3,2},{4,5},{5,4},{6,7},{7,6},{8,9},{9,8},{10,11... | collective-permute-start | bytes 1671176 | tf_op jit(solution)/shard_map/ppermute | solution.py:480
  95.9 16.5 %collective-permute-start.16 = (bf16[128,2176]{1,0:T(8,128)(2,1)S(1)}, bf16[128,2176]{1,0:T(8,128)(2,1)S(1)}, u32[]{:S(2)}, u32[]{:S(2)}) collective-permute-start(bf16[128,2176]{1,0:T(8,128)(2,1)S(1)} %get-tuple-element.76.refs_7_.refs_9_.refs_8_.refs_11_.refs_6_.refs_2_.refs_3_.refs_0_), channel_id=1, source_target_pairs={{0,2},{1,3},{6,4},{7,5},{10,8},{11,9},{14,12},{15,13},{12,14},{13,... | collective-permute-start | bytes 1671176 | tf_op jit(solution)/shard_map/ppermute | solution.py:509
  99.4 24.0 %collective-permute-start.17 = (bf16[128,2176]{1,0:T(8,128)(2,1)S(1)}, bf16[128,2176]{1,0:T(8,128)(2,1)S(1)}, u32[]{:S(2)}, u32[]{:S(2)}) collective-permute-start(bf16[128,2176]{1,0:T(8,128)(2,1)S(1)} %get-tuple-element.75.refs_2_.refs_11_.refs_0_), channel_id=1, source_target_pairs={{0,2},{1,3},{6,4},{7,5},{24,26},{25,27},{30,28},{31,29}} | collective-permute-start | bytes 1671176 | tf_op jit(solution)/shard_map/ppermute | solution.py:509
  101.0 13.7 %collective-permute-start.13 = (bf16[128,2048]{1,0:T(8,128)(2,1)S(1)}, bf16[128,2048]{1,0:T(8,128)(2,1)S(1)}, u32[]{:S(2)}, u32[]{:S(2)}) collective-permute-start(bf16[128,2048]{1,0:T(8,128)(2,1)S(1)} %get-tuple-element.77.refs_4_), channel_id=1, source_target_pairs={{0,16},{8,24},{16,0},{24,8},{1,17},{9,25},{17,1},{25,9},{2,18},{10... | collective-permute-start | bytes 1572872 | tf_op jit(solution)/shard_map/ppermute | solution.py:481
  102.5 13.4 %collective-permute-start.14 = (bf16[128,2048]{1,0:T(8,128)(2,1)S(1)}, bf16[128,2048]{1,0:T(8,128)(2,1)S(1)}, u32[]{:S(2)}, u32[]{:S(2)}) collective-permute-start(bf16[128,2048]{1,0:T(8,128)(2,1)S(1)} %get-tuple-element.78), channel_id=1, source_target_pairs={{0,8},{8,0},{16,24},{24,16},{1,9},{9,1},{17,25},{25,17},{2,10},{10... | collective-permute-start | bytes 1572872 | tf_op jit(solution)/shard_map/ppermute | solution.py:481
  109.6 13.8 %collective-permute-start.18 = (bf16[2,128,2176]{2,1,0:T(8,128)(2,1)S(1)}, bf16[2,128,2176]{2,1,0:T(8,128)(2,1)S(1)}, u32[]{:S(2)}, u32[]{:S(2)}) collective-permute-start(bf16[2,128,2176]{2,1,0:T(8,128)(2,1)S(1)} %get-tuple-element.83), channel_id=1, source_target_pairs={{0,1},{1,0},{2,3},{3,2},{4,5},{5,4},{6,7},{7,6},{8,9},{9,8},{10,11... | collective-permute-start | bytes 3342344 | tf_op jit(solution)/shard_map/ppermute | solution.py:480
  112.5 10.9 %collective-permute-start.19 = (bf16[128,2176]{1,0:T(8,128)(2,1)S(1)}, bf16[128,2176]{1,0:T(8,128)(2,1)S(1)}, u32[]{:S(2)}, u32[]{:S(2)}) collective-permute-start(bf16[128,2176]{1,0:T(8,128)(2,1)S(1)} %add_next_0.1.refs_10_.refs_11_.refs_14_.refs_12_.refs_7_.refs_8_.refs_3_.refs_4_.refs_1_), channel_id=1, source_target_pairs={{2,4},{3,5},{4,2},{5,3},{12,8},{13,9},{10,14},{11,15},{20,16},{21,... | collective-permute-start | bytes 1671176 | tf_op jit(solution)/shard_map/ppermute | solution.py:509
  115.8 22.5 %collective-permute-start.23 = (bf16[128,2048]{1,0:T(8,128)(2,1)S(1)}, bf16[128,2048]{1,0:T(8,128)(2,1)S(1)}, u32[]{:S(2)}, u32[]{:S(2)}) collective-permute-start(bf16[128,2048]{1,0:T(8,128)(2,1)S(1)} %get-tuple-element.82.refs_0_), channel_id=1, source_target_pairs={{0,16},{8,24},{16,0},{24,8},{1,17},{9,25},{17,1},{25,9},{2,18},{10... | collective-permute-start | bytes 1572872 | tf_op jit(solution)/shard_map/ppermute | solution.py:481
  116.5 21.9 %collective-permute-start.24 = (bf16[128,2048]{1,0:T(8,128)(2,1)S(1)}, bf16[128,2048]{1,0:T(8,128)(2,1)S(1)}, u32[]{:S(2)}, u32[]{:S(2)}) collective-permute-start(bf16[128,2048]{1,0:T(8,128)(2,1)S(1)} %get-tuple-element.91), channel_id=1, source_target_pairs={{0,8},{8,0},{16,24},{24,16},{1,9},{9,1},{17,25},{25,17},{2,10},{10... | collective-permute-start | bytes 1572872 | tf_op jit(solution)/shard_map/ppermute | solution.py:481
  127.2 8.9 %collective-permute-start.22 = (bf16[1,128,1152]{2,1,0:T(8,128)(2,1)S(1)}, bf16[1,128,1152]{2,1,0:T(8,128)(2,1)S(1)}, u32[]{:S(2)}, u32[]{:S(2)}) collective-permute-start(bf16[1,128,1152]{2,1,0:T(8,128)(2,1)S(1)} %get-tuple-element.88), channel_id=1, source_target_pairs={{0,1},{1,0},{2,3},{3,2},{4,5},{5,4},{6,7},{7,6},{8,9},{9,8},{10,11... | collective-permute-start | bytes 884744 | tf_op jit(solution)/shard_map/ppermute | solution.py:480
  127.3 8.8 %collective-permute-start.21 = (bf16[1,128,1024]{2,1,0:T(8,128)(2,1)S(1)}, bf16[1,128,1024]{2,1,0:T(8,128)(2,1)S(1)}, u32[]{:S(2)}, u32[]{:S(2)}) collective-permute-start(bf16[1,128,1024]{2,1,0:T(8,128)(2,1)S(1)} %get-tuple-element.87), channel_id=1, source_target_pairs={{0,1},{1,0},{2,3},{3,2},{4,5},{5,4},{6,7},{7,6},{8,9},{9,8},{10,11... | collective-permute-start | bytes 786440 | tf_op jit(solution)/shard_map/ppermute | solution.py:480
  127.8 21.2 %collective-permute-start.20 = (bf16[128,2176]{1,0:T(8,128)(2,1)S(1)}, bf16[128,2176]{1,0:T(8,128)(2,1)S(1)}, u32[]{:S(2)}, u32[]{:S(2)}) collective-permute-start(bf16[128,2176]{1,0:T(8,128)(2,1)S(1)} %get-tuple-element.84.refs_14_.refs_15_.refs_10_.refs_11_.refs_6_.refs_7_.refs_2_.refs_8_.refs_0_), channel_id=1, source_target_pairs={{0,2},{1,3},{6,4},{7,5},{10,8},{11,9},{14,12},{15,13},{12,14},{13,... | collective-permute-start | bytes 1671176 | tf_op jit(solution)/shard_map/ppermute | solution.py:509
  136.4 24.5 %collective-permute-start.29 = (bf16[128,2176]{1,0:T(8,128)(2,1)S(1)}, bf16[128,2176]{1,0:T(8,128)(2,1)S(1)}, u32[]{:S(2)}, u32[]{:S(2)}) collective-permute-start(bf16[128,2176]{1,0:T(8,128)(2,1)S(1)} %get-tuple-element.89.refs_12_.refs_13_.refs_8_.refs_9_.refs_4_), channel_id=1, source_target_pairs={{2,0},{3,1},{6,4},{7,5},{4,6},{5,7},{0,2},{1,3},{8,10},{9,11},{14,... | collective-permute-start | bytes 1671176 | tf_op jit(solution)/shard_map/ppermute | solution.py:509
  141.7 2.0 %collective-permute-start.26 = (bf16[1,128,1152]{2,1,0:T(8,128)(2,1)S(1)}, bf16[1,128,1152]{2,1,0:T(8,128)(2,1)S(1)}, u32[]{:S(2)}, u32[]{:S(2)}) collective-permute-start(bf16[1,128,1152]{2,1,0:T(8,128)(2,1)S(1)} %get-tuple-element.94), channel_id=1, source_target_pairs={{0,1},{1,0},{2,3},{3,2},{4,5},{5,4},{6,7},{7,6},{8,9},{9,8},{10,11... | collective-permute-start | bytes 884744 | tf_op jit(solution)/shard_map/ppermute | solution.py:480
  141.8 1.9 collective-permute-start.25
  149.1 13.9 %collective-permute-start.28 = (bf16[128,2176]{1,0:T(8,128)(2,1)S(1)}, bf16[128,2176]{1,0:T(8,128)(2,1)S(1)}, u32[]{:S(2)}, u32[]{:S(2)}) collective-permute-start(bf16[128,2176]{1,0:T(8,128)(2,1)S(1)} %add_next_1.1.refs_12_.refs_13_.refs_3_.refs_9_.refs_1_), channel_id=1, source_target_pairs={{2,4},{3,5},{4,2},{5,3},{12,8},{13,9},{10,14},{11,15},{20,16},{21,... | collective-permute-start | bytes 1671176 | tf_op jit(solution)/shard_map/ppermute | solution.py:509
  149.8 36.0 %collective-permute-start.27 = (bf16[128,2176]{1,0:T(8,128)(2,1)S(1)}, bf16[128,2176]{1,0:T(8,128)(2,1)S(1)}, u32[]{:S(2)}, u32[]{:S(2)}) collective-permute-start(bf16[128,2176]{1,0:T(8,128)(2,1)S(1)} %get-tuple-element.95.refs_10_.refs_11_.refs_4_), channel_id=1, source_target_pairs={{2,0},{3,1},{6,4},{7,5},{4,6},{5,7},{0,2},{1,3},{8,10},{9,11},{14,... | collective-permute-start | bytes 1671176 | tf_op jit(solution)/shard_map/ppermute | solution.py:509
  157.0 34.7 %collective-permute-start.33 = (bf16[128,2176]{1,0:T(8,128)(2,1)S(1)}, bf16[128,2176]{1,0:T(8,128)(2,1)S(1)}, u32[]{:S(2)}, u32[]{:S(2)}) collective-permute-start(bf16[128,2176]{1,0:T(8,128)(2,1)S(1)} %get-tuple-element.90.refs_13_.refs_14_.refs_9_.refs_0_.refs_10_), channel_id=1, source_target_pairs={{8,10},{9,11},{14,12},{15,13},{16,18},{17,19},{22,20},{23,21}} | collective-permute-start | bytes 1671176 | tf_op jit(solution)/shard_map/ppermute | solution.py:509
  161.1 30.7 %collective-permute-start.34 = (bf16[128,2176]{1,0:T(8,128)(2,1)S(1)}, bf16[128,2176]{1,0:T(8,128)(2,1)S(1)}, u32[]{:S(2)}, u32[]{:S(2)}) collective-permute-start(bf16[128,2176]{1,0:T(8,128)(2,1)S(1)} %add_opposite_0.1.refs_14_.refs_5_), channel_id=1, source_target_pairs={{4,0},{5,1},{2,6},{3,7},{10,12},{11,13},{12,10},{13,11},{18,20},{1... | collective-permute-start | bytes 1671176 | tf_op jit(solution)/shard_map/ppermute | solution.py:509
  162.4 30.7 %collective-permute-start.31 = (bf16[128,2176]{1,0:T(8,128)(2,1)S(1)}, bf16[128,2176]{1,0:T(8,128)(2,1)S(1)}, u32[]{:S(2)}, u32[]{:S(2)}) collective-permute-start(bf16[128,2176]{1,0:T(8,128)(2,1)S(1)} %get-tuple-element.96.refs_11_.refs_0_.refs_12_), channel_id=1, source_target_pairs={{8,10},{9,11},{14,12},{15,13},{16,18},{17,19},{22,20},{23,21}} | collective-permute-start | bytes 1671176 | tf_op jit(solution)/shard_map/ppermute | solution.py:509
  185.9 12.8 %collective-permute-start.32 = (bf16[128,2176]{1,0:T(8,128)(2,1)S(1)}, bf16[128,2176]{1,0:T(8,128)(2,1)S(1)}, u32[]{:S(2)}, u32[]{:S(2)}) collective-permute-start(bf16[128,2176]{1,0:T(8,128)(2,1)S(1)} %add_opposite_1.1.refs_0_.refs_12_.refs_5_), channel_id=1, source_target_pairs={{4,0},{5,1},{2,6},{3,7},{10,12},{11,13},{12,10},{13,11},{18,20},{1... | collective-permute-start | bytes 1671176 | tf_op jit(solution)/shard_map/ppermute | solution.py:509
  187.2 11.5 %collective-permute-start.30 = (bf16[128,2176]{1,0:T(8,128)(2,1)S(1)}, bf16[128,2176]{1,0:T(8,128)(2,1)S(1)}, u32[]{:S(2)}, u32[]{:S(2)}) collective-permute-start(bf16[128,2176]{1,0:T(8,128)(2,1)S(1)} %release_2.1), channel_id=1, source_target_pairs={{0,2},{1,3},{6,4},{7,5},{24,26},{25,27},{30,28},{31,29}} | collective-permute-start | bytes 1671176 | tf_op jit(solution)/shard_map/ppermute | solution.py:509
where the time goes:
time: 200 us
  waiting for transfers between devices  79 us (40%)
  starting transfers between devices  65.3 us (33%)
  Pallas kernels  55.1 us (28%)
    pallas_call x26, Pallas kernels, call(): pl.pallas_call(body, name=name, in_specs=[IN_VMEM] * len(operands) + [ANY...  52.6 us
    ppermute x12, waiting for transfers between devices, turn(): return lax.ppermute(value, ('seq', 'head'), sends(kinds, i))  45.1 us
    ppermute x12, starting transfers between devices, turn(): return lax.ppermute(value, ('seq', 'head'), sends(kinds, i))  32.3 us
    ppermute x8, waiting for transfers between devices, fast(): beside = lambda a, k: lax.ppermute(a, 'seq', xor_pairs(n_seq, k))  25.1 us
    ppermute x8, starting transfers between devices, fast(): beside = lambda a, k: lax.ppermute(a, 'seq', xor_pairs(n_seq, k))  21.4 us
    ppermute x1, starting transfers between devices, fast(): near0 = lax.ppermute(msg0, 'seq', ring)  4.88 us
    ppermute x1, waiting for transfers between devices, fast(): near1 = lax.ppermute(msg1, 'seq', ring)  4.35 us
  transfers between devices with their start and end apart: 35, of which 13 were waited for; matrix products, arithmetic and copies ran while one was open for 0% of the time, Pallas kernels for 24%

commit v1 on v0

--- a/solution.py
+++ b/solution.py
@@ -509,17 +509,19 @@
         return lax.ppermute(value, ("seq", "head"), sends(kinds, i))
 
     xy, od = (1, 2), (0, 3)
-    keep_n0, *send_n0, f0, l0 = project("next_0", 0, [(x0,), (y0,), (g0,)], w, (g1,), True, "blocks")
+    keep_o0, send_o0 = project("own_0", 0, [(g0,)], w, (g1,))
+    keep_o1, send_o1 = project("own_1", 1, [(g1,)], w, (keep_o0, send_o0))
+    held = (*w, keep_o0, keep_o1, send_o1)
+    keep_n0, *send_n0, f0, l0 = project("next_0", 0, [(x0,), (y0,)], w, (send_o0, *held), True, "blocks")
     got_n0 = [across(a) for a in send_n0]
-    keep_o1, send_o1 = project("own_1", 1, [(g1,)], w, (keep_n0, f0, l0))
-    held = (*w, keep_n0, keep_o1)
+    got_o0 = across(send_o0)
     first_n0, second_n0 = pair_sums(
-        "sum_next_0", (keep_n0, 0, got_n0[:1], 0), (keep_n0, 1, got_n0[1:2], 0), (f0, l0, got_n0[2], send_o1, *held)
+        "sum_next_0", (keep_n0, 0, got_n0[:1], 0), (keep_n0, 1, got_n0[1:], 0), (f0, l0, got_o0, *held)
     )
     one_n0, two_n0 = turn(first_n0, xy, 0), turn(second_n0, xy, 1)
     got_o1 = across(send_o1)
-    own0, own1 = (keep_n0, 2, got_n0[2:], 0), (keep_o1, 0, (got_o1,), 0)
-    held = (*held, first_n0, got_n0[2])
+    own0, own1 = (keep_o0, 0, (got_o0,), 0), (keep_o1, 0, (got_o1,), 0)
+    held = (*w, keep_o0, keep_o1, first_n0, got_o0)
     f0, l0 = release("release_0", (f0, l0), (x1, y1, second_n0, *held), HEAVY)
     d0 = both((f0, l0))
     held = (*held, second_n0)
@@ -533,28 +535,31 @@
     d1 = both((f1, l1))
     keep_n1, = release("gate_1", (keep_n1,), (f1, two_n0, *d0, *held), HEAVY)
     held = (*held, two_n0)
-    first_n1, second_n1 = pair_sums("sum_next_1", (keep_n1, 0, (got_n1,), 0), (keep_n1, 1, (got_n1,), 1), (three_n0, *d0, *held))
-    one_n1 = turn(first_n1, xy, 0)
-    held = (*held, three_n0, first_n1, second_n1)
+    first_n1, second_n1 = pair_sums(
+        "sum_next_1", (keep_n1, 0, (got_n1,), 0), (keep_n1, 1, (got_n1,), 1), (*d0, *held)
+    )
+    held = (*held, first_n1, second_n1)
     keep_d0, *send_d0 = project("opposite_0", 0, [d0], w, held, False, "columns")
     got_d0 = [across(a) for a in send_d0]
     first_d0, second_d0 = pair_sums("sum_opposite_0", own0, (keep_d0, 0, got_d0, 0), held)
     one_d0, two_d0 = turn(first_d0, od, 0), turn(second_d0, od, 1)
+    first_n1, = release("release_n1", (first_n1,), (first_d0, second_d0, *held[:-2], second_n1))
+    one_n1 = turn(first_n1, xy, 0)
     held = (keep_o1, got_o1, first_n0, join_n0, two_n0, three_n0, first_n1, second_n1, first_d0, second_d0)
     keep_d1, *send_d1 = project("opposite_1", 1, [d1], w, held, False, "columns", HEAVY)
     got_d1 = [across(a) for a in send_d1]
     first_d1, second_d1 = pair_sums("sum_opposite_1", own1, (keep_d1, 0, got_d1, 0), held)
     one_d1, two_d1 = turn(first_d1, od, 0), turn(second_d1, od, 1)
     held = (*held[2:], first_d1, second_d1)
+    join_d0, = add("add_opposite_0", second_d0, one_d0, held)
+    three_d0 = turn(join_d0, od, 2)
+    held = (*held, join_d0)
     join_n1, = add("add_next_1", second_n1, one_n1, held)
     three_n1 = turn(join_n1, xy, 2)
     held = (*held, join_n1)
-    join_d0, = add("add_opposite_0", second_d0, one_d0, held)
-    three_d0 = turn(join_d0, od, 2)
-    held = (*held, join_d0)
-    join_d1, = add("add_opposite_1", second_d1, one_d1, (three_n1, *held))
+    join_d1, = add("add_opposite_1", second_d1, one_d1, (three_d0, *held))
     three_d1 = turn(join_d1, od, 2)
-    second_n1, = release("release_2", (second_n1,), (join_d1, three_n1, first_n1, join_n1, first_d1))
+    second_n1, = release("release_2", (second_n1,), (join_d1, three_d0, first_n1, join_n1, first_d1))
     two_n1 = turn(second_n1, xy, 1)
     held = (first_n1, join_n1, three_n1, first_d1, join_d1)
     out = last(0, total, (first_n0, join_n0, two_n0, three_n0), (first_d0, join_d0, two_d0, three_d0), None, held)

time: 200 us -> 187 us (0.935)
  starting transfers between devices: 65.3 us -> 56.6 us
  waiting for transfers between devices: 79 us -> 73.2 us
    ppermute x12, starting transfers between devices: 32.3 us -> 24.3 us  [turn(): return lax.ppermute(value, ('seq', 'head'), sends(kinds, i))]
    ppermute x12, waiting for transfers between devices: 45.1 us -> 39.3 us  [turn(): return lax.ppermute(value, ('seq', 'head'), sends(kinds, i))]
    ppermute x9, waiting for transfers between devices: 1.47 us -> 5.07 us  [fast(): across = lambda a: lax.ppermute(a, 'head', xor_pairs(n_head, 1))]
    ppermute x8, waiting for transfers between devices: 25.1 us -> 21.5 us  [fast(): beside = lambda a, k: lax.ppermute(a, 'seq', xor_pairs(n_seq, k))]
    pallas_call x26 -> x28, Pallas kernels: 52.6 us -> 53.5 us  [call(): pl.pallas_call(body, name=name, in_specs=[IN_VMEM] * len(operands) + [ANY...]
  transfers between devices with their start and end apart: 35 -> 35, of which waited for: 13 -> 17; matrix products, arithmetic and copies ran while one was open for 0% -> 0% of each run, Pallas kernels for 24% -> 27%
where the time goes in v1:
time: 187 us; the launch traced here: 186 us
  waiting for transfers between devices  73.2 us (39%)
  starting transfers between devices  56.6 us (30%)
  Pallas kernels  56 us (30%)
    pallas_call x28, Pallas kernels, call(): pl.pallas_call(body, name=name, in_specs=[IN_VMEM] * len(operands) + [ANY...  53.5 us
    ppermute x12, waiting for transfers between devices, turn(): return lax.ppermute(value, ('seq', 'head'), sends(kinds, i))  39.3 us
    ppermute x12, starting transfers between devices, turn(): return lax.ppermute(value, ('seq', 'head'), sends(kinds, i))  24.3 us
    ppermute x8, waiting for transfers between devices, fast(): beside = lambda a, k: lax.ppermute(a, 'seq', xor_pairs(n_seq, k))  21.5 us
    ppermute x8, starting transfers between devices, fast(): beside = lambda a, k: lax.ppermute(a, 'seq', xor_pairs(n_seq, k))  21.1 us
    ppermute x9, waiting for transfers between devices, fast(): across = lambda a: lax.ppermute(a, 'head', xor_pairs(n_head, 1))  5.07 us
    ppermute x1, starting transfers between devices, fast(): near0 = lax.ppermute(msg0, 'seq', ring)  4.88 us
    ppermute x1, waiting for transfers between devices, fast(): near1 = lax.ppermute(msg1, 'seq', ring)  4.35 us
  transfers between devices with their start and end apart: 35, of which 17 were waited for; matrix products, arithmetic and copies ran while one was open for 0% of the time, Pallas kernels for 27%

profile of v1, /device:TPU:0, one launch (start us, length us, event | category | flops | bytes accessed | tf_op | source)
XLA Modules:
  0.0 186.3 jit_solution(8271187091675646155)
XLA Ops:
  0.0 3.9 %prep_0.1 = (bf16[144,2048]{1,0:T(8,128)(2,1)S(1)}, f32[32,384]{1,0:T(8,128)S(1)}, f32[32,256]{1,0:T(8,128)S(1)}, f32[32,256]{1,0:T(8,128)S(1)}, f32[1,256]{1,0:T(1,128)S(1)}) custom-call(bf16[2,256,2048]{2,1,0:T(8,128)(2,1)} %refs_4_.7, bf16[2,256,128]{2,1,0:T(8,128)(2,1)} %refs_6_.3, f32[2,32,256]{2,1,0:T(8,128)} %bitcast.2, f32[2,32]{1,0:T(2,128)} %refs_3_.5, ...), custom_call_target="tpu_custom_call" | custom-call | flops 1 | bytes 1 | tf_op jit(solution)/shard_map/prep_0/pallas_call | solution.py:31
  4.0 4.9 %collective-permute-start = (bf16[144,2048]{1,0:T(8,128)(2,1)S(1)}, bf16[144,2048]{1,0:T(8,128)(2,1)S(1)}, u32[]{:S(2)}, u32[]{:S(2)}) collective-permute-start(bf16[144,2048]{1,0:T(8,128)(2,1)S(1)} %get-tuple-element.52.refs_7_.refs_8_.refs_0_), channel_id=1, source_target_pairs={{0,8},{16,24},{1,9},{17,25},{2,10},{18,26},{3,11},{19,27},{4,12},{... | collective-permute-start | bytes 1769480 | tf_op jit(solution)/shard_map/ppermute | solution.py:489
  8.8 4.0 %prep_1.1 = (bf16[144,2048]{1,0:T(8,128)(2,1)S(1)}, f32[32,384]{1,0:T(8,128)S(1)}, f32[32,256]{1,0:T(8,128)S(1)}, f32[32,256]{1,0:T(8,128)S(1)}, f32[1,256]{1,0:T(1,128)S(1)}) custom-call(bf16[2,256,2048]{2,1,0:T(8,128)(2,1)} %refs_4_.7, bf16[2,256,128]{2,1,0:T(8,128)(2,1)} %refs_6_.3, f32[2,32,256]{2,1,0:T(8,128)} %bitcast.3, f32[2,32]{1,0:T(2,128)} %refs_3_.5, ...), custom_call_target="tpu_custom_call" | custom-call | flops 1 | bytes 1 | tf_op jit(solution)/shard_map/prep_1/pallas_call | solution.py:31
  12.8 1.3 collective-permute-start.3
  14.1 5.4 %inside_0.1 = (bf16[256,2048]{1,0:T(8,128)(2,1)S(1)}, bf16[256,2048]{1,0:T(8,128)(2,1)S(1)}) custom-call(f32[32,384]{1,0:T(8,128)S(1)} %get-tuple-element.53.refs_8_.refs_0_, f32[32,256]{1,0:T(8,128)S(1)} %get-tuple-element.54.refs_9_.refs_1_, f32[32,256]{1,0:T(8,128)S(1)} %get-tuple-element.55.refs_10_.refs_2_, ...), custom_call_target="tpu_custom_call" | custom-call | flops 1 | bytes 1 | tf_op jit(solution)/shard_map/inside_0/pallas_call | solution.py:31
  19.5 3.0 %collective-permute-done.refs_1_.refs_11_.refs_4_.refs_3_.refs_0_ = bf16[144,2048]{1,0:T(8,128)(2,1)S(1)} collective-permute-done((bf16[144,2048]{1,0:T(8,128)(2,1)S(1)}, bf16[144,2048]{1,0:T(8,128)(2,1)S(1)}, u32[]{:S(2)}, u32[]{:S(2)}) %collective-permute-start) | collective-permute-done | bytes 589856 | tf_op jit(solution)/shard_map/ppermute | solution.py:489
  22.5 0.2 join_0.1.refs_8_
  22.7 0.7 collective-permute-start.1
  23.4 0.9 collective-permute-start.2
  24.3 5.4 %inside_1.1 = (bf16[256,2048]{1,0:T(8,128)(2,1)S(1)}, bf16[256,2048]{1,0:T(8,128)(2,1)S(1)}) custom-call(f32[32,384]{1,0:T(8,128)S(1)} %get-tuple-element.58.refs_10_.refs_6_.refs_0_, f32[32,256]{1,0:T(8,128)S(1)} %get-tuple-element.59.refs_11_.refs_7_.refs_1_, f32[32,256]{1,0:T(8,128)S(1)} %get-tuple-element.60.refs_12_.refs_8_.refs_2_, ...), custom_call_target="tpu_custom_call" | custom-call | flops 1 | bytes 1 | tf_op jit(solution)/shard_map/inside_1/pallas_call | solution.py:31
  29.7 4.4 %collective-permute-done.3.refs_1_.refs_9_.refs_12_.refs_0_ = bf16[144,2048]{1,0:T(8,128)(2,1)S(1)} collective-permute-done((bf16[144,2048]{1,0:T(8,128)(2,1)S(1)}, bf16[144,2048]{1,0:T(8,128)(2,1)S(1)}, u32[]{:S(2)}, u32[]{:S(2)}) %collective-permute-start.3) | collective-permute-done | bytes 589856 | tf_op jit(solution)/shard_map/ppermute | solution.py:491
  34.2 0.8 collective-permute-start.4
  35.1 0.7 collective-permute-start.5
  35.8 5.8 %load.1 = (bf16[2,2048,2048]{2,1,0:T(8,128)(2,1)S(1)}, f32[2,2048]{1,0:T(2,128)S(1)}) custom-call(bf16[2,2048,2048]{2,1,0:T(8,128)(2,1)} %refs_0_.5, f32[2,2048]{1,0:T(2,128)} %refs_7_.7, bf16[144,2048]{1,0:T(8,128)(2,1)S(1)} %join_1.1.refs_2_, bf16[144,2048]{1,0:T(8,128)(2,1)S(1)} %collective-permute-done.refs_1_.refs_11_.refs_4_.refs_3_.refs_0_, ...), custom_call_target="tpu_custom_call" | custom-call | flops 1 | bytes 1 | tf_op jit(solution)/shard_map/load/pallas_call | solution.py:31
  41.6 0.9 gated_0.1.refs_10_.refs_0_
  42.5 13.7 %collective-permute-start.8 = (bf16[256,2048]{1,0:T(8,128)(2,1)S(1)}, bf16[256,2048]{1,0:T(8,128)(2,1)S(1)}, u32[]{:S(2)}, u32[]{:S(2)}) collective-permute-start(bf16[256,2048]{1,0:T(8,128)(2,1)S(1)} %gated_0.1.refs_10_.refs_0_), channel_id=1, source_target_pairs={{0,8},{8,0},{16,24},{24,16},{1,9},{9,1},{17,25},{25,17},{2,10},{10... | collective-permute-start | bytes 3145736 | tf_op jit(solution)/shard_map/ppermute | solution.py:481
  56.2 2.5 %collective-permute-start.9 = (bf16[256,2048]{1,0:T(8,128)(2,1)S(1)}, bf16[256,2048]{1,0:T(8,128)(2,1)S(1)}, u32[]{:S(2)}, u32[]{:S(2)}) collective-permute-start(bf16[256,2048]{1,0:T(8,128)(2,1)S(1)} %gated_0.1.refs_10_.refs_0_), channel_id=1, source_target_pairs={{0,16},{8,24},{16,0},{24,8},{1,17},{9,25},{17,1},{25,9},{2,18},{10... | collective-permute-start | bytes 3145736 | tf_op jit(solution)/shard_map/ppermute | solution.py:481
  58.7 0.9 gated_1.1.refs_3_.refs_0_
  59.6 0.8 collective-permute-start.6
  60.3 3.3 %own_0.1 = (bf16[1,128,2176]{2,1,0:T(8,128)(2,1)S(1)}, bf16[1,128,2176]{2,1,0:T(8,128)(2,1)S(1)}) custom-call(bf16[256,2048]{1,0:T(8,128)(2,1)S(1)} %gated_0.1.refs_10_.refs_0_, bf16[2,2048,2048]{2,1,0:T(8,128)(2,1)S(1)} %get-tuple-element.66.refs_8_.refs_1_.refs_2_.refs_5_.refs_7_.refs_3_.refs_4_.refs_6_, ...), custom_call_target="tpu_custom_call" | custom-call | flops 1 | bytes 1 | tf_op jit(solution)/shard_map/own_0/pallas_call | solution.py:31
  63.8 3.3 %own_1.1 = (bf16[1,128,2176]{2,1,0:T(8,128)(2,1)S(1)}, bf16[1,128,2176]{2,1,0:T(8,128)(2,1)S(1)}) custom-call(bf16[256,2048]{1,0:T(8,128)(2,1)S(1)} %gated_1.1.refs_3_.refs_0_, bf16[2,2048,2048]{2,1,0:T(8,128)(2,1)S(1)} %get-tuple-element.66.refs_8_.refs_1_.refs_2_.refs_5_.refs_7_.refs_3_.refs_4_.refs_6_, ...), custom_call_target="tpu_custom_call" | custom-call | flops 1 | bytes 1 | tf_op jit(solution)/shard_map/own_1/pallas_call | solution.py:31
  67.1 13.2 %collective-permute-done.8.refs_0_ = bf16[256,2048]{1,0:T(8,128)(2,1)S(1)} collective-permute-done((bf16[256,2048]{1,0:T(8,128)(2,1)S(1)}, bf16[256,2048]{1,0:T(8,128)(2,1)S(1)}, u32[]{:S(2)}, u32[]{:S(2)}) %collective-permute-start.8) | collective-permute-done | bytes 1048608 | tf_op jit(solution)/shard_map/ppermute | solution.py:481
  80.3 2.5 %collective-permute-done.9.refs_1_ = bf16[256,2048]{1,0:T(8,128)(2,1)S(1)} collective-permute-done((bf16[256,2048]{1,0:T(8,128)(2,1)S(1)}, bf16[256,2048]{1,0:T(8,128)(2,1)S(1)}, u32[]{:S(2)}, u32[]{:S(2)}) %collective-permute-start.9) | collective-permute-done | bytes 1048608 | tf_op jit(solution)/shard_map/ppermute | solution.py:481
  82.8 5.8 %next_0.1 = (bf16[2,128,2176]{2,1,0:T(8,128)(2,1)S(1)}, bf16[1,128,2176]{2,1,0:T(8,128)(2,1)S(1)}, bf16[1,128,2176]{2,1,0:T(8,128)(2,1)S(1)}, bf16[128,2048]{1,0:T(8,128)(2,1)S(1)}, bf16[128,2048]{1,0:T(8,128)(2,1)S(1)}) custom-call(bf16[256,2048]{1,0:T(8,128)(2,1)S(1)} %collective-permute-done.8.refs_0_, ...), custom_call_target="tpu_custom_call" | custom-call | flops 1 | bytes 1 | tf_op jit(solution)/shard_map/next_0/pallas_call | solution.py:31
  88.7 0.5 collective-permute-start.11
  89.2 1.4 collective-permute-done.10.refs_2_
  90.6 0.8 collective-permute-done.11.refs_3_
  91.4 0.4 sum_next_0.1
  91.8 3.5 %collective-permute-start.16 = (bf16[128,2176]{1,0:T(8,128)(2,1)S(1)}, bf16[128,2176]{1,0:T(8,128)(2,1)S(1)}, u32[]{:S(2)}, u32[]{:S(2)}) collective-permute-start(bf16[128,2176]{1,0:T(8,128)(2,1)S(1)} %get-tuple-element.78.refs_7_.refs_9_.refs_8_.refs_10_.refs_6_.refs_2_.refs_3_.refs_0_), channel_id=1, source_target_pairs={{0,2},{1,3},{6,4},{7,5},{10,8},{11,9},{14,12},{15,13},{12,14},{13,... | collective-permute-start | bytes 1671176 | tf_op jit(solution)/shard_map/ppermute | solution.py:509
  95.3 1.5 collective-permute-start.17
  96.8 2.0 %collective-permute-done.6.refs_0_ = bf16[256,2048]{1,0:T(8,128)(2,1)S(1)} collective-permute-done((bf16[256,2048]{1,0:T(8,128)(2,1)S(1)}, bf16[256,2048]{1,0:T(8,128)(2,1)S(1)}, u32[]{:S(2)}, u32[]{:S(2)}) %collective-permute-start.6) | collective-permute-done | bytes 1048608 | tf_op jit(solution)/shard_map/ppermute | solution.py:481
  98.8 1.4 collective-permute-done.7.refs_1_
  100.2 2.1 %collective-permute-start.13 = (bf16[128,2048]{1,0:T(8,128)(2,1)S(1)}, bf16[128,2048]{1,0:T(8,128)(2,1)S(1)}, u32[]{:S(2)}, u32[]{:S(2)}) collective-permute-start(bf16[128,2048]{1,0:T(8,128)(2,1)S(1)} %get-tuple-element.79.refs_4_), channel_id=1, source_target_pairs={{0,16},{8,24},{16,0},{24,8},{1,17},{9,25},{17,1},{25,9},{2,18},{10... | collective-permute-start | bytes 1572872 | tf_op jit(solution)/shard_map/ppermute | solution.py:481
  102.5 5.8 %next_1.1 = (bf16[2,128,2176]{2,1,0:T(8,128)(2,1)S(1)}, bf16[2,128,2176]{2,1,0:T(8,128)(2,1)S(1)}, bf16[128,2048]{1,0:T(8,128)(2,1)S(1)}, bf16[128,2048]{1,0:T(8,128)(2,1)S(1)}) custom-call(bf16[256,2048]{1,0:T(8,128)(2,1)S(1)} %collective-permute-done.6.refs_0_, bf16[256,2048]{1,0:T(8,128)(2,1)S(1)} %collective-permute-done.7.refs_1_, ...), custom_call_target="tpu_custom_call" | custom-call | flops 1 | bytes 1 | tf_op jit(solution)/shard_map/next_1/pallas_call | solution.py:31
  108.6 0.7 collective-permute-start.22
  109.3 1.8 collective-permute-done.13.refs_0_.refs_2_.refs_4_
  111.1 0.6 collective-permute-done.14.refs_1_.refs_3_.refs_5_
  111.7 1.1 collective-permute-start.23
  112.8 0.8 collective-permute-start.24
  113.6 5.8 %collective-permute-done.17.refs_1_.refs_14_.refs_12_.refs_13_.refs_10_.refs_8_.refs_9_.refs_4_.refs_5_.refs_2_ = bf16[128,2176]{1,0:T(8,128)(2,1)S(1)} collective-permute-done((bf16[128,2176]{1,0:T(8,128)(2,1)S(1)}, bf16[128,2176]{1,0:T(8,128)(2,1)S(1)}, u32[]{:S(2)}, u32[]{:S(2)}) %collective-permute-start.17) | collective-permute-done | bytes 557088 | tf_op jit(solution)/shard_map/ppermute | solution.py:509
  119.4 0.4 sum_next_1.1
  119.7 3.3 %opposite_0.1 = (bf16[1,128,2176]{2,1,0:T(8,128)(2,1)S(1)}, bf16[1,128,1024]{2,1,0:T(8,128)(2,1)S(1)}, bf16[1,128,1152]{2,1,0:T(8,128)(2,1)S(1)}) custom-call(bf16[128,2048]{1,0:T(8,128)(2,1)S(1)} %collective-permute-done.13.refs_0_.refs_2_.refs_4_, bf16[128,2048]{1,0:T(8,128)(2,1)S(1)} %collective-permute-done.14.refs_1_.refs_3_.refs_5_, ...), custom_call_target="tpu_custom_call" | custom-call | flops 1 | bytes 1 | tf_op jit(solution)/shard_map/opposite_0/pallas_call | solution.py:31
  123.2 0.5 collective-permute-start.19
  123.7 1.4 collective-permute-done.19.refs_3_
  125.1 0.4 sum_opposite_0.1
  125.5 4.4 %collective-permute-start.27 = (bf16[128,2176]{1,0:T(8,128)(2,1)S(1)}, bf16[128,2176]{1,0:T(8,128)(2,1)S(1)}, u32[]{:S(2)}, u32[]{:S(2)}) collective-permute-start(bf16[128,2176]{1,0:T(8,128)(2,1)S(1)} %get-tuple-element.91.refs_0_.refs_12_.refs_13_.refs_8_.refs_9_.refs_4_), channel_id=1, source_target_pairs={{2,0},{3,1},{6,4},{7,5},{4,6},{5,7},{0,2},{1,3},{8,10},{9,11},{14,... | collective-permute-start | bytes 1671176 | tf_op jit(solution)/shard_map/ppermute | solution.py:509
  129.9 2.0 %collective-permute-start.21 = (bf16[128,2176]{1,0:T(8,128)(2,1)S(1)}, bf16[128,2176]{1,0:T(8,128)(2,1)S(1)}, u32[]{:S(2)}, u32[]{:S(2)}) collective-permute-start(bf16[128,2176]{1,0:T(8,128)(2,1)S(1)} %release_n1.1.refs_10_.refs_11_.refs_6_.refs_7_.refs_2_.refs_8_.refs_0_), channel_id=1, source_target_pairs={{0,2},{1,3},{6,4},{7,5},{10,8},{11,9},{14,12},{15,13},{12,14},{13,... | collective-permute-start | bytes 1671176 | tf_op jit(solution)/shard_map/ppermute | solution.py:509
  131.9 3.4 %opposite_1.1 = (bf16[1,128,2176]{2,1,0:T(8,128)(2,1)S(1)}, bf16[1,128,1024]{2,1,0:T(8,128)(2,1)S(1)}, bf16[1,128,1152]{2,1,0:T(8,128)(2,1)S(1)}) custom-call(bf16[128,2048]{1,0:T(8,128)(2,1)S(1)} %collective-permute-done.23.refs_0_, bf16[128,2048]{1,0:T(8,128)(2,1)S(1)} %collective-permute-done.24.refs_1_, ...), custom_call_target="tpu_custom_call" | custom-call | flops 99999997952 | bytes 1 | tf_op jit(solution)/shard_map/opposite_1/pallas_call | solution.py:31
  135.3 0.5 collective-permute-start.25
  135.8 1.4 collective-permute-done.25.refs_3_
  137.3 0.4 sum_opposite_1.1
  137.6 1.9 %collective-permute-start.28 = (bf16[128,2176]{1,0:T(8,128)(2,1)S(1)}, bf16[128,2176]{1,0:T(8,128)(2,1)S(1)}, u32[]{:S(2)}, u32[]{:S(2)}) collective-permute-start(bf16[128,2176]{1,0:T(8,128)(2,1)S(1)} %get-tuple-element.97.refs_10_.refs_11_.refs_4_), channel_id=1, source_target_pairs={{2,0},{3,1},{6,4},{7,5},{4,6},{5,7},{0,2},{1,3},{8,10},{9,11},{14,... | collective-permute-start | bytes 1671176 | tf_op jit(solution)/shard_map/ppermute | solution.py:509
  139.6 3.7 %collective-permute-done.27.refs_1_ = bf16[128,2176]{1,0:T(8,128)(2,1)S(1)} collective-permute-done((bf16[128,2176]{1,0:T(8,128)(2,1)S(1)}, bf16[128,2176]{1,0:T(8,128)(2,1)S(1)}, u32[]{:S(2)}, u32[]{:S(2)}) %collective-permute-start.27) | collective-permute-done | bytes 557088 | tf_op jit(solution)/shard_map/ppermute | solution.py:509
  143.4 1.3 collective-permute-start.29
  144.7 0.7 collective-permute-start.34
  145.4 9.4 %collective-permute-done.21.refs_1_ = bf16[128,2176]{1,0:T(8,128)(2,1)S(1)} collective-permute-done((bf16[128,2176]{1,0:T(8,128)(2,1)S(1)}, bf16[128,2176]{1,0:T(8,128)(2,1)S(1)}, u32[]{:S(2)}, u32[]{:S(2)}) %collective-permute-start.21) | collective-permute-done | bytes 557088 | tf_op jit(solution)/shard_map/ppermute | solution.py:509
  154.9 0.7 collective-permute-start.31
  155.6 0.7 collective-permute-start.32
  156.3 10.3 %collective-permute-done.28.refs_1_ = bf16[128,2176]{1,0:T(8,128)(2,1)S(1)} collective-permute-done((bf16[128,2176]{1,0:T(8,128)(2,1)S(1)}, bf16[128,2176]{1,0:T(8,128)(2,1)S(1)}, u32[]{:S(2)}, u32[]{:S(2)}) %collective-permute-start.28) | collective-permute-done | bytes 557088 | tf_op jit(solution)/shard_map/ppermute | solution.py:509
  166.8 1.3 collective-permute-start.33
  168.1 5.6 %collective-permute-start.30 = (bf16[128,2176]{1,0:T(8,128)(2,1)S(1)}, bf16[128,2176]{1,0:T(8,128)(2,1)S(1)}, u32[]{:S(2)}, u32[]{:S(2)}) collective-permute-start(bf16[128,2176]{1,0:T(8,128)(2,1)S(1)} %release_2.1), channel_id=1, source_target_pairs={{0,2},{1,3},{6,4},{7,5},{24,26},{25,27},{30,28},{31,29}} | collective-permute-start | bytes 1671176 | tf_op jit(solution)/shard_map/ppermute | solution.py:509
  173.7 1.3 last_0.1.refs_8_
  175.0 10.0 %collective-permute-done.30.refs_2_ = bf16[128,2176]{1,0:T(8,128)(2,1)S(1)} collective-permute-done((bf16[128,2176]{1,0:T(8,128)(2,1)S(1)}, bf16[128,2176]{1,0:T(8,128)(2,1)S(1)}, u32[]{:S(2)}, u32[]{:S(2)}) %collective-permute-start.30) | collective-permute-done | bytes 557088 | tf_op jit(solution)/shard_map/ppermute | solution.py:509
  185.1 1.2 last_1.1
  (40 shorter events, 1.4 us)
Async XLA Ops:
  4.0 18.6 %collective-permute-start = (bf16[144,2048]{1,0:T(8,128)(2,1)S(1)}, bf16[144,2048]{1,0:T(8,128)(2,1)S(1)}, u32[]{:S(2)}, u32[]{:S(2)}) collective-permute-start(bf16[144,2048]{1,0:T(8,128)(2,1)S(1)} %get-tuple-element.52.refs_7_.refs_8_.refs_0_), channel_id=1, source_target_pairs={{0,8},{16,24},{1,9},{17,25},{2,10},{18,26},{3,11},{19,27},{4,12},{... | collective-permute-start | bytes 1769480 | tf_op jit(solution)/shard_map/ppermute | solution.py:489
  12.8 21.2 %collective-permute-start.3 = (bf16[144,2048]{1,0:T(8,128)(2,1)S(1)}, bf16[144,2048]{1,0:T(8,128)(2,1)S(1)}, u32[]{:S(2)}, u32[]{:S(2)}) collective-permute-start(bf16[144,2048]{1,0:T(8,128)(2,1)S(1)} %get-tuple-element.57.refs_9_.refs_4_.refs_12_.refs_0_), channel_id=1, source_target_pairs={{0,8},{16,24},{1,9},{17,25},{2,10},{18,26},{3,11},{19,27},{4,12},{... | collective-permute-start | bytes 1769480 | tf_op jit(solution)/shard_map/ppermute | solution.py:491
  22.7 11.3 %collective-permute-start.1 = (bf16[144,2048]{1,0:T(8,128)(2,1)S(1)}, bf16[144,2048]{1,0:T(8,128)(2,1)S(1)}, u32[]{:S(2)}, u32[]{:S(2)}) collective-permute-start(bf16[144,2048]{1,0:T(8,128)(2,1)S(1)} %join_0.1.refs_8_), channel_id=1, source_target_pairs={{8,16},{9,17},{10,18},{11,19},{12,20},{13,21},{14,22},{15,23}} | collective-permute-start | bytes 1769480 | tf_op jit(solution)/shard_map/ppermute | solution.py:494
  23.4 10.6 %collective-permute-start.2 = (bf16[144,2048]{1,0:T(8,128)(2,1)S(1)}, bf16[144,2048]{1,0:T(8,128)(2,1)S(1)}, u32[]{:S(2)}, u32[]{:S(2)}) collective-permute-start(bf16[144,2048]{1,0:T(8,128)(2,1)S(1)} %join_0.1.refs_8_), channel_id=1, source_target_pairs={{8,24},{9,25},{10,26},{11,27},{12,28},{13,29},{14,30},{15,31}} | collective-permute-start | bytes 1769480 | tf_op jit(solution)/shard_map/ppermute | solution.py:494
  34.2 7.4 %copy-start = (bf16[2,256,128]{2,1,0:T(8,128)(2,1)S(1)}, bf16[2,256,128]{2,1,0:T(8,128)(2,1)}, u32[]{:S(2)}) copy-start(bf16[2,256,128]{2,1,0:T(8,128)(2,1)} %refs_3_.7) | copy-start | bytes 393220
  34.2 7.4 %copy-start.1 = (f32[2,2048]{1,0:T(2,128)S(1)}, f32[2,2048]{1,0:T(2,128)}, u32[]{:S(2)}) copy-start(f32[2,2048]{1,0:T(2,128)} %refs_7_.7) | copy-start | bytes 49156
  34.2 7.4 %collective-permute-start.4 = (bf16[144,2048]{1,0:T(8,128)(2,1)S(1)}, bf16[144,2048]{1,0:T(8,128)(2,1)S(1)}, u32[]{:S(2)}, u32[]{:S(2)}) collective-permute-start(bf16[144,2048]{1,0:T(8,128)(2,1)S(1)} %join_1.1.refs_2_), channel_id=1, source_target_pairs={{8,16},{9,17},{10,18},{11,19},{12,20},{13,21},{14,22},{15,23}} | collective-permute-start | bytes 1769480 | tf_op jit(solution)/shard_map/ppermute | solution.py:497
  35.1 6.5 %collective-permute-start.5 = (bf16[144,2048]{1,0:T(8,128)(2,1)S(1)}, bf16[144,2048]{1,0:T(8,128)(2,1)S(1)}, u32[]{:S(2)}, u32[]{:S(2)}) collective-permute-start(bf16[144,2048]{1,0:T(8,128)(2,1)S(1)} %join_1.1.refs_2_), channel_id=1, source_target_pairs={{8,24},{9,25},{10,26},{11,27},{12,28},{13,29},{14,30},{15,31}} | collective-permute-start | bytes 1769480 | tf_op jit(solution)/shard_map/ppermute | solution.py:497
  42.5 37.8 %collective-permute-start.8 = (bf16[256,2048]{1,0:T(8,128)(2,1)S(1)}, bf16[256,2048]{1,0:T(8,128)(2,1)S(1)}, u32[]{:S(2)}, u32[]{:S(2)}) collective-permute-start(bf16[256,2048]{1,0:T(8,128)(2,1)S(1)} %gated_0.1.refs_10_.refs_0_), channel_id=1, source_target_pairs={{0,8},{8,0},{16,24},{24,16},{1,9},{9,1},{17,25},{25,17},{2,10},{10... | collective-permute-start | bytes 3145736 | tf_op jit(solution)/shard_map/ppermute | solution.py:481
  56.2 26.6 %collective-permute-start.9 = (bf16[256,2048]{1,0:T(8,128)(2,1)S(1)}, bf16[256,2048]{1,0:T(8,128)(2,1)S(1)}, u32[]{:S(2)}, u32[]{:S(2)}) collective-permute-start(bf16[256,2048]{1,0:T(8,128)(2,1)S(1)} %gated_0.1.refs_10_.refs_0_), channel_id=1, source_target_pairs={{0,16},{8,24},{16,0},{24,8},{1,17},{9,25},{17,1},{25,9},{2,18},{10... | collective-permute-start | bytes 3145736 | tf_op jit(solution)/shard_map/ppermute | solution.py:481
  59.6 39.2 %collective-permute-start.6 = (bf16[256,2048]{1,0:T(8,128)(2,1)S(1)}, bf16[256,2048]{1,0:T(8,128)(2,1)S(1)}, u32[]{:S(2)}, u32[]{:S(2)}) collective-permute-start(bf16[256,2048]{1,0:T(8,128)(2,1)S(1)} %gated_1.1.refs_3_.refs_0_), channel_id=1, source_target_pairs={{0,8},{8,0},{16,24},{24,16},{1,9},{9,1},{17,25},{25,17},{2,10},{10... | collective-permute-start | bytes 3145736 | tf_op jit(solution)/shard_map/ppermute | solution.py:481
  60.3 39.9 %collective-permute-start.7 = (bf16[256,2048]{1,0:T(8,128)(2,1)S(1)}, bf16[256,2048]{1,0:T(8,128)(2,1)S(1)}, u32[]{:S(2)}, u32[]{:S(2)}) collective-permute-start(bf16[256,2048]{1,0:T(8,128)(2,1)S(1)} %gated_1.1.refs_3_.refs_0_), channel_id=1, source_target_pairs={{0,16},{8,24},{16,0},{24,8},{1,17},{9,25},{17,1},{25,9},{2,18},{10... | collective-permute-start | bytes 3145736 | tf_op jit(solution)/shard_map/ppermute | solution.py:481
  63.7 25.5 %collective-permute-start.12 = (bf16[1,128,2176]{2,1,0:T(8,128)(2,1)S(1)}, bf16[1,128,2176]{2,1,0:T(8,128)(2,1)S(1)}, u32[]{:S(2)}, u32[]{:S(2)}) collective-permute-start(bf16[1,128,2176]{2,1,0:T(8,128)(2,1)S(1)} %get-tuple-element.69.refs_4_), channel_id=1, source_target_pairs={{0,1},{1,0},{2,3},{3,2},{4,5},{5,4},{6,7},{7,6},{8,9},{9,8},{10,11... | collective-permute-start | bytes 1671176 | tf_op jit(solution)/shard_map/ppermute | solution.py:480
  88.6 2.0 %collective-permute-start.10 = (bf16[1,128,2176]{2,1,0:T(8,128)(2,1)S(1)}, bf16[1,128,2176]{2,1,0:T(8,128)(2,1)S(1)}, u32[]{:S(2)}, u32[]{:S(2)}) collective-permute-start(bf16[1,128,2176]{2,1,0:T(8,128)(2,1)S(1)} %get-tuple-element.73), channel_id=1, source_target_pairs={{0,1},{1,0},{2,3},{3,2},{4,5},{5,4},{6,7},{7,6},{8,9},{9,8},{10,11... | collective-permute-start | bytes 1671176 | tf_op jit(solution)/shard_map/ppermute | solution.py:480
  88.7 2.7 %collective-permute-start.11 = (bf16[1,128,2176]{2,1,0:T(8,128)(2,1)S(1)}, bf16[1,128,2176]{2,1,0:T(8,128)(2,1)S(1)}, u32[]{:S(2)}, u32[]{:S(2)}) collective-permute-start(bf16[1,128,2176]{2,1,0:T(8,128)(2,1)S(1)} %get-tuple-element.74), channel_id=1, source_target_pairs={{0,1},{1,0},{2,3},{3,2},{4,5},{5,4},{6,7},{7,6},{8,9},{9,8},{10,11... | collective-permute-start | bytes 1671176 | tf_op jit(solution)/shard_map/ppermute | solution.py:480
  89.2 19.2 %collective-permute-start.15 = (bf16[1,128,2176]{2,1,0:T(8,128)(2,1)S(1)}, bf16[1,128,2176]{2,1,0:T(8,128)(2,1)S(1)}, u32[]{:S(2)}, u32[]{:S(2)}) collective-permute-start(bf16[1,128,2176]{2,1,0:T(8,128)(2,1)S(1)} %get-tuple-element.71.refs_9_.refs_11_), channel_id=1, source_target_pairs={{0,1},{1,0},{2,3},{3,2},{4,5},{5,4},{6,7},{7,6},{8,9},{9,8},{10,11... | collective-permute-start | bytes 1671176 | tf_op jit(solution)/shard_map/ppermute | solution.py:480
  91.8 16.7 %collective-permute-start.16 = (bf16[128,2176]{1,0:T(8,128)(2,1)S(1)}, bf16[128,2176]{1,0:T(8,128)(2,1)S(1)}, u32[]{:S(2)}, u32[]{:S(2)}) collective-permute-start(bf16[128,2176]{1,0:T(8,128)(2,1)S(1)} %get-tuple-element.78.refs_7_.refs_9_.refs_8_.refs_10_.refs_6_.refs_2_.refs_3_.refs_0_), channel_id=1, source_target_pairs={{0,2},{1,3},{6,4},{7,5},{10,8},{11,9},{14,12},{15,13},{12,14},{13,... | collective-permute-start | bytes 1671176 | tf_op jit(solution)/shard_map/ppermute | solution.py:509
  95.3 24.1 %collective-permute-start.17 = (bf16[128,2176]{1,0:T(8,128)(2,1)S(1)}, bf16[128,2176]{1,0:T(8,128)(2,1)S(1)}, u32[]{:S(2)}, u32[]{:S(2)}) collective-permute-start(bf16[128,2176]{1,0:T(8,128)(2,1)S(1)} %get-tuple-element.77.refs_2_.refs_11_.refs_0_), channel_id=1, source_target_pairs={{0,2},{1,3},{6,4},{7,5},{24,26},{25,27},{30,28},{31,29}} | collective-permute-start | bytes 1671176 | tf_op jit(solution)/shard_map/ppermute | solution.py:509
  100.2 10.8 %collective-permute-start.13 = (bf16[128,2048]{1,0:T(8,128)(2,1)S(1)}, bf16[128,2048]{1,0:T(8,128)(2,1)S(1)}, u32[]{:S(2)}, u32[]{:S(2)}) collective-permute-start(bf16[128,2048]{1,0:T(8,128)(2,1)S(1)} %get-tuple-element.79.refs_4_), channel_id=1, source_target_pairs={{0,16},{8,24},{16,0},{24,8},{1,17},{9,25},{17,1},{25,9},{2,18},{10... | collective-permute-start | bytes 1572872 | tf_op jit(solution)/shard_map/ppermute | solution.py:481
  102.4 9.3 %collective-permute-start.14 = (bf16[128,2048]{1,0:T(8,128)(2,1)S(1)}, bf16[128,2048]{1,0:T(8,128)(2,1)S(1)}, u32[]{:S(2)}, u32[]{:S(2)}) collective-permute-start(bf16[128,2048]{1,0:T(8,128)(2,1)S(1)} %get-tuple-element.80), channel_id=1, source_target_pairs={{0,8},{8,0},{16,24},{24,16},{1,9},{9,1},{17,25},{25,17},{2,10},{10... | collective-permute-start | bytes 1572872 | tf_op jit(solution)/shard_map/ppermute | solution.py:481
  108.4 11.0 %collective-permute-start.18 = (bf16[2,128,2176]{2,1,0:T(8,128)(2,1)S(1)}, bf16[2,128,2176]{2,1,0:T(8,128)(2,1)S(1)}, u32[]{:S(2)}, u32[]{:S(2)}) collective-permute-start(bf16[2,128,2176]{2,1,0:T(8,128)(2,1)S(1)} %get-tuple-element.85), channel_id=1, source_target_pairs={{0,1},{1,0},{2,3},{3,2},{4,5},{5,4},{6,7},{7,6},{8,9},{9,8},{10,11... | collective-permute-start | bytes 3342344 | tf_op jit(solution)/shard_map/ppermute | solution.py:480
  108.6 23.3 %collective-permute-start.22 = (bf16[128,2176]{1,0:T(8,128)(2,1)S(1)}, bf16[128,2176]{1,0:T(8,128)(2,1)S(1)}, u32[]{:S(2)}, u32[]{:S(2)}) collective-permute-start(bf16[128,2176]{1,0:T(8,128)(2,1)S(1)} %add_next_0.1.refs_10_.refs_11_.refs_13_.refs_12_.refs_9_.refs_7_.refs_8_.refs_3_.refs_4_.refs_1_), channel_id=1, source_target_pairs={{2,4},{3,5},{4,2},{5,3},{12,8},{13,9},{10,14},{11,15},{20,16},{21,... | collective-permute-start | bytes 1671176 | tf_op jit(solution)/shard_map/ppermute | solution.py:509
  111.7 20.1 %collective-permute-start.23 = (bf16[128,2048]{1,0:T(8,128)(2,1)S(1)}, bf16[128,2048]{1,0:T(8,128)(2,1)S(1)}, u32[]{:S(2)}, u32[]{:S(2)}) collective-permute-start(bf16[128,2048]{1,0:T(8,128)(2,1)S(1)} %get-tuple-element.84.refs_0_), channel_id=1, source_target_pairs={{0,16},{8,24},{16,0},{24,8},{1,17},{9,25},{17,1},{25,9},{2,18},{10... | collective-permute-start | bytes 1572872 | tf_op jit(solution)/shard_map/ppermute | solution.py:481
  112.8 19.0 %collective-permute-start.24 = (bf16[128,2048]{1,0:T(8,128)(2,1)S(1)}, bf16[128,2048]{1,0:T(8,128)(2,1)S(1)}, u32[]{:S(2)}, u32[]{:S(2)}) collective-permute-start(bf16[128,2048]{1,0:T(8,128)(2,1)S(1)} %get-tuple-element.93), channel_id=1, source_target_pairs={{0,8},{8,0},{16,24},{24,16},{1,9},{9,1},{17,25},{25,17},{2,10},{10... | collective-permute-start | bytes 1572872 | tf_op jit(solution)/shard_map/ppermute | solution.py:481
  123.1 2.0 %collective-permute-start.20 = (bf16[1,128,1152]{2,1,0:T(8,128)(2,1)S(1)}, bf16[1,128,1152]{2,1,0:T(8,128)(2,1)S(1)}, u32[]{:S(2)}, u32[]{:S(2)}) collective-permute-start(bf16[1,128,1152]{2,1,0:T(8,128)(2,1)S(1)} %get-tuple-element.90), channel_id=1, source_target_pairs={{0,1},{1,0},{2,3},{3,2},{4,5},{5,4},{6,7},{7,6},{8,9},{9,8},{10,11... | collective-permute-start | bytes 884744 | tf_op jit(solution)/shard_map/ppermute | solution.py:480
  123.2 1.9 %collective-permute-start.19 = (bf16[1,128,1024]{2,1,0:T(8,128)(2,1)S(1)}, bf16[1,128,1024]{2,1,0:T(8,128)(2,1)S(1)}, u32[]{:S(2)}, u32[]{:S(2)}) collective-permute-start(bf16[1,128,1024]{2,1,0:T(8,128)(2,1)S(1)} %get-tuple-element.89), channel_id=1, source_target_pairs={{0,1},{1,0},{2,3},{3,2},{4,5},{5,4},{6,7},{7,6},{8,9},{9,8},{10,11... | collective-permute-start | bytes 786440 | tf_op jit(solution)/shard_map/ppermute | solution.py:480
  125.5 17.8 %collective-permute-start.27 = (bf16[128,2176]{1,0:T(8,128)(2,1)S(1)}, bf16[128,2176]{1,0:T(8,128)(2,1)S(1)}, u32[]{:S(2)}, u32[]{:S(2)}) collective-permute-start(bf16[128,2176]{1,0:T(8,128)(2,1)S(1)} %get-tuple-element.91.refs_0_.refs_12_.refs_13_.refs_8_.refs_9_.refs_4_), channel_id=1, source_target_pairs={{2,0},{3,1},{6,4},{7,5},{4,6},{5,7},{0,2},{1,3},{8,10},{9,11},{14,... | collective-permute-start | bytes 1671176 | tf_op jit(solution)/shard_map/ppermute | solution.py:509
  129.9 24.9 %collective-permute-start.21 = (bf16[128,2176]{1,0:T(8,128)(2,1)S(1)}, bf16[128,2176]{1,0:T(8,128)(2,1)S(1)}, u32[]{:S(2)}, u32[]{:S(2)}) collective-permute-start(bf16[128,2176]{1,0:T(8,128)(2,1)S(1)} %release_n1.1.refs_10_.refs_11_.refs_6_.refs_7_.refs_2_.refs_8_.refs_0_), channel_id=1, source_target_pairs={{0,2},{1,3},{6,4},{7,5},{10,8},{11,9},{14,12},{15,13},{12,14},{13,... | collective-permute-start | bytes 1671176 | tf_op jit(solution)/shard_map/ppermute | solution.py:509
  135.2 2.0 %collective-permute-start.26 = (bf16[1,128,1152]{2,1,0:T(8,128)(2,1)S(1)}, bf16[1,128,1152]{2,1,0:T(8,128)(2,1)S(1)}, u32[]{:S(2)}, u32[]{:S(2)}) collective-permute-start(bf16[1,128,1152]{2,1,0:T(8,128)(2,1)S(1)} %get-tuple-element.96), channel_id=1, source_target_pairs={{0,1},{1,0},{2,3},{3,2},{4,5},{5,4},{6,7},{7,6},{8,9},{9,8},{10,11... | collective-permute-start | bytes 884744 | tf_op jit(solution)/shard_map/ppermute | solution.py:480
  135.3 1.9 %collective-permute-start.25 = (bf16[1,128,1024]{2,1,0:T(8,128)(2,1)S(1)}, bf16[1,128,1024]{2,1,0:T(8,128)(2,1)S(1)}, u32[]{:S(2)}, u32[]{:S(2)}) collective-permute-start(bf16[1,128,1024]{2,1,0:T(8,128)(2,1)S(1)} %get-tuple-element.95), channel_id=1, source_target_pairs={{0,1},{1,0},{2,3},{3,2},{4,5},{5,4},{6,7},{7,6},{8,9},{9,8},{10,11... | collective-permute-start | bytes 786440 | tf_op jit(solution)/shard_map/ppermute | solution.py:480
  137.6 29.0 %collective-permute-start.28 = (bf16[128,2176]{1,0:T(8,128)(2,1)S(1)}, bf16[128,2176]{1,0:T(8,128)(2,1)S(1)}, u32[]{:S(2)}, u32[]{:S(2)}) collective-permute-start(bf16[128,2176]{1,0:T(8,128)(2,1)S(1)} %get-tuple-element.97.refs_10_.refs_11_.refs_4_), channel_id=1, source_target_pairs={{2,0},{3,1},{6,4},{7,5},{4,6},{5,7},{0,2},{1,3},{8,10},{9,11},{14,... | collective-permute-start | bytes 1671176 | tf_op jit(solution)/shard_map/ppermute | solution.py:509
  143.4 23.3 %collective-permute-start.29 = (bf16[128,2176]{1,0:T(8,128)(2,1)S(1)}, bf16[128,2176]{1,0:T(8,128)(2,1)S(1)}, u32[]{:S(2)}, u32[]{:S(2)}) collective-permute-start(bf16[128,2176]{1,0:T(8,128)(2,1)S(1)} %add_opposite_0.1.refs_12_.refs_13_.refs_5_), channel_id=1, source_target_pairs={{4,0},{5,1},{2,6},{3,7},{10,12},{11,13},{12,10},{13,11},{18,20},{1... | collective-permute-start | bytes 1671176 | tf_op jit(solution)/shard_map/ppermute | solution.py:509
  144.7 29.0 %collective-permute-start.34 = (bf16[128,2176]{1,0:T(8,128)(2,1)S(1)}, bf16[128,2176]{1,0:T(8,128)(2,1)S(1)}, u32[]{:S(2)}, u32[]{:S(2)}) collective-permute-start(bf16[128,2176]{1,0:T(8,128)(2,1)S(1)} %get-tuple-element.92.refs_1_.refs_13_.refs_14_.refs_0_.refs_9_.refs_10_), channel_id=1, source_target_pairs={{8,10},{9,11},{14,12},{15,13},{16,18},{17,19},{22,20},{23,21}} | collective-permute-start | bytes 1671176 | tf_op jit(solution)/shard_map/ppermute | solution.py:509
  154.9 18.8 %collective-permute-start.31 = (bf16[128,2176]{1,0:T(8,128)(2,1)S(1)}, bf16[128,2176]{1,0:T(8,128)(2,1)S(1)}, u32[]{:S(2)}, u32[]{:S(2)}) collective-permute-start(bf16[128,2176]{1,0:T(8,128)(2,1)S(1)} %add_next_1.1.refs_14_.refs_3_.refs_9_.refs_1_), channel_id=1, source_target_pairs={{2,4},{3,5},{4,2},{5,3},{12,8},{13,9},{10,14},{11,15},{20,16},{21,... | collective-permute-start | bytes 1671176 | tf_op jit(solution)/shard_map/ppermute | solution.py:509
  155.6 19.4 %collective-permute-start.32 = (bf16[128,2176]{1,0:T(8,128)(2,1)S(1)}, bf16[128,2176]{1,0:T(8,128)(2,1)S(1)}, u32[]{:S(2)}, u32[]{:S(2)}) collective-permute-start(bf16[128,2176]{1,0:T(8,128)(2,1)S(1)} %get-tuple-element.98.refs_11_.refs_0_.refs_12_), channel_id=1, source_target_pairs={{8,10},{9,11},{14,12},{15,13},{16,18},{17,19},{22,20},{23,21}} | collective-permute-start | bytes 1671176 | tf_op jit(solution)/shard_map/ppermute | solution.py:509
  166.8 18.3 %collective-permute-start.33 = (bf16[128,2176]{1,0:T(8,128)(2,1)S(1)}, bf16[128,2176]{1,0:T(8,128)(2,1)S(1)}, u32[]{:S(2)}, u32[]{:S(2)}) collective-permute-start(bf16[128,2176]{1,0:T(8,128)(2,1)S(1)} %add_opposite_1.1.refs_0_.refs_12_.refs_5_), channel_id=1, source_target_pairs={{4,0},{5,1},{2,6},{3,7},{10,12},{11,13},{12,10},{13,11},{18,20},{1... | collective-permute-start | bytes 1671176 | tf_op jit(solution)/shard_map/ppermute | solution.py:509
  168.1 17.0 %collective-permute-start.30 = (bf16[128,2176]{1,0:T(8,128)(2,1)S(1)}, bf16[128,2176]{1,0:T(8,128)(2,1)S(1)}, u32[]{:S(2)}, u32[]{:S(2)}) collective-permute-start(bf16[128,2176]{1,0:T(8,128)(2,1)S(1)} %release_2.1), channel_id=1, source_target_pairs={{0,2},{1,3},{6,4},{7,5},{24,26},{25,27},{30,28},{31,29}} | collective-permute-start | bytes 1671176 | tf_op jit(solution)/shard_map/ppermute | solution.py:509

commit v2 on v1

--- a/solution.py
+++ b/solution.py
@@ -226,24 +226,13 @@
     )
 
 
-def load_kernel(w_all, gain_all, w_ref, inverse_ref, gain_ref, sems):
-    fetches = start_all(sems, [(gain_all, gain_ref)] + [(w_all.at[i], w_ref.at[i]) for i in range(w_all.shape[0])])
-    fetches[0].wait()
-    inverse_ref[...] = 1.0 / gain_ref[...]
-    for fetch in fetches[1:]:
+def load_kernel(w_all, w_ref, sems):
+    for fetch in start_all(sems, [(w_all.at[i], w_ref.at[i]) for i in range(w_all.shape[0])]):
         fetch.wait()
 
 
-def load(w, gain, after):
-    return call(
-        load_kernel,
-        "load",
-        (),
-        [(w.shape, BF16), (gain.shape, F32)],
-        (w, gain),
-        after,
-        scratch=[pltpu.VMEM(gain.shape, F32), pltpu.SemaphoreType.DMA((1 + w.shape[0],))],
-    )
+def load(w, after):
+    return call(load_kernel, "load", (), [(w.shape, BF16)], (w,), after, scratch=[pltpu.SemaphoreType.DMA((w.shape[0],))])
 
 
 def join_kernel(state, own_ref, got_ref, out_ref):
@@ -259,9 +248,8 @@
 
 
 def gate_kernel(model, state, alone, near_ref, *refs):
-    further = 7 if alone else 6
-    far_refs, refs = refs[:-further], refs[-further:]
-    c_ref, seg_ref, yg_ref, fg_ref, gain_ref, g_ref, *ss_ref = refs
+    far_refs, refs = refs[:-7], refs[-7:]
+    c_ref, seg_ref, yg_ref, fg_ref, gain_ref, g_ref, ss_ref = refs
     rows, channels = yg_ref.shape
     paired = True if alone else lax.axis_index("seq") % 2 == 1
     seg_col = column(seg_ref[...])
@@ -278,13 +266,11 @@
         reached = (seg_col == anchor).astype(F32)
         gated = yg_ref[:, cols].astype(F32) + reached * fg_ref[:, cols].astype(F32) * dot(c_ref[model], entering)
         g_ref[:, cols] = (gated * gain_ref[model : model + 1, cols]).astype(BF16)
-        if alone:
-            ones = jnp.ones((8, cols.stop - cols.start), BF16)
-            squares += lax.dot_general(
-                ones, (gated * gated).astype(BF16), (((1,), (1,)), ((), ())), preferred_element_type=F32
-            )
-    if alone:
-        ss_ref[0][...] = squares
+        ones = jnp.ones((8, cols.stop - cols.start), BF16)
+        squares += lax.dot_general(
+            ones, (gated * gated).astype(BF16), (((1,), (1,)), ((), ())), preferred_element_type=F32
+        )
+    ss_ref[...] = squares
 
 
 def gate_all(model, alone, near, far, c, seg_row, yg, fg, gain, after=()):
@@ -292,14 +278,14 @@
         functools.partial(gate_kernel, model, c.shape[2], alone),
         f"gated_{model}",
         (near, *far, c, seg_row, yg, fg, gain),
-        [(yg.shape, BF16)] + [((8, yg.shape[0]), F32)] * alone,
+        [(yg.shape, BF16), ((8, yg.shape[0]), F32)],
         (),
         after,
     )
 
 
 def project_kernel(model, shapes, forward, sends, *refs):
-    given, (w_ref, inverse_ref, keep_ref, *refs) = refs[: sum(shapes)], refs[sum(shapes) :]
+    given, (w_ref, keep_ref, *refs) = refs[: sum(shapes)], refs[sum(shapes) :]
     count = len(shapes)
     half, width = keep_ref.shape[1], w_ref.shape[2]
     send_refs, (*refs, lhs) = refs[: len(sends)], refs[len(sends) :]
@@ -311,11 +297,6 @@
     for ref in given:
         lhs[row : row + ref.shape[0], :] = ref[...]
         row += ref.shape[0]
-    squares = jnp.zeros((row, LANES), F32)
-    for part in tiles(w_ref.shape[1]):
-        gated = lhs[:, part].astype(F32) * inverse_ref[model : model + 1, part]
-        squares += dot((gated * gated).astype(BF16), jnp.ones((part.stop - part.start, LANES), BF16))
-
     def put(result, ref, blocks, start, at, size):
         for k in range(count):
             early = result[2 * k * half : (2 * k + 1) * half].astype(BF16)
@@ -338,16 +319,14 @@
             put(dot(lhs[...], w_ref[model, :, pl.ds(start + at, tile)]), ref, blocks, start, at, tile)
             return 0
 
-        lax.fori_loop(0, (min(stop, width) - start) // tile, step, 0)
-        if stop > width:
-            put(squares, ref, blocks, start, width - start, LANES)
+        lax.fori_loop(0, (stop - start) // tile, step, 0)
 
 
 def project(name, model, blocks, weights, after=(), forward=False, split=None, weight=1):
-    w, inverse = weights
+    w, = weights
     flat = [a for block in blocks for a in block]
     depth, width = w.shape[1:]
-    n, full = len(blocks), width + LANES
+    n, full = len(blocks), width
     half = sum(a.shape[0] for a in flat) // (2 * n)
     if split == "blocks":
         sends = [([k], 0, full) for k in range(n)]
@@ -358,7 +337,7 @@
     return call(
         functools.partial(project_kernel, model, [len(block) for block in blocks], forward, sends),
         name,
-        (*flat, w, inverse),
+        (*flat, w),
         [((n, half, full), BF16)]
         + [((len(part), half, stop - start), BF16) for part, start, stop in sends]
         + [((half, depth), BF16)] * (2 * forward),
@@ -373,10 +352,17 @@
     return call(lambda *refs: None, name, (), [], (), after, carry=arrays, weight=weight)
 
 
-def pair_kernel(places, counts, *refs):
+def inner_column():
+    s = lax.axis_index("seq")
+    return (s == 1) | (s == 2)
+
+
+def pair_kernel(places, counts, own_sent, *refs):
     keeps, gots = refs[:2], (refs[2 : 2 + counts[0]], refs[2 + counts[0] : 2 + sum(counts)])
     first_ref, second_ref = refs[-2:]
     turned_round = (lax.axis_index("seq") // 2 + lax.axis_index("head") // 2) % 2 == 0
+    if own_sent:
+        turned_round = turned_round | inner_column()
 
     def ends(pieces):
         stops = [0]
@@ -396,9 +382,9 @@
         second_ref[:, start:stop] = jnp.where(turned_round, sums[0], sums[1]).astype(BF16)
 
 
-def pair_sums(name, one, other, after=()):
+def pair_sums(name, one, other, after=(), own_sent=False):
     return call(
-        functools.partial(pair_kernel, ((one[1], one[3]), (other[1], other[3])), (len(one[2]), len(other[2]))),
+        functools.partial(pair_kernel, ((one[1], one[3]), (other[1], other[3])), (len(one[2]), len(other[2])), own_sent),
         name,
         (one[0], other[0], *one[2], *other[2]),
         [(one[0].shape[1:], BF16)] * 2,
@@ -415,29 +401,65 @@
     return call(add_kernel, name, (own, got), [(own.shape, BF16)], (), after)
 
 
-def last_kernel(total, model, *refs):
-    beside, opposite, out_ref = refs[:4], refs[4:8], refs[8]
-    width = out_ref.shape[2]
+def join_own_kernel(first_ref, second_ref, one_ref, two_ref, out_ref):
+    mine = inner_column() & (lax.axis_index("seq") == lax.axis_index("head") // 2)
+    other = inner_column() & ~mine
+    base = jnp.where(mine, first_ref[...], second_ref[...])
+    got = jnp.where(other, two_ref[...], one_ref[...])
+    out_ref[...] = (base.astype(F32) + got.astype(F32)).astype(BF16)
+
+
+def pick_kernel(beside_ref, *refs):
+    *terms, out_ref = refs
+    value = sum((ref[...] if len(ref.shape) == 2 else ref[0]).astype(F32) for ref in terms)
+    out_ref[...] = jnp.where(inner_column(), value.astype(BF16), beside_ref[...])
+
+
+def pick(name, beside, terms, after=()):
+    return call(pick_kernel, name, (beside, *terms), [(beside.shape, BF16)], (), after)[0]
+
+
+def first_sums_kernel(one_ref, other_ref, out_ref):
+    rows = lax.broadcasted_iota(jnp.int32, out_ref.shape, 0)
+    out_ref[...] = jnp.where(rows < 4, one_ref[...], other_ref[...])
+
+
+def sums_kernel(one_ref, other_ref, out_ref):
+    out_ref[...] = one_ref[...] + other_ref[...]
+
+
+def last_kernel(total, model, own_sent, *refs):
+    first_n, join_n, three_n, first_d, second_d, one_d, join_d, three_d, two, ss_ref, out_ref = refs
+    half = out_ref.shape[1]
     s, z = lax.axis_index("seq"), lax.axis_index("head") // 2
+    row = ss_ref[4 * model : 4 * model + 1, :]
+    row = jnp.where(lax.axis_index("head") % 2 == 0, row[:, :half], row[:, half:])
+    scale = column(lax.rsqrt(row / total + EPS))
     straight = (s == z) | (s + z == 3)
-    inner = (z == 1) | (z == 2)
-
-    def write(refs):
-        value = jnp.where(inner, refs[0][...], refs[1][...]).astype(F32)
-        for ref in refs[2:]:
-            value = value + ref[...].astype(F32)
-        scale = lax.rsqrt(value[:, width : width + 1] / total + EPS)
-        out_ref[0] = (value[:, :width] * scale).astype(BF16)
-
-    pl.when(straight)(lambda: write(opposite))
-    pl.when(~straight)(lambda: write(beside))
-
-
-def last(model, total, beside, opposite, before, after=()):
-    half, width = beside[0].shape[0], beside[0].shape[1] - LANES
-    operands = (*beside, *opposite)
+    inner = inner_column()
+
+    def write(condition, *terms):
+        @pl.when(condition)
+        def _():
+            value = terms[0][...].astype(F32)
+            for ref in terms[1:]:
+                value = value + ref[...].astype(F32)
+            out_ref[0] = (value * scale).astype(BF16)
+
+    write(~straight & ~inner, first_n, two, three_n)
+    write(~straight & inner, join_n, three_n)
+    write(straight & ~inner, join_d, three_d)
+    if own_sent:
+        write(straight & inner & (s == z), second_d, two, three_d)
+        write(straight & inner & (s != z), first_d, one_d, three_d)
+    else:
+        write(straight & inner, first_d, two, three_d)
+
+
+def last(model, total, own_sent, operands, before, after=()):
+    half, width = operands[0].shape
     earlier = () if before is None else (before,)
-    kernel = functools.partial(last_kernel, total, model)
+    kernel = functools.partial(last_kernel, total, model, own_sent)
     return pl.pallas_call(
         lambda *refs: kernel(*refs[: len(operands)], refs[-1]),
         name=f"last_{model}",
@@ -469,10 +491,12 @@
     def sends(kinds, turn):
         pairs = []
         for si in range(n_seq):
-            if 0 in [si ^ k for k in kinds]:
-                steps = ([(1, 0), (3, 2), (2, 3), (0, 1)], [], [(2, 0), (1, 3)])[turn]
+            if turn == 1:
+                steps = [(0, 1), (3, 2)]
+            elif 0 in [si ^ k for k in kinds]:
+                steps = [(1, 0), (3, 2), (2, 3), (0, 1)] if turn == 0 else [(2, 0), (1, 3)]
             else:
-                steps = ([(0, 1), (3, 2)], [(0, 1), (3, 2)], [(1, 2), (2, 1)])[turn]
+                steps = [(0, 1), (3, 2)] if turn == 0 else [(1, 2), (2, 1)]
             pairs += [(flat(si, a, ci), flat(si, o, ci)) for a, o in steps for ci in range(2)]
         return pairs
 
@@ -484,7 +508,7 @@
     x, gate, raw, bias, rate, skip, w = (
         pltpu.with_memory_space_constraint(a, pltpu.HBM) for a in (x, gate, raw, bias, rate, skip, w)
     )
-    b_far, c_far, seg_far, gain_far = (pltpu.with_memory_space_constraint(a, pltpu.HBM) for a in (b, c, seg_row, gain))
+    b_far, c_far, seg_far = (pltpu.with_memory_space_constraint(a, pltpu.HBM) for a in (b, c, seg_row))
     msg0, *scan0 = prep(0, head_size, x, b_far, raw, bias, rate, skip, seg_far)
     near0 = lax.ppermute(msg0, "seq", ring)
     msg1, *scan1 = prep(1, head_size, x, b_far, raw, bias, rate, skip, seg_far, (msg0, *scan0))
@@ -496,10 +520,10 @@
     end1 = join(1, state, msg1, near1, (yg0, fg0, near0, yg1, fg1, scan0[-1], scan1[-1], *far0))
     far1 = [lax.ppermute(end1, "seq", [(1, t)]) for t in (2, 3)]
     held = (near1, yg1, fg1, scan1[-1])
-    w = load(w, gain_far, (end1, near0, yg0, fg0, scan0[-1], *far0, *held))
-    g0, = gate_all(0, False, near0, far0, c, scan0[-1], yg0, fg0, gain, (*w, *far1, *held))
+    w = load(w, (end1, near0, yg0, fg0, scan0[-1], *far0, *held))
+    g0, ss0 = gate_all(0, False, near0, far0, c, scan0[-1], yg0, fg0, gain, (*w, *far1, *held))
     x0, y0 = beside(g0, 1), beside(g0, 2)
-    g1, = gate_all(1, False, near1, far1, c, scan1[-1], yg1, fg1, gain, (*w, g0))
+    g1, ss1 = gate_all(1, False, near1, far1, c, scan1[-1], yg1, fg1, gain, (*w, g0, ss0))
     x1, y1 = beside(g1, 1), beside(g1, 2)
 
     def both(forwarded):
@@ -509,20 +533,29 @@
         return lax.ppermute(value, ("seq", "head"), sends(kinds, i))
 
     xy, od = (1, 2), (0, 3)
-    keep_o0, send_o0 = project("own_0", 0, [(g0,)], w, (g1,))
-    keep_o1, send_o1 = project("own_1", 1, [(g1,)], w, (keep_o0, send_o0))
+    def add_sums(k, ss, after):
+        return call(sums_kernel, f"sums_{k}", (ss, lax.ppermute(ss, "head", xor_pairs(n_head, k))), [(ss.shape, F32)], (), after)[0]
+
+    ss, = call(first_sums_kernel, "sums_0", (ss0, ss1), [(ss0.shape, F32)], (), (*w, g0, g1))
+    keep_o0, send_o0 = project("own_0", 0, [(g0,)], w, (g1, ss))
+    ss = add_sums(1, ss, (*w, g1, keep_o0, send_o0))
+    keep_o1, send_o1 = project("own_1", 1, [(g1,)], w, (ss, keep_o0, send_o0))
     held = (*w, keep_o0, keep_o1, send_o1)
-    keep_n0, *send_n0, f0, l0 = project("next_0", 0, [(x0,), (y0,)], w, (send_o0, *held), True, "blocks")
+    ss = add_sums(2, ss, (send_o0, *held))
+    ss = add_sums(4, ss, (send_o0, *held))
+    keep_n0, *send_n0, f0, l0 = project("next_0", 0, [(x0,), (y0,)], w, (ss, send_o0, *held), True, "blocks")
     got_n0 = [across(a) for a in send_n0]
     got_o0 = across(send_o0)
     first_n0, second_n0 = pair_sums(
         "sum_next_0", (keep_n0, 0, got_n0[:1], 0), (keep_n0, 1, got_n0[1:], 0), (f0, l0, got_o0, *held)
     )
-    one_n0, two_n0 = turn(first_n0, xy, 0), turn(second_n0, xy, 1)
+    one_n0 = turn(first_n0, xy, 0)
+    third_0 = pick("pick_0", second_n0, (keep_o0, got_o0), (first_n0, f0, l0, *held))
+    two_n0 = turn(third_0, xy, 1)
     got_o1 = across(send_o1)
     own0, own1 = (keep_o0, 0, (got_o0,), 0), (keep_o1, 0, (got_o1,), 0)
     held = (*w, keep_o0, keep_o1, first_n0, got_o0)
-    f0, l0 = release("release_0", (f0, l0), (x1, y1, second_n0, *held), HEAVY)
+    f0, l0 = release("release_0", (f0, l0), (x1, y1, second_n0, third_0, *held), HEAVY)
     d0 = both((f0, l0))
     held = (*held, second_n0)
     keep_n1, send_n1, f1, l1 = project("next_1", 1, [(x1,), (y1,)], w, (f0, *held), True)
@@ -541,29 +574,40 @@
     held = (*held, first_n1, second_n1)
     keep_d0, *send_d0 = project("opposite_0", 0, [d0], w, held, False, "columns")
     got_d0 = [across(a) for a in send_d0]
-    first_d0, second_d0 = pair_sums("sum_opposite_0", own0, (keep_d0, 0, got_d0, 0), held)
-    one_d0, two_d0 = turn(first_d0, od, 0), turn(second_d0, od, 1)
+    first_d0, second_d0 = pair_sums("sum_opposite_0", own0, (keep_d0, 0, got_d0, 0), held, True)
+    one_d0 = turn(first_d0, od, 0)
     first_n1, = release("release_n1", (first_n1,), (first_d0, second_d0, *held[:-2], second_n1))
     one_n1 = turn(first_n1, xy, 0)
     held = (keep_o1, got_o1, first_n0, join_n0, two_n0, three_n0, first_n1, second_n1, first_d0, second_d0)
     keep_d1, *send_d1 = project("opposite_1", 1, [d1], w, held, False, "columns", HEAVY)
     got_d1 = [across(a) for a in send_d1]
     first_d1, second_d1 = pair_sums("sum_opposite_1", own1, (keep_d1, 0, got_d1, 0), held)
-    one_d1, two_d1 = turn(first_d1, od, 0), turn(second_d1, od, 1)
+    one_d1 = turn(first_d1, od, 0)
     held = (*held[2:], first_d1, second_d1)
-    join_d0, = add("add_opposite_0", second_d0, one_d0, held)
+    join_d0, = call(
+        join_own_kernel, "add_opposite_0", (first_d0, second_d0, one_d0, two_n0), [(first_d0.shape, BF16)], (), held
+    )
     three_d0 = turn(join_d0, od, 2)
-    held = (*held, join_d0)
-    join_n1, = add("add_next_1", second_n1, one_n1, held)
+    held = (*held, one_d0, join_d0)
+    third_1 = pick("pick_1", second_n1, (second_d1,), held)
+    two_1 = turn(third_1, xy, 1)
+    join_n1, = add("add_next_1", second_n1, one_n1, (third_1, *held))
     three_n1 = turn(join_n1, xy, 2)
     held = (*held, join_n1)
     join_d1, = add("add_opposite_1", second_d1, one_d1, (three_d0, *held))
     three_d1 = turn(join_d1, od, 2)
-    second_n1, = release("release_2", (second_n1,), (join_d1, three_d0, first_n1, join_n1, first_d1))
-    two_n1 = turn(second_n1, xy, 1)
-    held = (first_n1, join_n1, three_n1, first_d1, join_d1)
-    out = last(0, total, (first_n0, join_n0, two_n0, three_n0), (first_d0, join_d0, two_d0, three_d0), None, held)
-    return last(1, total, (first_n1, join_n1, two_n1, three_n1), (first_d1, join_d1, two_d1, three_d1), out)
+    ss, = release("release_sums", (ss,), (first_d1, second_d1))
+    ss = lax.ppermute(
+        ss, ("seq", "head"),
+        [(flat(zi, si, ci), flat(si, zi, ci)) for si in range(n_seq) for zi in range(n_seq) for ci in range(2)],
+    )
+    held = (first_n1, join_n1, three_n1, first_d1, second_d1, one_d1, join_d1, two_1)
+    out = last(
+        0, total, True, (first_n0, join_n0, three_n0, first_d0, second_d0, one_d0, join_d0, three_d0, two_n0, ss), None, held
+    )
+    return last(
+        1, total, False, (first_n1, join_n1, three_n1, first_d1, second_d1, one_d1, join_d1, three_d1, two_1, ss), out
+    )
 
 
 def plain(x, gate, b, c, raw, bias, rate, skip, gain, w, seg):

time: 187 us -> 182 us (0.973)
  waiting for transfers between devices: 73.2 us -> 59.7 us
  starting transfers between devices: 56.6 us -> 67.5 us
  Pallas kernels: 56 us -> 53.7 us
    ppermute x12 -> x10, waiting for transfers between devices: 39.3 us -> 27.9 us  [turn(): return lax.ppermute(value, ('seq', 'head'), sends(kinds, i))]
    ppermute x12 -> x10, starting transfers between devices: 24.3 us -> 30.3 us  [turn(): return lax.ppermute(value, ('seq', 'head'), sends(kinds, i))]
    ppermute x0 -> x4, starting transfers between devices: none -> 4.95 us  [the longest x3 4.29 us: add_sums(): lax.ppermute(ss, 'head', xor_pairs(n_head, k))]
    ppermute x8, waiting for transfers between devices: 21.5 us -> 17.5 us  [fast(): beside = lambda a, k: lax.ppermute(a, 'seq', xor_pairs(n_seq, k))]
    ppermute x0 -> x4, waiting for transfers between devices: none -> 1.99 us  [the longest x3 1.98 us: add_sums(): lax.ppermute(ss, 'head', xor_pairs(n_head, k))]
    pallas_call x28 -> x34, Pallas kernels: 53.5 us -> 51.5 us  [call(): pl.pallas_call(body, name=name, in_specs=[IN_VMEM] * len(operands) + [ANY...]
  transfers between devices with their start and end apart: 35 -> 37, of which waited for: 17 -> 18; matrix products, arithmetic and copies ran while one was open for 0% -> 0% of each run, Pallas kernels for 27% -> 26%
where the time goes in v2:
time: 182 us; the launch traced here: 181 us
  starting transfers between devices  67.5 us (37%)
  waiting for transfers between devices  59.7 us (33%)
  Pallas kernels  53.7 us (30%)
    pallas_call x34, Pallas kernels, call(): pl.pallas_call(body, name=name, in_specs=[IN_VMEM] * len(operands) + [ANY...  51.5 us
    ppermute x10, starting transfers between devices, turn(): return lax.ppermute(value, ('seq', 'head'), sends(kinds, i))  30.3 us
    ppermute x10, waiting for transfers between devices, turn(): return lax.ppermute(value, ('seq', 'head'), sends(kinds, i))  27.9 us
    ppermute x8, starting transfers between devices, fast(): beside = lambda a, k: lax.ppermute(a, 'seq', xor_pairs(n_seq, k))  21.1 us
    ppermute x8, waiting for transfers between devices, fast(): beside = lambda a, k: lax.ppermute(a, 'seq', xor_pairs(n_seq, k))  17.5 us
    ppermute x1, starting transfers between devices, fast(): near0 = lax.ppermute(msg0, 'seq', ring)  4.88 us
    ppermute x9, waiting for transfers between devices, fast(): across = lambda a: lax.ppermute(a, 'head', xor_pairs(n_head, 1))  4.87 us
    ppermute x1, waiting for transfers between devices, fast(): near1 = lax.ppermute(msg1, 'seq', ring)  4.36 us
  transfers between devices with their start and end apart: 37, of which 18 were waited for; matrix products, arithmetic and copies ran while one was open for 0% of the time, Pallas kernels for 26%

profile of v2, /device:TPU:0, one launch (start us, length us, event | category | flops | bytes accessed | tf_op | source)
XLA Modules:
  0.0 181.4 jit_solution(13245230773960886867)
XLA Ops:
  0.0 3.9 %prep_0.1 = (bf16[144,2048]{1,0:T(8,128)(2,1)S(1)}, f32[32,384]{1,0:T(8,128)S(1)}, f32[32,256]{1,0:T(8,128)S(1)}, f32[32,256]{1,0:T(8,128)S(1)}, f32[1,256]{1,0:T(1,128)S(1)}) custom-call(bf16[2,256,2048]{2,1,0:T(8,128)(2,1)} %refs_4_.7, bf16[2,256,128]{2,1,0:T(8,128)(2,1)} %refs_6_.3, f32[2,32,256]{2,1,0:T(8,128)} %bitcast.2, f32[2,32]{1,0:T(2,128)} %refs_3_.5, ...), custom_call_target="tpu_custom_call" | custom-call | flops 1 | bytes 1 | tf_op jit(solution)/shard_map/prep_0/pallas_call | solution.py:31
  4.0 4.9 %collective-permute-start = (bf16[144,2048]{1,0:T(8,128)(2,1)S(1)}, bf16[144,2048]{1,0:T(8,128)(2,1)S(1)}, u32[]{:S(2)}, u32[]{:S(2)}) collective-permute-start(bf16[144,2048]{1,0:T(8,128)(2,1)S(1)} %get-tuple-element.54.refs_7_.refs_8_.refs_0_), channel_id=1, source_target_pairs={{0,8},{16,24},{1,9},{17,25},{2,10},{18,26},{3,11},{19,27},{4,12},{... | collective-permute-start | bytes 1769480 | tf_op jit(solution)/shard_map/ppermute | solution.py:513
  8.8 4.0 %prep_1.1 = (bf16[144,2048]{1,0:T(8,128)(2,1)S(1)}, f32[32,384]{1,0:T(8,128)S(1)}, f32[32,256]{1,0:T(8,128)S(1)}, f32[32,256]{1,0:T(8,128)S(1)}, f32[1,256]{1,0:T(1,128)S(1)}) custom-call(bf16[2,256,2048]{2,1,0:T(8,128)(2,1)} %refs_4_.7, bf16[2,256,128]{2,1,0:T(8,128)(2,1)} %refs_6_.3, f32[2,32,256]{2,1,0:T(8,128)} %bitcast.3, f32[2,32]{1,0:T(2,128)} %refs_3_.5, ...), custom_call_target="tpu_custom_call" | custom-call | flops 1 | bytes 1 | tf_op jit(solution)/shard_map/prep_1/pallas_call | solution.py:31
  12.8 1.3 collective-permute-start.3
  14.1 5.4 %inside_0.1 = (bf16[256,2048]{1,0:T(8,128)(2,1)S(1)}, bf16[256,2048]{1,0:T(8,128)(2,1)S(1)}) custom-call(f32[32,384]{1,0:T(8,128)S(1)} %get-tuple-element.55.refs_8_.refs_0_, f32[32,256]{1,0:T(8,128)S(1)} %get-tuple-element.56.refs_9_.refs_1_, f32[32,256]{1,0:T(8,128)S(1)} %get-tuple-element.57.refs_10_.refs_2_, ...), custom_call_target="tpu_custom_call" | custom-call | flops 1 | bytes 1 | tf_op jit(solution)/shard_map/inside_0/pallas_call | solution.py:31
  19.5 3.0 %collective-permute-done.refs_1_.refs_11_.refs_4_.refs_2_.refs_0_ = bf16[144,2048]{1,0:T(8,128)(2,1)S(1)} collective-permute-done((bf16[144,2048]{1,0:T(8,128)(2,1)S(1)}, bf16[144,2048]{1,0:T(8,128)(2,1)S(1)}, u32[]{:S(2)}, u32[]{:S(2)}) %collective-permute-start) | collective-permute-done | bytes 589856 | tf_op jit(solution)/shard_map/ppermute | solution.py:513
  22.7 0.7 collective-permute-start.1
  23.4 0.9 collective-permute-start.2
  24.3 5.4 %inside_1.1 = (bf16[256,2048]{1,0:T(8,128)(2,1)S(1)}, bf16[256,2048]{1,0:T(8,128)(2,1)S(1)}) custom-call(f32[32,384]{1,0:T(8,128)S(1)} %get-tuple-element.60.refs_10_.refs_6_.refs_0_, f32[32,256]{1,0:T(8,128)S(1)} %get-tuple-element.61.refs_11_.refs_7_.refs_1_, f32[32,256]{1,0:T(8,128)S(1)} %get-tuple-element.62.refs_12_.refs_8_.refs_2_, ...), custom_call_target="tpu_custom_call" | custom-call | flops 1 | bytes 1 | tf_op jit(solution)/shard_map/inside_1/pallas_call | solution.py:31
  29.7 4.4 %collective-permute-done.3.refs_1_.refs_8_.refs_11_.refs_0_ = bf16[144,2048]{1,0:T(8,128)(2,1)S(1)} collective-permute-done((bf16[144,2048]{1,0:T(8,128)(2,1)S(1)}, bf16[144,2048]{1,0:T(8,128)(2,1)S(1)}, u32[]{:S(2)}, u32[]{:S(2)}) %collective-permute-start.3) | collective-permute-done | bytes 589856 | tf_op jit(solution)/shard_map/ppermute | solution.py:515
  34.2 0.8 collective-permute-start.4
  35.1 0.7 collective-permute-start.5
  35.8 5.8 %load.1.refs_8_.refs_2_.refs_1_.refs_3_.refs_5_.refs_7_.refs_6_.refs_4_ = bf16[2,2048,2048]{2,1,0:T(8,128)(2,1)S(1)} custom-call(bf16[2,2048,2048]{2,1,0:T(8,128)(2,1)} %refs_0_.5, bf16[144,2048]{1,0:T(8,128)(2,1)S(1)} %join_1.1.refs_1_, bf16[144,2048]{1,0:T(8,128)(2,1)S(1)} %collective-permute-done.refs_1_.refs_11_.refs_4_.refs_2_.refs_0_, ...), custom_call_target="tpu_custom_call" | custom-call | flops 1 | bytes 1 | tf_op jit(solution)/shard_map/load/pallas_call | solution.py:31
  41.6 1.1 gated_0.1
  42.7 13.5 %collective-permute-start.8 = (bf16[256,2048]{1,0:T(8,128)(2,1)S(1)}, bf16[256,2048]{1,0:T(8,128)(2,1)S(1)}, u32[]{:S(2)}, u32[]{:S(2)}) collective-permute-start(bf16[256,2048]{1,0:T(8,128)(2,1)S(1)} %get-tuple-element.68.refs_9_.refs_3_.refs_0_), channel_id=1, source_target_pairs={{0,8},{8,0},{16,24},{24,16},{1,9},{9,1},{17,25},{25,17},{2,10},{10... | collective-permute-start | bytes 3145736 | tf_op jit(solution)/shard_map/ppermute | solution.py:505
  56.3 2.5 %collective-permute-start.9 = (bf16[256,2048]{1,0:T(8,128)(2,1)S(1)}, bf16[256,2048]{1,0:T(8,128)(2,1)S(1)}, u32[]{:S(2)}, u32[]{:S(2)}) collective-permute-start(bf16[256,2048]{1,0:T(8,128)(2,1)S(1)} %get-tuple-element.68.refs_9_.refs_3_.refs_0_), channel_id=1, source_target_pairs={{0,16},{8,24},{16,0},{24,8},{1,17},{9,25},{17,1},{25,9},{2,18},{10... | collective-permute-start | bytes 3145736 | tf_op jit(solution)/shard_map/ppermute | solution.py:505
  58.8 1.1 gated_1.1
  59.9 0.7 collective-permute-start.6
  60.6 2.9 %own_0.1 = (bf16[1,128,2048]{2,1,0:T(8,128)(2,1)S(1)}, bf16[1,128,2048]{2,1,0:T(8,128)(2,1)S(1)}) custom-call(bf16[256,2048]{1,0:T(8,128)(2,1)S(1)} %get-tuple-element.68.refs_9_.refs_3_.refs_0_, bf16[2,2048,2048]{2,1,0:T(8,128)(2,1)S(1)} %load.1.refs_8_.refs_2_.refs_1_.refs_3_.refs_5_.refs_7_.refs_6_.refs_4_, ...), custom_call_target="tpu_custom_call" | custom-call | flops 1 | bytes 1 | tf_op jit(solution)/shard_map/own_0/pallas_call | solution.py:31
  63.6 1.6 collective-permute-start.11
  65.2 2.9 %own_1.1 = (bf16[1,128,2048]{2,1,0:T(8,128)(2,1)S(1)}, bf16[1,128,2048]{2,1,0:T(8,128)(2,1)S(1)}) custom-call(bf16[256,2048]{1,0:T(8,128)(2,1)S(1)} %get-tuple-element.70.refs_4_.refs_2_.refs_3_.refs_0_, bf16[2,2048,2048]{2,1,0:T(8,128)(2,1)S(1)} %load.1.refs_8_.refs_2_.refs_1_.refs_3_.refs_5_.refs_7_.refs_6_.refs_4_, f32[8,256]{1,0:T(8,128)S(1)} %sums_1.1.refs_2_.refs_0_, ...), custom_call_target="tpu_custom_call" | custom-call | flops 1 | bytes 1 | tf_op jit(solution)/shard_map/own_1/pallas_call | solution.py:31
  68.2 2.6 %collective-permute-start.12 = (f32[8,256]{1,0:T(8,128)S(1)}, f32[8,256]{1,0:T(8,128)S(1)}, u32[]{:S(2)}, u32[]{:S(2)}) collective-permute-start(f32[8,256]{1,0:T(8,128)S(1)} %sums_2.1.refs_0_), channel_id=1, source_target_pairs={{0,4},{1,5},{2,6},{3,7},{4,0},{5,1},{6,2},{7,3},{8,12},{9,13},{10,... | collective-permute-start | bytes 24584 | tf_op jit(solution)/shard_map/ppermute | solution.py:537
  70.8 2.0 %collective-permute-done.12.refs_1_ = f32[8,256]{1,0:T(8,128)S(1)} collective-permute-done((f32[8,256]{1,0:T(8,128)S(1)}, f32[8,256]{1,0:T(8,128)S(1)}, u32[]{:S(2)}, u32[]{:S(2)}) %collective-permute-start.12) | collective-permute-done | bytes 8224 | tf_op jit(solution)/shard_map/ppermute | solution.py:537
  72.8 7.5 %collective-permute-done.8.refs_0_ = bf16[256,2048]{1,0:T(8,128)(2,1)S(1)} collective-permute-done((bf16[256,2048]{1,0:T(8,128)(2,1)S(1)}, bf16[256,2048]{1,0:T(8,128)(2,1)S(1)}, u32[]{:S(2)}, u32[]{:S(2)}) %collective-permute-start.8) | collective-permute-done | bytes 1048608 | tf_op jit(solution)/shard_map/ppermute | solution.py:505
  80.3 2.5 %collective-permute-done.9.refs_1_ = bf16[256,2048]{1,0:T(8,128)(2,1)S(1)} collective-permute-done((bf16[256,2048]{1,0:T(8,128)(2,1)S(1)}, bf16[256,2048]{1,0:T(8,128)(2,1)S(1)}, u32[]{:S(2)}, u32[]{:S(2)}) %collective-permute-start.9) | collective-permute-done | bytes 1048608 | tf_op jit(solution)/shard_map/ppermute | solution.py:505
  82.8 5.3 %next_0.1 = (bf16[2,128,2048]{2,1,0:T(8,128)(2,1)S(1)}, bf16[1,128,2048]{2,1,0:T(8,128)(2,1)S(1)}, bf16[1,128,2048]{2,1,0:T(8,128)(2,1)S(1)}, bf16[128,2048]{1,0:T(8,128)(2,1)S(1)}, bf16[128,2048]{1,0:T(8,128)(2,1)S(1)}) custom-call(bf16[256,2048]{1,0:T(8,128)(2,1)S(1)} %collective-permute-done.8.refs_0_, ...), custom_call_target="tpu_custom_call" | custom-call | flops 1 | bytes 1 | tf_op jit(solution)/shard_map/next_0/pallas_call | solution.py:31
  88.2 0.5 collective-permute-start.14
  88.8 1.3 collective-permute-done.13.refs_2_
  90.1 0.7 collective-permute-done.14.refs_3_
  90.8 0.3 sum_next_0.1
  91.2 3.5 %collective-permute-start.19 = (bf16[128,2048]{1,0:T(8,128)(2,1)S(1)}, bf16[128,2048]{1,0:T(8,128)(2,1)S(1)}, u32[]{:S(2)}, u32[]{:S(2)}) collective-permute-start(bf16[128,2048]{1,0:T(8,128)(2,1)S(1)} %get-tuple-element.82.refs_3_.refs_7_.refs_6_.refs_9_.refs_8_.refs_5_.refs_4_.refs_2_.refs_0_), channel_id=1, source_target_pairs={{0,2},{1,3},{6,4},{7,5},{10,8},{11,9},{14,12},{15,13},{12,14},{13,... | collective-permute-start | bytes 1572872 | tf_op jit(solution)/shard_map/ppermute | solution.py:533
  94.9 3.9 %collective-permute-done.6.refs_0_ = bf16[256,2048]{1,0:T(8,128)(2,1)S(1)} collective-permute-done((bf16[256,2048]{1,0:T(8,128)(2,1)S(1)}, bf16[256,2048]{1,0:T(8,128)(2,1)S(1)}, u32[]{:S(2)}, u32[]{:S(2)}) %collective-permute-start.6) | collective-permute-done | bytes 1048608 | tf_op jit(solution)/shard_map/ppermute | solution.py:505
  98.8 3.6 %collective-permute-done.7.refs_1_ = bf16[256,2048]{1,0:T(8,128)(2,1)S(1)} collective-permute-done((bf16[256,2048]{1,0:T(8,128)(2,1)S(1)}, bf16[256,2048]{1,0:T(8,128)(2,1)S(1)}, u32[]{:S(2)}, u32[]{:S(2)}) %collective-permute-start.7) | collective-permute-done | bytes 1048608 | tf_op jit(solution)/shard_map/ppermute | solution.py:505
  102.4 1.7 collective-permute-start.16
  104.1 0.4 collective-permute-start.17
  104.5 4.0 %collective-permute-start.20 = (bf16[128,2048]{1,0:T(8,128)(2,1)S(1)}, bf16[128,2048]{1,0:T(8,128)(2,1)S(1)}, u32[]{:S(2)}, u32[]{:S(2)}) collective-permute-start(bf16[128,2048]{1,0:T(8,128)(2,1)S(1)} %pick_0.1.refs_3_), channel_id=1, source_target_pairs={{0,2},{1,3},{6,4},{7,5},{8,10},{9,11},{14,12},{15,13},{16,18},{17,... | collective-permute-start | bytes 1572872 | tf_op jit(solution)/shard_map/ppermute | solution.py:533
  108.6 5.3 %next_1.1 = (bf16[2,128,2048]{2,1,0:T(8,128)(2,1)S(1)}, bf16[2,128,2048]{2,1,0:T(8,128)(2,1)S(1)}, bf16[128,2048]{1,0:T(8,128)(2,1)S(1)}, bf16[128,2048]{1,0:T(8,128)(2,1)S(1)}) custom-call(bf16[256,2048]{1,0:T(8,128)(2,1)S(1)} %collective-permute-done.6.refs_0_, bf16[256,2048]{1,0:T(8,128)(2,1)S(1)} %collective-permute-done.7.refs_1_, ...), custom_call_target="tpu_custom_call" | custom-call | flops 1 | bytes 1 | tf_op jit(solution)/shard_map/next_1/pallas_call | solution.py:31
  114.1 0.9 collective-permute-start.27
  115.0 0.7 collective-permute-start.25
  115.7 1.6 collective-permute-start.26
  117.4 0.3 sum_next_1.1
  117.7 2.9 %opposite_0.1 = (bf16[1,128,2048]{2,1,0:T(8,128)(2,1)S(1)}, bf16[1,128,1024]{2,1,0:T(8,128)(2,1)S(1)}, bf16[1,128,1024]{2,1,0:T(8,128)(2,1)S(1)}) custom-call(bf16[128,2048]{1,0:T(8,128)(2,1)S(1)} %collective-permute-done.16.refs_0_.refs_2_.refs_4_, bf16[128,2048]{1,0:T(8,128)(2,1)S(1)} %collective-permute-done.17.refs_1_.refs_3_.refs_5_, ...), custom_call_target="tpu_custom_call" | custom-call | flops 1 | bytes 1 | tf_op jit(solution)/shard_map/opposite_0/pallas_call | solution.py:31
  120.9 0.4 collective-permute-start.23
  121.2 1.0 collective-permute-done.22.refs_3_
  122.3 0.4 collective-permute-done.23.refs_4_
  122.6 0.3 sum_opposite_0.1
  123.0 5.0 %collective-permute-start.30 = (bf16[128,2048]{1,0:T(8,128)(2,1)S(1)}, bf16[128,2048]{1,0:T(8,128)(2,1)S(1)}, u32[]{:S(2)}, u32[]{:S(2)}) collective-permute-start(bf16[128,2048]{1,0:T(8,128)(2,1)S(1)} %get-tuple-element.95.refs_0_.refs_11_.refs_13_.refs_10_.refs_8_.refs_9_.refs_3_), channel_id=1, source_target_pairs={{2,0},{3,1},{6,4},{7,5},{4,6},{5,7},{0,2},{1,3},{8,10},{9,11},{14,... | collective-permute-start | bytes 1572872 | tf_op jit(solution)/shard_map/ppermute | solution.py:533
  128.0 1.9 %collective-permute-start.24 = (bf16[128,2048]{1,0:T(8,128)(2,1)S(1)}, bf16[128,2048]{1,0:T(8,128)(2,1)S(1)}, u32[]{:S(2)}, u32[]{:S(2)}) collective-permute-start(bf16[128,2048]{1,0:T(8,128)(2,1)S(1)} %release_n1.1.refs_9_.refs_11_.refs_8_.refs_6_.refs_7_.refs_10_.refs_0_), channel_id=1, source_target_pairs={{0,2},{1,3},{6,4},{7,5},{10,8},{11,9},{14,12},{15,13},{12,14},{13,... | collective-permute-start | bytes 1572872 | tf_op jit(solution)/shard_map/ppermute | solution.py:533
  130.0 2.9 %opposite_1.1 = (bf16[1,128,2048]{2,1,0:T(8,128)(2,1)S(1)}, bf16[1,128,1024]{2,1,0:T(8,128)(2,1)S(1)}, bf16[1,128,1024]{2,1,0:T(8,128)(2,1)S(1)}) custom-call(bf16[128,2048]{1,0:T(8,128)(2,1)S(1)} %collective-permute-done.25.refs_0_, bf16[128,2048]{1,0:T(8,128)(2,1)S(1)} %collective-permute-done.26.refs_1_, ...), custom_call_target="tpu_custom_call" | custom-call | flops 99999997952 | bytes 1 | tf_op jit(solution)/shard_map/opposite_1/pallas_call | solution.py:31
  133.1 0.5 collective-permute-start.29
  133.6 1.0 collective-permute-done.28.refs_3_
  134.6 0.4 collective-permute-done.29.refs_4_
  135.3 5.0 %collective-permute-start.32 = (bf16[128,2048]{1,0:T(8,128)(2,1)S(1)}, bf16[128,2048]{1,0:T(8,128)(2,1)S(1)}, u32[]{:S(2)}, u32[]{:S(2)}) collective-permute-start(bf16[128,2048]{1,0:T(8,128)(2,1)S(1)} %get-tuple-element.102.refs_12_.refs_10_.refs_11_.refs_0_.refs_13_.refs_3_), channel_id=1, source_target_pairs={{2,0},{3,1},{6,4},{7,5},{4,6},{5,7},{0,2},{1,3},{8,10},{9,11},{14,... | collective-permute-start | bytes 1572872 | tf_op jit(solution)/shard_map/ppermute | solution.py:533
  140.5 1.3 collective-permute-start.33
  141.9 9.6 %collective-permute-done.24.refs_1_ = bf16[128,2048]{1,0:T(8,128)(2,1)S(1)} collective-permute-done((bf16[128,2048]{1,0:T(8,128)(2,1)S(1)}, bf16[128,2048]{1,0:T(8,128)(2,1)S(1)}, u32[]{:S(2)}, u32[]{:S(2)}) %collective-permute-start.24) | collective-permute-done | bytes 524320 | tf_op jit(solution)/shard_map/ppermute | solution.py:533
  151.6 0.7 collective-permute-start.31
  152.4 6.6 %collective-permute-start.35 = (bf16[128,2048]{1,0:T(8,128)(2,1)S(1)}, bf16[128,2048]{1,0:T(8,128)(2,1)S(1)}, u32[]{:S(2)}, u32[]{:S(2)}) collective-permute-start(bf16[128,2048]{1,0:T(8,128)(2,1)S(1)} %pick_1.1.refs_2_), channel_id=1, source_target_pairs={{0,2},{1,3},{6,4},{7,5},{8,10},{9,11},{14,12},{15,13},{16,18},{17,... | collective-permute-start | bytes 1572872 | tf_op jit(solution)/shard_map/ppermute | solution.py:533
  158.9 0.7 collective-permute-start.36
  159.6 4.3 %collective-permute-done.32.refs_1_.refs_15_.refs_5_ = bf16[128,2048]{1,0:T(8,128)(2,1)S(1)} collective-permute-done((bf16[128,2048]{1,0:T(8,128)(2,1)S(1)}, bf16[128,2048]{1,0:T(8,128)(2,1)S(1)}, u32[]{:S(2)}, u32[]{:S(2)}) %collective-permute-start.32) | collective-permute-done | bytes 524320 | tf_op jit(solution)/shard_map/ppermute | solution.py:533
  164.0 1.3 collective-permute-start.34
  165.3 7.9 %collective-permute-done.35.refs_17_.refs_8_ = bf16[128,2048]{1,0:T(8,128)(2,1)S(1)} collective-permute-done((bf16[128,2048]{1,0:T(8,128)(2,1)S(1)}, bf16[128,2048]{1,0:T(8,128)(2,1)S(1)}, u32[]{:S(2)}, u32[]{:S(2)}) %collective-permute-start.35) | collective-permute-done | bytes 524320 | tf_op jit(solution)/shard_map/ppermute | solution.py:533
  173.2 1.1 last_0.1.refs_10_
  174.3 6.1 %collective-permute-done.34.refs_7_ = bf16[128,2048]{1,0:T(8,128)(2,1)S(1)} collective-permute-done((bf16[128,2048]{1,0:T(8,128)(2,1)S(1)}, bf16[128,2048]{1,0:T(8,128)(2,1)S(1)}, u32[]{:S(2)}, u32[]{:S(2)}) %collective-permute-start.34) | collective-permute-done | bytes 524320 | tf_op jit(solution)/shard_map/ppermute | solution.py:533
  180.3 1.1 last_1.1
  (54 shorter events, 2.2 us)
Async XLA Ops:
  4.0 18.6 %collective-permute-start = (bf16[144,2048]{1,0:T(8,128)(2,1)S(1)}, bf16[144,2048]{1,0:T(8,128)(2,1)S(1)}, u32[]{:S(2)}, u32[]{:S(2)}) collective-permute-start(bf16[144,2048]{1,0:T(8,128)(2,1)S(1)} %get-tuple-element.54.refs_7_.refs_8_.refs_0_), channel_id=1, source_target_pairs={{0,8},{16,24},{1,9},{17,25},{2,10},{18,26},{3,11},{19,27},{4,12},{... | collective-permute-start | bytes 1769480 | tf_op jit(solution)/shard_map/ppermute | solution.py:513
  12.8 21.2 %collective-permute-start.3 = (bf16[144,2048]{1,0:T(8,128)(2,1)S(1)}, bf16[144,2048]{1,0:T(8,128)(2,1)S(1)}, u32[]{:S(2)}, u32[]{:S(2)}) collective-permute-start(bf16[144,2048]{1,0:T(8,128)(2,1)S(1)} %get-tuple-element.59.refs_9_.refs_4_.refs_12_.refs_0_), channel_id=1, source_target_pairs={{0,8},{16,24},{1,9},{17,25},{2,10},{18,26},{3,11},{19,27},{4,12},{... | collective-permute-start | bytes 1769480 | tf_op jit(solution)/shard_map/ppermute | solution.py:515
  22.7 11.3 %collective-permute-start.1 = (bf16[144,2048]{1,0:T(8,128)(2,1)S(1)}, bf16[144,2048]{1,0:T(8,128)(2,1)S(1)}, u32[]{:S(2)}, u32[]{:S(2)}) collective-permute-start(bf16[144,2048]{1,0:T(8,128)(2,1)S(1)} %join_0.1.refs_8_), channel_id=1, source_target_pairs={{8,16},{9,17},{10,18},{11,19},{12,20},{13,21},{14,22},{15,23}} | collective-permute-start | bytes 1769480 | tf_op jit(solution)/shard_map/ppermute | solution.py:518
  23.4 10.6 %collective-permute-start.2 = (bf16[144,2048]{1,0:T(8,128)(2,1)S(1)}, bf16[144,2048]{1,0:T(8,128)(2,1)S(1)}, u32[]{:S(2)}, u32[]{:S(2)}) collective-permute-start(bf16[144,2048]{1,0:T(8,128)(2,1)S(1)} %join_0.1.refs_8_), channel_id=1, source_target_pairs={{8,24},{9,25},{10,26},{11,27},{12,28},{13,29},{14,30},{15,31}} | collective-permute-start | bytes 1769480 | tf_op jit(solution)/shard_map/ppermute | solution.py:518
  34.2 7.4 %copy-start = (bf16[2,256,128]{2,1,0:T(8,128)(2,1)S(1)}, bf16[2,256,128]{2,1,0:T(8,128)(2,1)}, u32[]{:S(2)}) copy-start(bf16[2,256,128]{2,1,0:T(8,128)(2,1)} %refs_3_.7) | copy-start | bytes 393220
  34.2 7.4 %copy-start.3 = (f32[2,2048]{1,0:T(2,128)S(1)}, f32[2,2048]{1,0:T(2,128)}, u32[]{:S(2)}) copy-start(f32[2,2048]{1,0:T(2,128)} %refs_7_.7) | copy-start | bytes 49156
  34.2 7.3 %collective-permute-start.4 = (bf16[144,2048]{1,0:T(8,128)(2,1)S(1)}, bf16[144,2048]{1,0:T(8,128)(2,1)S(1)}, u32[]{:S(2)}, u32[]{:S(2)}) collective-permute-start(bf16[144,2048]{1,0:T(8,128)(2,1)S(1)} %join_1.1.refs_1_), channel_id=1, source_target_pairs={{8,16},{9,17},{10,18},{11,19},{12,20},{13,21},{14,22},{15,23}} | collective-permute-start | bytes 1769480 | tf_op jit(solution)/shard_map/ppermute | solution.py:521
  35.1 6.5 %collective-permute-start.5 = (bf16[144,2048]{1,0:T(8,128)(2,1)S(1)}, bf16[144,2048]{1,0:T(8,128)(2,1)S(1)}, u32[]{:S(2)}, u32[]{:S(2)}) collective-permute-start(bf16[144,2048]{1,0:T(8,128)(2,1)S(1)} %join_1.1.refs_1_), channel_id=1, source_target_pairs={{8,24},{9,25},{10,26},{11,27},{12,28},{13,29},{14,30},{15,31}} | collective-permute-start | bytes 1769480 | tf_op jit(solution)/shard_map/ppermute | solution.py:521
  42.7 37.6 %collective-permute-start.8 = (bf16[256,2048]{1,0:T(8,128)(2,1)S(1)}, bf16[256,2048]{1,0:T(8,128)(2,1)S(1)}, u32[]{:S(2)}, u32[]{:S(2)}) collective-permute-start(bf16[256,2048]{1,0:T(8,128)(2,1)S(1)} %get-tuple-element.68.refs_9_.refs_3_.refs_0_), channel_id=1, source_target_pairs={{0,8},{8,0},{16,24},{24,16},{1,9},{9,1},{17,25},{25,17},{2,10},{10... | collective-permute-start | bytes 3145736 | tf_op jit(solution)/shard_map/ppermute | solution.py:505
  56.3 26.6 %collective-permute-start.9 = (bf16[256,2048]{1,0:T(8,128)(2,1)S(1)}, bf16[256,2048]{1,0:T(8,128)(2,1)S(1)}, u32[]{:S(2)}, u32[]{:S(2)}) collective-permute-start(bf16[256,2048]{1,0:T(8,128)(2,1)S(1)} %get-tuple-element.68.refs_9_.refs_3_.refs_0_), channel_id=1, source_target_pairs={{0,16},{8,24},{16,0},{24,8},{1,17},{9,25},{17,1},{25,9},{2,18},{10... | collective-permute-start | bytes 3145736 | tf_op jit(solution)/shard_map/ppermute | solution.py:505
  59.9 38.9 %collective-permute-start.6 = (bf16[256,2048]{1,0:T(8,128)(2,1)S(1)}, bf16[256,2048]{1,0:T(8,128)(2,1)S(1)}, u32[]{:S(2)}, u32[]{:S(2)}) collective-permute-start(bf16[256,2048]{1,0:T(8,128)(2,1)S(1)} %get-tuple-element.70.refs_4_.refs_2_.refs_3_.refs_0_), channel_id=1, source_target_pairs={{0,8},{8,0},{16,24},{24,16},{1,9},{9,1},{17,25},{25,17},{2,10},{10... | collective-permute-start | bytes 3145736 | tf_op jit(solution)/shard_map/ppermute | solution.py:505
  60.6 41.8 %collective-permute-start.7 = (bf16[256,2048]{1,0:T(8,128)(2,1)S(1)}, bf16[256,2048]{1,0:T(8,128)(2,1)S(1)}, u32[]{:S(2)}, u32[]{:S(2)}) collective-permute-start(bf16[256,2048]{1,0:T(8,128)(2,1)S(1)} %get-tuple-element.70.refs_4_.refs_2_.refs_3_.refs_0_), channel_id=1, source_target_pairs={{0,16},{8,24},{16,0},{24,8},{1,17},{9,25},{17,1},{25,9},{2,18},{10... | collective-permute-start | bytes 3145736 | tf_op jit(solution)/shard_map/ppermute | solution.py:505
  60.6 3.0 %collective-permute-start.10 = (f32[8,256]{1,0:T(8,128)S(1)}, f32[8,256]{1,0:T(8,128)S(1)}, u32[]{:S(2)}, u32[]{:S(2)}) collective-permute-start(f32[8,256]{1,0:T(8,128)S(1)} %sums_0.1.refs_3_.refs_0_), channel_id=1, source_target_pairs={{0,1},{1,0},{2,3},{3,2},{4,5},{5,4},{6,7},{7,6},{8,9},{9,8},{10,11... | collective-permute-start | bytes 24584 | tf_op jit(solution)/shard_map/ppermute | solution.py:537
  63.6 4.6 %collective-permute-start.11 = (f32[8,256]{1,0:T(8,128)S(1)}, f32[8,256]{1,0:T(8,128)S(1)}, u32[]{:S(2)}, u32[]{:S(2)}) collective-permute-start(f32[8,256]{1,0:T(8,128)S(1)} %sums_1.1.refs_2_.refs_0_), channel_id=1, source_target_pairs={{0,2},{1,3},{2,0},{3,1},{4,6},{5,7},{6,4},{7,5},{8,10},{9,11},{10,... | collective-permute-start | bytes 24584 | tf_op jit(solution)/shard_map/ppermute | solution.py:537
  68.2 4.6 %collective-permute-start.12 = (f32[8,256]{1,0:T(8,128)S(1)}, f32[8,256]{1,0:T(8,128)S(1)}, u32[]{:S(2)}, u32[]{:S(2)}) collective-permute-start(f32[8,256]{1,0:T(8,128)S(1)} %sums_2.1.refs_0_), channel_id=1, source_target_pairs={{0,4},{1,5},{2,6},{3,7},{4,0},{5,1},{6,2},{7,3},{8,12},{9,13},{10,... | collective-permute-start | bytes 24584 | tf_op jit(solution)/shard_map/ppermute | solution.py:537
  72.8 15.9 %collective-permute-start.15 = (bf16[1,128,2048]{2,1,0:T(8,128)(2,1)S(1)}, bf16[1,128,2048]{2,1,0:T(8,128)(2,1)S(1)}, u32[]{:S(2)}, u32[]{:S(2)}) collective-permute-start(bf16[1,128,2048]{2,1,0:T(8,128)(2,1)S(1)} %get-tuple-element.73.refs_5_.refs_4_.refs_2_), channel_id=1, source_target_pairs={{0,1},{1,0},{2,3},{3,2},{4,5},{5,4},{6,7},{7,6},{8,9},{9,8},{10,11... | collective-permute-start | bytes 1572872 | tf_op jit(solution)/shard_map/ppermute | solution.py:504
  72.8 15.3 %copy-start.1 = (f32[8,256]{1,0:T(8,128)}, f32[8,256]{1,0:T(8,128)S(1)}, u32[]{:S(2)}) copy-start(f32[8,256]{1,0:T(8,128)S(1)} %sums_4.1.refs_3_.refs_2_) | copy-start | bytes 24580
  88.1 2.0 %collective-permute-start.13 = (bf16[1,128,2048]{2,1,0:T(8,128)(2,1)S(1)}, bf16[1,128,2048]{2,1,0:T(8,128)(2,1)S(1)}, u32[]{:S(2)}, u32[]{:S(2)}) collective-permute-start(bf16[1,128,2048]{2,1,0:T(8,128)(2,1)S(1)} %get-tuple-element.77), channel_id=1, source_target_pairs={{0,1},{1,0},{2,3},{3,2},{4,5},{5,4},{6,7},{7,6},{8,9},{9,8},{10,11... | collective-permute-start | bytes 1572872 | tf_op jit(solution)/shard_map/ppermute | solution.py:504
  88.2 2.6 %collective-permute-start.14 = (bf16[1,128,2048]{2,1,0:T(8,128)(2,1)S(1)}, bf16[1,128,2048]{2,1,0:T(8,128)(2,1)S(1)}, u32[]{:S(2)}, u32[]{:S(2)}) collective-permute-start(bf16[1,128,2048]{2,1,0:T(8,128)(2,1)S(1)} %get-tuple-element.78), channel_id=1, source_target_pairs={{0,1},{1,0},{2,3},{3,2},{4,5},{5,4},{6,7},{7,6},{8,9},{9,8},{10,11... | collective-permute-start | bytes 1572872 | tf_op jit(solution)/shard_map/ppermute | solution.py:504
  88.7 25.2 %collective-permute-start.18 = (bf16[1,128,2048]{2,1,0:T(8,128)(2,1)S(1)}, bf16[1,128,2048]{2,1,0:T(8,128)(2,1)S(1)}, u32[]{:S(2)}, u32[]{:S(2)}) collective-permute-start(bf16[1,128,2048]{2,1,0:T(8,128)(2,1)S(1)} %get-tuple-element.75.refs_6_.refs_8_.refs_10_.refs_9_), channel_id=1, source_target_pairs={{0,1},{1,0},{2,3},{3,2},{4,5},{5,4},{6,7},{7,6},{8,9},{9,8},{10,11... | collective-permute-start | bytes 1572872 | tf_op jit(solution)/shard_map/ppermute | solution.py:504
  91.2 22.8 %collective-permute-start.19 = (bf16[128,2048]{1,0:T(8,128)(2,1)S(1)}, bf16[128,2048]{1,0:T(8,128)(2,1)S(1)}, u32[]{:S(2)}, u32[]{:S(2)}) collective-permute-start(bf16[128,2048]{1,0:T(8,128)(2,1)S(1)} %get-tuple-element.82.refs_3_.refs_7_.refs_6_.refs_9_.refs_8_.refs_5_.refs_4_.refs_2_.refs_0_), channel_id=1, source_target_pairs={{0,2},{1,3},{6,4},{7,5},{10,8},{11,9},{14,12},{15,13},{12,14},{13,... | collective-permute-start | bytes 1572872 | tf_op jit(solution)/shard_map/ppermute | solution.py:533
  102.4 12.6 %collective-permute-start.16 = (bf16[128,2048]{1,0:T(8,128)(2,1)S(1)}, bf16[128,2048]{1,0:T(8,128)(2,1)S(1)}, u32[]{:S(2)}, u32[]{:S(2)}) collective-permute-start(bf16[128,2048]{1,0:T(8,128)(2,1)S(1)} %get-tuple-element.83.refs_3_), channel_id=1, source_target_pairs={{0,16},{8,24},{16,0},{24,8},{1,17},{9,25},{17,1},{25,9},{2,18},{10... | collective-permute-start | bytes 1572872 | tf_op jit(solution)/shard_map/ppermute | solution.py:505
  104.1 10.9 %collective-permute-start.17 = (bf16[128,2048]{1,0:T(8,128)(2,1)S(1)}, bf16[128,2048]{1,0:T(8,128)(2,1)S(1)}, u32[]{:S(2)}, u32[]{:S(2)}) collective-permute-start(bf16[128,2048]{1,0:T(8,128)(2,1)S(1)} %get-tuple-element.84), channel_id=1, source_target_pairs={{0,8},{8,0},{16,24},{24,16},{1,9},{9,1},{17,25},{25,17},{2,10},{10... | collective-permute-start | bytes 1572872 | tf_op jit(solution)/shard_map/ppermute | solution.py:505
  104.5 12.8 %collective-permute-start.20 = (bf16[128,2048]{1,0:T(8,128)(2,1)S(1)}, bf16[128,2048]{1,0:T(8,128)(2,1)S(1)}, u32[]{:S(2)}, u32[]{:S(2)}) collective-permute-start(bf16[128,2048]{1,0:T(8,128)(2,1)S(1)} %pick_0.1.refs_3_), channel_id=1, source_target_pairs={{0,2},{1,3},{6,4},{7,5},{8,10},{9,11},{14,12},{15,13},{16,18},{17,... | collective-permute-start | bytes 1572872 | tf_op jit(solution)/shard_map/ppermute | solution.py:533
  113.8 3.5 %collective-permute-start.21 = (bf16[2,128,2048]{2,1,0:T(8,128)(2,1)S(1)}, bf16[2,128,2048]{2,1,0:T(8,128)(2,1)S(1)}, u32[]{:S(2)}, u32[]{:S(2)}) collective-permute-start(bf16[2,128,2048]{2,1,0:T(8,128)(2,1)S(1)} %get-tuple-element.89), channel_id=1, source_target_pairs={{0,1},{1,0},{2,3},{3,2},{4,5},{5,4},{6,7},{7,6},{8,9},{9,8},{10,11... | collective-permute-start | bytes 3145736 | tf_op jit(solution)/shard_map/ppermute | solution.py:504
  114.1 15.9 %collective-permute-start.27 = (bf16[128,2048]{1,0:T(8,128)(2,1)S(1)}, bf16[128,2048]{1,0:T(8,128)(2,1)S(1)}, u32[]{:S(2)}, u32[]{:S(2)}) collective-permute-start(bf16[128,2048]{1,0:T(8,128)(2,1)S(1)} %add_next_0.1.refs_9_.refs_10_.refs_12_.refs_11_.refs_8_.refs_6_.refs_5_.refs_3_.refs_4_.refs_1_), channel_id=1, source_target_pairs={{2,4},{3,5},{4,2},{5,3},{12,8},{13,9},{10,14},{11,15},{20,16},{21,... | collective-permute-start | bytes 1572872 | tf_op jit(solution)/shard_map/ppermute | solution.py:533
  115.0 15.0 %collective-permute-start.25 = (bf16[128,2048]{1,0:T(8,128)(2,1)S(1)}, bf16[128,2048]{1,0:T(8,128)(2,1)S(1)}, u32[]{:S(2)}, u32[]{:S(2)}) collective-permute-start(bf16[128,2048]{1,0:T(8,128)(2,1)S(1)} %get-tuple-element.88.refs_0_), channel_id=1, source_target_pairs={{0,16},{8,24},{16,0},{24,8},{1,17},{9,25},{17,1},{25,9},{2,18},{10... | collective-permute-start | bytes 1572872 | tf_op jit(solution)/shard_map/ppermute | solution.py:505
  115.7 14.3 %collective-permute-start.26 = (bf16[128,2048]{1,0:T(8,128)(2,1)S(1)}, bf16[128,2048]{1,0:T(8,128)(2,1)S(1)}, u32[]{:S(2)}, u32[]{:S(2)}) collective-permute-start(bf16[128,2048]{1,0:T(8,128)(2,1)S(1)} %get-tuple-element.97), channel_id=1, source_target_pairs={{0,8},{8,0},{16,24},{24,16},{1,9},{9,1},{17,25},{25,17},{2,10},{10... | collective-permute-start | bytes 1572872 | tf_op jit(solution)/shard_map/ppermute | solution.py:505
  120.7 1.6 collective-permute-start.22
  120.9 1.8 collective-permute-start.23
  123.0 17.4 %collective-permute-start.30 = (bf16[128,2048]{1,0:T(8,128)(2,1)S(1)}, bf16[128,2048]{1,0:T(8,128)(2,1)S(1)}, u32[]{:S(2)}, u32[]{:S(2)}) collective-permute-start(bf16[128,2048]{1,0:T(8,128)(2,1)S(1)} %get-tuple-element.95.refs_0_.refs_11_.refs_13_.refs_10_.refs_8_.refs_9_.refs_3_), channel_id=1, source_target_pairs={{2,0},{3,1},{6,4},{7,5},{4,6},{5,7},{0,2},{1,3},{8,10},{9,11},{14,... | collective-permute-start | bytes 1572872 | tf_op jit(solution)/shard_map/ppermute | solution.py:533
  128.0 23.5 %collective-permute-start.24 = (bf16[128,2048]{1,0:T(8,128)(2,1)S(1)}, bf16[128,2048]{1,0:T(8,128)(2,1)S(1)}, u32[]{:S(2)}, u32[]{:S(2)}) collective-permute-start(bf16[128,2048]{1,0:T(8,128)(2,1)S(1)} %release_n1.1.refs_9_.refs_11_.refs_8_.refs_6_.refs_7_.refs_10_.refs_0_), channel_id=1, source_target_pairs={{0,2},{1,3},{6,4},{7,5},{10,8},{11,9},{14,12},{15,13},{12,14},{13,... | collective-permute-start | bytes 1572872 | tf_op jit(solution)/shard_map/ppermute | solution.py:533
  133.0 25.9 %copy-start.2 = (f32[8,256]{1,0:T(8,128)S(1)}, f32[8,256]{1,0:T(8,128)}, u32[]{:S(2)}) copy-start(f32[8,256]{1,0:T(8,128)} %copy-done.1) | copy-start | bytes 24580
  133.0 1.6 collective-permute-start.28
  133.1 1.9 %collective-permute-start.29 = (bf16[1,128,1024]{2,1,0:T(8,128)(2,1)S(1)}, bf16[1,128,1024]{2,1,0:T(8,128)(2,1)S(1)}, u32[]{:S(2)}, u32[]{:S(2)}) collective-permute-start(bf16[1,128,1024]{2,1,0:T(8,128)(2,1)S(1)} %get-tuple-element.100), channel_id=1, source_target_pairs={{0,1},{1,0},{2,3},{3,2},{4,5},{5,4},{6,7},{7,6},{8,9},{9,8},{10,11... | collective-permute-start | bytes 786440 | tf_op jit(solution)/shard_map/ppermute | solution.py:504
  135.3 28.6 %collective-permute-start.32 = (bf16[128,2048]{1,0:T(8,128)(2,1)S(1)}, bf16[128,2048]{1,0:T(8,128)(2,1)S(1)}, u32[]{:S(2)}, u32[]{:S(2)}) collective-permute-start(bf16[128,2048]{1,0:T(8,128)(2,1)S(1)} %get-tuple-element.102.refs_12_.refs_10_.refs_11_.refs_0_.refs_13_.refs_3_), channel_id=1, source_target_pairs={{2,0},{3,1},{6,4},{7,5},{4,6},{5,7},{0,2},{1,3},{8,10},{9,11},{14,... | collective-permute-start | bytes 1572872 | tf_op jit(solution)/shard_map/ppermute | solution.py:533
  140.5 23.3 %collective-permute-start.33 = (bf16[128,2048]{1,0:T(8,128)(2,1)S(1)}, bf16[128,2048]{1,0:T(8,128)(2,1)S(1)}, u32[]{:S(2)}, u32[]{:S(2)}) collective-permute-start(bf16[128,2048]{1,0:T(8,128)(2,1)S(1)} %add_opposite_0.1.refs_13_.refs_14_.refs_6_), channel_id=1, source_target_pairs={{4,0},{5,1},{2,6},{3,7},{10,12},{11,13},{12,10},{13,11},{18,20},{1... | collective-permute-start | bytes 1572872 | tf_op jit(solution)/shard_map/ppermute | solution.py:533
  151.6 13.7 %collective-permute-start.31 = (bf16[128,2048]{1,0:T(8,128)(2,1)S(1)}, bf16[128,2048]{1,0:T(8,128)(2,1)S(1)}, u32[]{:S(2)}, u32[]{:S(2)}) collective-permute-start(bf16[128,2048]{1,0:T(8,128)(2,1)S(1)} %add_next_1.1.refs_15_.refs_11_.refs_1_), channel_id=1, source_target_pairs={{2,4},{3,5},{4,2},{5,3},{12,8},{13,9},{10,14},{11,15},{20,16},{21,... | collective-permute-start | bytes 1572872 | tf_op jit(solution)/shard_map/ppermute | solution.py:533
  152.4 20.8 %collective-permute-start.35 = (bf16[128,2048]{1,0:T(8,128)(2,1)S(1)}, bf16[128,2048]{1,0:T(8,128)(2,1)S(1)}, u32[]{:S(2)}, u32[]{:S(2)}) collective-permute-start(bf16[128,2048]{1,0:T(8,128)(2,1)S(1)} %pick_1.1.refs_2_), channel_id=1, source_target_pairs={{0,2},{1,3},{6,4},{7,5},{8,10},{9,11},{14,12},{15,13},{16,18},{17,... | collective-permute-start | bytes 1572872 | tf_op jit(solution)/shard_map/ppermute | solution.py:533
  158.9 6.4 %collective-permute-start.36 = (f32[8,256]{1,0:T(8,128)S(1)}, f32[8,256]{1,0:T(8,128)S(1)}, u32[]{:S(2)}, u32[]{:S(2)}) collective-permute-start(f32[8,256]{1,0:T(8,128)S(1)} %release_sums.1), channel_id=1, source_target_pairs={{0,0},{1,1},{8,2},{9,3},{16,4},{17,5},{24,6},{25,7},{2,8},{3,9},{1... | collective-permute-start | bytes 24584 | tf_op jit(solution)/shard_map/ppermute | solution.py:600
  164.0 16.3 %collective-permute-start.34 = (bf16[128,2048]{1,0:T(8,128)(2,1)S(1)}, bf16[128,2048]{1,0:T(8,128)(2,1)S(1)}, u32[]{:S(2)}, u32[]{:S(2)}) collective-permute-start(bf16[128,2048]{1,0:T(8,128)(2,1)S(1)} %add_opposite_1.1.refs_16_.refs_6_), channel_id=1, source_target_pairs={{4,0},{5,1},{2,6},{3,7},{10,12},{11,13},{12,10},{13,11},{18,20},{1... | collective-permute-start | bytes 1572872 | tf_op jit(solution)/shard_map/ppermute | solution.py:533

commit v3 on v2

--- a/solution.py
+++ b/solution.py
@@ -307,7 +307,7 @@
                 which, place = [(r, part.index(k)) for r, (part, *_) in zip(send_refs, sends) if k in part][0]
             which[place, :, pl.ds(at, size)] = jnp.where(first, late, early)
 
-    tile = min(512, width)
+    tile = min(1024, width)
     done = set()
     for ref, (blocks, start, stop) in zip(send_refs, sends):
         if start in done:

time: 182 us -> 181 us (level)
  Pallas kernels: 53.7 us -> 51 us
    pallas_call x34, Pallas kernels: 51.5 us -> 48.8 us  [call(): pl.pallas_call(body, name=name, in_specs=[IN_VMEM] * len(operands) + [ANY...]
  transfers between devices with their start and end apart: 37 -> 37, of which waited for: 18 -> 20; matrix products, arithmetic and copies ran while one was open for 0% -> 0% of each run, Pallas kernels for 26% -> 25%
where the time goes in v3:
time: 181 us; the launch traced here: 180 us
  starting transfers between devices  67.5 us (37%)
  waiting for transfers between devices  61.2 us (34%)
  Pallas kernels  51 us (28%)
    pallas_call x34, Pallas kernels, call(): pl.pallas_call(body, name=name, in_specs=[IN_VMEM] * len(operands) + [ANY...  48.8 us
    ppermute x10, starting transfers between devices, turn(): return lax.ppermute(value, ('seq', 'head'), sends(kinds, i))  30.3 us
    ppermute x10, waiting for transfers between devices, turn(): return lax.ppermute(value, ('seq', 'head'), sends(kinds, i))  28.1 us
    ppermute x8, starting transfers between devices, fast(): beside = lambda a, k: lax.ppermute(a, 'seq', xor_pairs(n_seq, k))  21.1 us
    ppermute x8, waiting for transfers between devices, fast(): beside = lambda a, k: lax.ppermute(a, 'seq', xor_pairs(n_seq, k))  18.9 us
    ppermute x1, starting transfers between devices, fast(): near0 = lax.ppermute(msg0, 'seq', ring)  4.88 us
    ppermute x9, waiting for transfers between devices, fast(): across = lambda a: lax.ppermute(a, 'head', xor_pairs(n_head, 1))  4.87 us
    ppermute x1, waiting for transfers between devices, fast(): near1 = lax.ppermute(msg1, 'seq', ring)  4.36 us
  transfers between devices with their start and end apart: 37, of which 20 were waited for; matrix products, arithmetic and copies ran while one was open for 0% of the time, Pallas kernels for 25%

profile of v3, /device:TPU:0, one launch (start us, length us, event | category | flops | bytes accessed | tf_op | source)
XLA Modules:
  0.0 180.2 jit_solution(17287131219524609971)
XLA Ops:
  0.0 3.9 %prep_0.1 = (bf16[144,2048]{1,0:T(8,128)(2,1)S(1)}, f32[32,384]{1,0:T(8,128)S(1)}, f32[32,256]{1,0:T(8,128)S(1)}, f32[32,256]{1,0:T(8,128)S(1)}, f32[1,256]{1,0:T(1,128)S(1)}) custom-call(bf16[2,256,2048]{2,1,0:T(8,128)(2,1)} %refs_4_.7, bf16[2,256,128]{2,1,0:T(8,128)(2,1)} %refs_6_.3, f32[2,32,256]{2,1,0:T(8,128)} %bitcast.2, f32[2,32]{1,0:T(2,128)} %refs_3_.5, ...), custom_call_target="tpu_custom_call" | custom-call | flops 1 | bytes 1 | tf_op jit(solution)/shard_map/prep_0/pallas_call | solution.py:31
  4.0 4.9 %collective-permute-start = (bf16[144,2048]{1,0:T(8,128)(2,1)S(1)}, bf16[144,2048]{1,0:T(8,128)(2,1)S(1)}, u32[]{:S(2)}, u32[]{:S(2)}) collective-permute-start(bf16[144,2048]{1,0:T(8,128)(2,1)S(1)} %get-tuple-element.54.refs_7_.refs_8_.refs_0_), channel_id=1, source_target_pairs={{0,8},{16,24},{1,9},{17,25},{2,10},{18,26},{3,11},{19,27},{4,12},{... | collective-permute-start | bytes 1769480 | tf_op jit(solution)/shard_map/ppermute | solution.py:513
  8.8 4.0 %prep_1.1 = (bf16[144,2048]{1,0:T(8,128)(2,1)S(1)}, f32[32,384]{1,0:T(8,128)S(1)}, f32[32,256]{1,0:T(8,128)S(1)}, f32[32,256]{1,0:T(8,128)S(1)}, f32[1,256]{1,0:T(1,128)S(1)}) custom-call(bf16[2,256,2048]{2,1,0:T(8,128)(2,1)} %refs_4_.7, bf16[2,256,128]{2,1,0:T(8,128)(2,1)} %refs_6_.3, f32[2,32,256]{2,1,0:T(8,128)} %bitcast.3, f32[2,32]{1,0:T(2,128)} %refs_3_.5, ...), custom_call_target="tpu_custom_call" | custom-call | flops 1 | bytes 1 | tf_op jit(solution)/shard_map/prep_1/pallas_call | solution.py:31
  12.8 1.3 collective-permute-start.3
  14.1 5.4 %inside_0.1 = (bf16[256,2048]{1,0:T(8,128)(2,1)S(1)}, bf16[256,2048]{1,0:T(8,128)(2,1)S(1)}) custom-call(f32[32,384]{1,0:T(8,128)S(1)} %get-tuple-element.55.refs_8_.refs_0_, f32[32,256]{1,0:T(8,128)S(1)} %get-tuple-element.56.refs_9_.refs_1_, f32[32,256]{1,0:T(8,128)S(1)} %get-tuple-element.57.refs_10_.refs_2_, ...), custom_call_target="tpu_custom_call" | custom-call | flops 1 | bytes 1 | tf_op jit(solution)/shard_map/inside_0/pallas_call | solution.py:31
  19.5 3.0 %collective-permute-done.refs_1_.refs_11_.refs_4_.refs_2_.refs_0_ = bf16[144,2048]{1,0:T(8,128)(2,1)S(1)} collective-permute-done((bf16[144,2048]{1,0:T(8,128)(2,1)S(1)}, bf16[144,2048]{1,0:T(8,128)(2,1)S(1)}, u32[]{:S(2)}, u32[]{:S(2)}) %collective-permute-start) | collective-permute-done | bytes 589856 | tf_op jit(solution)/shard_map/ppermute | solution.py:513
  22.7 0.7 collective-permute-start.1
  23.4 0.9 collective-permute-start.2
  24.3 5.4 %inside_1.1 = (bf16[256,2048]{1,0:T(8,128)(2,1)S(1)}, bf16[256,2048]{1,0:T(8,128)(2,1)S(1)}) custom-call(f32[32,384]{1,0:T(8,128)S(1)} %get-tuple-element.60.refs_10_.refs_6_.refs_0_, f32[32,256]{1,0:T(8,128)S(1)} %get-tuple-element.61.refs_11_.refs_7_.refs_1_, f32[32,256]{1,0:T(8,128)S(1)} %get-tuple-element.62.refs_12_.refs_8_.refs_2_, ...), custom_call_target="tpu_custom_call" | custom-call | flops 1 | bytes 1 | tf_op jit(solution)/shard_map/inside_1/pallas_call | solution.py:31
  29.7 4.4 %collective-permute-done.3.refs_1_.refs_8_.refs_11_.refs_0_ = bf16[144,2048]{1,0:T(8,128)(2,1)S(1)} collective-permute-done((bf16[144,2048]{1,0:T(8,128)(2,1)S(1)}, bf16[144,2048]{1,0:T(8,128)(2,1)S(1)}, u32[]{:S(2)}, u32[]{:S(2)}) %collective-permute-start.3) | collective-permute-done | bytes 589856 | tf_op jit(solution)/shard_map/ppermute | solution.py:515
  34.2 0.8 collective-permute-start.4
  35.1 0.7 collective-permute-start.5
  35.8 5.8 %load.1.refs_8_.refs_2_.refs_1_.refs_3_.refs_5_.refs_7_.refs_6_.refs_4_ = bf16[2,2048,2048]{2,1,0:T(8,128)(2,1)S(1)} custom-call(bf16[2,2048,2048]{2,1,0:T(8,128)(2,1)} %refs_0_.5, bf16[144,2048]{1,0:T(8,128)(2,1)S(1)} %join_1.1.refs_1_, bf16[144,2048]{1,0:T(8,128)(2,1)S(1)} %collective-permute-done.refs_1_.refs_11_.refs_4_.refs_2_.refs_0_, ...), custom_call_target="tpu_custom_call" | custom-call | flops 1 | bytes 1 | tf_op jit(solution)/shard_map/load/pallas_call | solution.py:31
  41.6 1.1 gated_0.1
  42.7 13.5 %collective-permute-start.8 = (bf16[256,2048]{1,0:T(8,128)(2,1)S(1)}, bf16[256,2048]{1,0:T(8,128)(2,1)S(1)}, u32[]{:S(2)}, u32[]{:S(2)}) collective-permute-start(bf16[256,2048]{1,0:T(8,128)(2,1)S(1)} %get-tuple-element.68.refs_9_.refs_3_.refs_0_), channel_id=1, source_target_pairs={{0,8},{8,0},{16,24},{24,16},{1,9},{9,1},{17,25},{25,17},{2,10},{10... | collective-permute-start | bytes 3145736 | tf_op jit(solution)/shard_map/ppermute | solution.py:505
  56.3 2.5 %collective-permute-start.9 = (bf16[256,2048]{1,0:T(8,128)(2,1)S(1)}, bf16[256,2048]{1,0:T(8,128)(2,1)S(1)}, u32[]{:S(2)}, u32[]{:S(2)}) collective-permute-start(bf16[256,2048]{1,0:T(8,128)(2,1)S(1)} %get-tuple-element.68.refs_9_.refs_3_.refs_0_), channel_id=1, source_target_pairs={{0,16},{8,24},{16,0},{24,8},{1,17},{9,25},{17,1},{25,9},{2,18},{10... | collective-permute-start | bytes 3145736 | tf_op jit(solution)/shard_map/ppermute | solution.py:505
  58.8 1.1 gated_1.1
  59.9 0.7 collective-permute-start.6
  60.6 2.6 %own_0.1 = (bf16[1,128,2048]{2,1,0:T(8,128)(2,1)S(1)}, bf16[1,128,2048]{2,1,0:T(8,128)(2,1)S(1)}) custom-call(bf16[256,2048]{1,0:T(8,128)(2,1)S(1)} %get-tuple-element.68.refs_9_.refs_3_.refs_0_, bf16[2,2048,2048]{2,1,0:T(8,128)(2,1)S(1)} %load.1.refs_8_.refs_2_.refs_1_.refs_3_.refs_5_.refs_7_.refs_6_.refs_4_, ...), custom_call_target="tpu_custom_call" | custom-call | flops 1 | bytes 1 | tf_op jit(solution)/shard_map/own_0/pallas_call | solution.py:31
  63.2 1.6 collective-permute-start.11
  64.8 2.6 %own_1.1 = (bf16[1,128,2048]{2,1,0:T(8,128)(2,1)S(1)}, bf16[1,128,2048]{2,1,0:T(8,128)(2,1)S(1)}) custom-call(bf16[256,2048]{1,0:T(8,128)(2,1)S(1)} %get-tuple-element.70.refs_4_.refs_2_.refs_3_.refs_0_, bf16[2,2048,2048]{2,1,0:T(8,128)(2,1)S(1)} %load.1.refs_8_.refs_2_.refs_1_.refs_3_.refs_5_.refs_7_.refs_6_.refs_4_, f32[8,256]{1,0:T(8,128)S(1)} %sums_1.1.refs_2_.refs_0_, ...), custom_call_target="tpu_custom_call" | custom-call | flops 1 | bytes 1 | tf_op jit(solution)/shard_map/own_1/pallas_call | solution.py:31
  67.4 2.6 %collective-permute-start.12 = (f32[8,256]{1,0:T(8,128)S(1)}, f32[8,256]{1,0:T(8,128)S(1)}, u32[]{:S(2)}, u32[]{:S(2)}) collective-permute-start(f32[8,256]{1,0:T(8,128)S(1)} %sums_2.1.refs_0_), channel_id=1, source_target_pairs={{0,4},{1,5},{2,6},{3,7},{4,0},{5,1},{6,2},{7,3},{8,12},{9,13},{10,... | collective-permute-start | bytes 24584 | tf_op jit(solution)/shard_map/ppermute | solution.py:537
  70.1 2.0 %collective-permute-done.12.refs_1_ = f32[8,256]{1,0:T(8,128)S(1)} collective-permute-done((f32[8,256]{1,0:T(8,128)S(1)}, f32[8,256]{1,0:T(8,128)S(1)}, u32[]{:S(2)}, u32[]{:S(2)}) %collective-permute-start.12) | collective-permute-done | bytes 8224 | tf_op jit(solution)/shard_map/ppermute | solution.py:537
  72.1 8.3 %collective-permute-done.8.refs_0_ = bf16[256,2048]{1,0:T(8,128)(2,1)S(1)} collective-permute-done((bf16[256,2048]{1,0:T(8,128)(2,1)S(1)}, bf16[256,2048]{1,0:T(8,128)(2,1)S(1)}, u32[]{:S(2)}, u32[]{:S(2)}) %collective-permute-start.8) | collective-permute-done | bytes 1048608 | tf_op jit(solution)/shard_map/ppermute | solution.py:505
  80.3 2.5 %collective-permute-done.9.refs_1_ = bf16[256,2048]{1,0:T(8,128)(2,1)S(1)} collective-permute-done((bf16[256,2048]{1,0:T(8,128)(2,1)S(1)}, bf16[256,2048]{1,0:T(8,128)(2,1)S(1)}, u32[]{:S(2)}, u32[]{:S(2)}) %collective-permute-start.9) | collective-permute-done | bytes 1048608 | tf_op jit(solution)/shard_map/ppermute | solution.py:505
  82.8 4.9 %next_0.1 = (bf16[2,128,2048]{2,1,0:T(8,128)(2,1)S(1)}, bf16[1,128,2048]{2,1,0:T(8,128)(2,1)S(1)}, bf16[1,128,2048]{2,1,0:T(8,128)(2,1)S(1)}, bf16[128,2048]{1,0:T(8,128)(2,1)S(1)}, bf16[128,2048]{1,0:T(8,128)(2,1)S(1)}) custom-call(bf16[256,2048]{1,0:T(8,128)(2,1)S(1)} %collective-permute-done.8.refs_0_, ...), custom_call_target="tpu_custom_call" | custom-call | flops 1 | bytes 1 | tf_op jit(solution)/shard_map/next_0/pallas_call | solution.py:31
  87.8 0.5 collective-permute-start.14
  88.4 1.3 collective-permute-done.13.refs_2_
  89.7 0.7 collective-permute-done.14.refs_3_
  90.4 0.3 sum_next_0.1
  90.8 3.7 %collective-permute-start.19 = (bf16[128,2048]{1,0:T(8,128)(2,1)S(1)}, bf16[128,2048]{1,0:T(8,128)(2,1)S(1)}, u32[]{:S(2)}, u32[]{:S(2)}) collective-permute-start(bf16[128,2048]{1,0:T(8,128)(2,1)S(1)} %get-tuple-element.82.refs_3_.refs_7_.refs_6_.refs_9_.refs_8_.refs_5_.refs_4_.refs_2_.refs_0_), channel_id=1, source_target_pairs={{0,2},{1,3},{6,4},{7,5},{10,8},{11,9},{14,12},{15,13},{12,14},{13,... | collective-permute-start | bytes 1572872 | tf_op jit(solution)/shard_map/ppermute | solution.py:533
  94.7 4.1 %collective-permute-done.6.refs_0_ = bf16[256,2048]{1,0:T(8,128)(2,1)S(1)} collective-permute-done((bf16[256,2048]{1,0:T(8,128)(2,1)S(1)}, bf16[256,2048]{1,0:T(8,128)(2,1)S(1)}, u32[]{:S(2)}, u32[]{:S(2)}) %collective-permute-start.6) | collective-permute-done | bytes 1048608 | tf_op jit(solution)/shard_map/ppermute | solution.py:505
  98.8 3.7 %collective-permute-done.7.refs_1_ = bf16[256,2048]{1,0:T(8,128)(2,1)S(1)} collective-permute-done((bf16[256,2048]{1,0:T(8,128)(2,1)S(1)}, bf16[256,2048]{1,0:T(8,128)(2,1)S(1)}, u32[]{:S(2)}, u32[]{:S(2)}) %collective-permute-start.7) | collective-permute-done | bytes 1048608 | tf_op jit(solution)/shard_map/ppermute | solution.py:505
  102.5 1.8 collective-permute-start.16
  104.3 0.4 collective-permute-start.17
  104.7 3.9 %collective-permute-start.20 = (bf16[128,2048]{1,0:T(8,128)(2,1)S(1)}, bf16[128,2048]{1,0:T(8,128)(2,1)S(1)}, u32[]{:S(2)}, u32[]{:S(2)}) collective-permute-start(bf16[128,2048]{1,0:T(8,128)(2,1)S(1)} %pick_0.1.refs_3_), channel_id=1, source_target_pairs={{0,2},{1,3},{6,4},{7,5},{8,10},{9,11},{14,12},{15,13},{16,18},{17,... | collective-permute-start | bytes 1572872 | tf_op jit(solution)/shard_map/ppermute | solution.py:533
  108.6 4.9 %next_1.1 = (bf16[2,128,2048]{2,1,0:T(8,128)(2,1)S(1)}, bf16[2,128,2048]{2,1,0:T(8,128)(2,1)S(1)}, bf16[128,2048]{1,0:T(8,128)(2,1)S(1)}, bf16[128,2048]{1,0:T(8,128)(2,1)S(1)}) custom-call(bf16[256,2048]{1,0:T(8,128)(2,1)S(1)} %collective-permute-done.6.refs_0_, bf16[256,2048]{1,0:T(8,128)(2,1)S(1)} %collective-permute-done.7.refs_1_, ...), custom_call_target="tpu_custom_call" | custom-call | flops 1 | bytes 1 | tf_op jit(solution)/shard_map/next_1/pallas_call | solution.py:31
  113.7 0.7 collective-permute-start.27
  114.4 0.7 collective-permute-start.25
  115.1 1.6 collective-permute-start.26
  117.0 0.3 sum_next_1.1
  117.3 2.3 %opposite_0.1 = (bf16[1,128,2048]{2,1,0:T(8,128)(2,1)S(1)}, bf16[1,128,1024]{2,1,0:T(8,128)(2,1)S(1)}, bf16[1,128,1024]{2,1,0:T(8,128)(2,1)S(1)}) custom-call(bf16[128,2048]{1,0:T(8,128)(2,1)S(1)} %collective-permute-done.16.refs_0_.refs_2_.refs_4_, bf16[128,2048]{1,0:T(8,128)(2,1)S(1)} %collective-permute-done.17.refs_1_.refs_3_.refs_5_, ...), custom_call_target="tpu_custom_call" | custom-call | flops 1 | bytes 1 | tf_op jit(solution)/shard_map/opposite_0/pallas_call | solution.py:31
  119.8 0.5 collective-permute-start.23
  120.3 1.0 collective-permute-done.22.refs_3_
  121.3 0.4 collective-permute-done.23.refs_4_
  121.7 0.3 sum_opposite_0.1
  122.0 5.0 %collective-permute-start.30 = (bf16[128,2048]{1,0:T(8,128)(2,1)S(1)}, bf16[128,2048]{1,0:T(8,128)(2,1)S(1)}, u32[]{:S(2)}, u32[]{:S(2)}) collective-permute-start(bf16[128,2048]{1,0:T(8,128)(2,1)S(1)} %get-tuple-element.95.refs_0_.refs_11_.refs_13_.refs_10_.refs_8_.refs_9_.refs_3_), channel_id=1, source_target_pairs={{2,0},{3,1},{6,4},{7,5},{4,6},{5,7},{0,2},{1,3},{8,10},{9,11},{14,... | collective-permute-start | bytes 1572872 | tf_op jit(solution)/shard_map/ppermute | solution.py:533
  127.0 1.9 %collective-permute-start.24 = (bf16[128,2048]{1,0:T(8,128)(2,1)S(1)}, bf16[128,2048]{1,0:T(8,128)(2,1)S(1)}, u32[]{:S(2)}, u32[]{:S(2)}) collective-permute-start(bf16[128,2048]{1,0:T(8,128)(2,1)S(1)} %release_n1.1.refs_9_.refs_11_.refs_8_.refs_6_.refs_7_.refs_10_.refs_0_), channel_id=1, source_target_pairs={{0,2},{1,3},{6,4},{7,5},{10,8},{11,9},{14,12},{15,13},{12,14},{13,... | collective-permute-start | bytes 1572872 | tf_op jit(solution)/shard_map/ppermute | solution.py:533
  129.3 2.3 %opposite_1.1 = (bf16[1,128,2048]{2,1,0:T(8,128)(2,1)S(1)}, bf16[1,128,1024]{2,1,0:T(8,128)(2,1)S(1)}, bf16[1,128,1024]{2,1,0:T(8,128)(2,1)S(1)}) custom-call(bf16[128,2048]{1,0:T(8,128)(2,1)S(1)} %collective-permute-done.25.refs_0_, bf16[128,2048]{1,0:T(8,128)(2,1)S(1)} %collective-permute-done.26.refs_1_, ...), custom_call_target="tpu_custom_call" | custom-call | flops 99999997952 | bytes 1 | tf_op jit(solution)/shard_map/opposite_1/pallas_call | solution.py:31
  131.7 0.5 collective-permute-start.29
  132.2 1.0 collective-permute-done.28.refs_3_
  133.2 0.4 collective-permute-done.29.refs_4_
  133.9 5.2 %collective-permute-start.32 = (bf16[128,2048]{1,0:T(8,128)(2,1)S(1)}, bf16[128,2048]{1,0:T(8,128)(2,1)S(1)}, u32[]{:S(2)}, u32[]{:S(2)}) collective-permute-start(bf16[128,2048]{1,0:T(8,128)(2,1)S(1)} %get-tuple-element.102.refs_12_.refs_10_.refs_11_.refs_0_.refs_13_.refs_3_), channel_id=1, source_target_pairs={{2,0},{3,1},{6,4},{7,5},{4,6},{5,7},{0,2},{1,3},{8,10},{9,11},{14,... | collective-permute-start | bytes 1572872 | tf_op jit(solution)/shard_map/ppermute | solution.py:533
  139.4 1.3 collective-permute-start.33
  140.8 9.7 %collective-permute-done.24.refs_1_ = bf16[128,2048]{1,0:T(8,128)(2,1)S(1)} collective-permute-done((bf16[128,2048]{1,0:T(8,128)(2,1)S(1)}, bf16[128,2048]{1,0:T(8,128)(2,1)S(1)}, u32[]{:S(2)}, u32[]{:S(2)}) %collective-permute-start.24) | collective-permute-done | bytes 524320 | tf_op jit(solution)/shard_map/ppermute | solution.py:533
  150.6 0.7 collective-permute-start.31
  151.3 6.6 %collective-permute-start.35 = (bf16[128,2048]{1,0:T(8,128)(2,1)S(1)}, bf16[128,2048]{1,0:T(8,128)(2,1)S(1)}, u32[]{:S(2)}, u32[]{:S(2)}) collective-permute-start(bf16[128,2048]{1,0:T(8,128)(2,1)S(1)} %pick_1.1.refs_2_), channel_id=1, source_target_pairs={{0,2},{1,3},{6,4},{7,5},{8,10},{9,11},{14,12},{15,13},{16,18},{17,... | collective-permute-start | bytes 1572872 | tf_op jit(solution)/shard_map/ppermute | solution.py:533
  157.9 0.7 collective-permute-start.36
  158.6 4.1 %collective-permute-done.32.refs_1_.refs_15_.refs_5_ = bf16[128,2048]{1,0:T(8,128)(2,1)S(1)} collective-permute-done((bf16[128,2048]{1,0:T(8,128)(2,1)S(1)}, bf16[128,2048]{1,0:T(8,128)(2,1)S(1)}, u32[]{:S(2)}, u32[]{:S(2)}) %collective-permute-start.32) | collective-permute-done | bytes 524320 | tf_op jit(solution)/shard_map/ppermute | solution.py:533
  162.8 1.3 collective-permute-start.34
  164.1 8.0 %collective-permute-done.35.refs_17_.refs_8_ = bf16[128,2048]{1,0:T(8,128)(2,1)S(1)} collective-permute-done((bf16[128,2048]{1,0:T(8,128)(2,1)S(1)}, bf16[128,2048]{1,0:T(8,128)(2,1)S(1)}, u32[]{:S(2)}, u32[]{:S(2)}) %collective-permute-start.35) | collective-permute-done | bytes 524320 | tf_op jit(solution)/shard_map/ppermute | solution.py:533
  172.1 1.1 last_0.1.refs_10_
  173.2 5.9 %collective-permute-done.34.refs_7_ = bf16[128,2048]{1,0:T(8,128)(2,1)S(1)} collective-permute-done((bf16[128,2048]{1,0:T(8,128)(2,1)S(1)}, bf16[128,2048]{1,0:T(8,128)(2,1)S(1)}, u32[]{:S(2)}, u32[]{:S(2)}) %collective-permute-start.34) | collective-permute-done | bytes 524320 | tf_op jit(solution)/shard_map/ppermute | solution.py:533
  179.1 1.1 last_1.1
  (54 shorter events, 2.7 us)
Async XLA Ops:
  4.0 18.6 %collective-permute-start = (bf16[144,2048]{1,0:T(8,128)(2,1)S(1)}, bf16[144,2048]{1,0:T(8,128)(2,1)S(1)}, u32[]{:S(2)}, u32[]{:S(2)}) collective-permute-start(bf16[144,2048]{1,0:T(8,128)(2,1)S(1)} %get-tuple-element.54.refs_7_.refs_8_.refs_0_), channel_id=1, source_target_pairs={{0,8},{16,24},{1,9},{17,25},{2,10},{18,26},{3,11},{19,27},{4,12},{... | collective-permute-start | bytes 1769480 | tf_op jit(solution)/shard_map/ppermute | solution.py:513
  12.8 21.2 %collective-permute-start.3 = (bf16[144,2048]{1,0:T(8,128)(2,1)S(1)}, bf16[144,2048]{1,0:T(8,128)(2,1)S(1)}, u32[]{:S(2)}, u32[]{:S(2)}) collective-permute-start(bf16[144,2048]{1,0:T(8,128)(2,1)S(1)} %get-tuple-element.59.refs_9_.refs_4_.refs_12_.refs_0_), channel_id=1, source_target_pairs={{0,8},{16,24},{1,9},{17,25},{2,10},{18,26},{3,11},{19,27},{4,12},{... | collective-permute-start | bytes 1769480 | tf_op jit(solution)/shard_map/ppermute | solution.py:515
  22.7 11.3 %collective-permute-start.1 = (bf16[144,2048]{1,0:T(8,128)(2,1)S(1)}, bf16[144,2048]{1,0:T(8,128)(2,1)S(1)}, u32[]{:S(2)}, u32[]{:S(2)}) collective-permute-start(bf16[144,2048]{1,0:T(8,128)(2,1)S(1)} %join_0.1.refs_8_), channel_id=1, source_target_pairs={{8,16},{9,17},{10,18},{11,19},{12,20},{13,21},{14,22},{15,23}} | collective-permute-start | bytes 1769480 | tf_op jit(solution)/shard_map/ppermute | solution.py:518
  23.4 10.6 %collective-permute-start.2 = (bf16[144,2048]{1,0:T(8,128)(2,1)S(1)}, bf16[144,2048]{1,0:T(8,128)(2,1)S(1)}, u32[]{:S(2)}, u32[]{:S(2)}) collective-permute-start(bf16[144,2048]{1,0:T(8,128)(2,1)S(1)} %join_0.1.refs_8_), channel_id=1, source_target_pairs={{8,24},{9,25},{10,26},{11,27},{12,28},{13,29},{14,30},{15,31}} | collective-permute-start | bytes 1769480 | tf_op jit(solution)/shard_map/ppermute | solution.py:518
  34.2 7.4 %copy-start = (bf16[2,256,128]{2,1,0:T(8,128)(2,1)S(1)}, bf16[2,256,128]{2,1,0:T(8,128)(2,1)}, u32[]{:S(2)}) copy-start(bf16[2,256,128]{2,1,0:T(8,128)(2,1)} %refs_3_.7) | copy-start | bytes 393220
  34.2 7.4 %copy-start.3 = (f32[2,2048]{1,0:T(2,128)S(1)}, f32[2,2048]{1,0:T(2,128)}, u32[]{:S(2)}) copy-start(f32[2,2048]{1,0:T(2,128)} %refs_7_.7) | copy-start | bytes 49156
  34.2 7.3 %collective-permute-start.4 = (bf16[144,2048]{1,0:T(8,128)(2,1)S(1)}, bf16[144,2048]{1,0:T(8,128)(2,1)S(1)}, u32[]{:S(2)}, u32[]{:S(2)}) collective-permute-start(bf16[144,2048]{1,0:T(8,128)(2,1)S(1)} %join_1.1.refs_1_), channel_id=1, source_target_pairs={{8,16},{9,17},{10,18},{11,19},{12,20},{13,21},{14,22},{15,23}} | collective-permute-start | bytes 1769480 | tf_op jit(solution)/shard_map/ppermute | solution.py:521
  35.1 6.5 %collective-permute-start.5 = (bf16[144,2048]{1,0:T(8,128)(2,1)S(1)}, bf16[144,2048]{1,0:T(8,128)(2,1)S(1)}, u32[]{:S(2)}, u32[]{:S(2)}) collective-permute-start(bf16[144,2048]{1,0:T(8,128)(2,1)S(1)} %join_1.1.refs_1_), channel_id=1, source_target_pairs={{8,24},{9,25},{10,26},{11,27},{12,28},{13,29},{14,30},{15,31}} | collective-permute-start | bytes 1769480 | tf_op jit(solution)/shard_map/ppermute | solution.py:521
  42.7 37.6 %collective-permute-start.8 = (bf16[256,2048]{1,0:T(8,128)(2,1)S(1)}, bf16[256,2048]{1,0:T(8,128)(2,1)S(1)}, u32[]{:S(2)}, u32[]{:S(2)}) collective-permute-start(bf16[256,2048]{1,0:T(8,128)(2,1)S(1)} %get-tuple-element.68.refs_9_.refs_3_.refs_0_), channel_id=1, source_target_pairs={{0,8},{8,0},{16,24},{24,16},{1,9},{9,1},{17,25},{25,17},{2,10},{10... | collective-permute-start | bytes 3145736 | tf_op jit(solution)/shard_map/ppermute | solution.py:505
  56.3 26.6 %collective-permute-start.9 = (bf16[256,2048]{1,0:T(8,128)(2,1)S(1)}, bf16[256,2048]{1,0:T(8,128)(2,1)S(1)}, u32[]{:S(2)}, u32[]{:S(2)}) collective-permute-start(bf16[256,2048]{1,0:T(8,128)(2,1)S(1)} %get-tuple-element.68.refs_9_.refs_3_.refs_0_), channel_id=1, source_target_pairs={{0,16},{8,24},{16,0},{24,8},{1,17},{9,25},{17,1},{25,9},{2,18},{10... | collective-permute-start | bytes 3145736 | tf_op jit(solution)/shard_map/ppermute | solution.py:505
  59.9 38.9 %collective-permute-start.6 = (bf16[256,2048]{1,0:T(8,128)(2,1)S(1)}, bf16[256,2048]{1,0:T(8,128)(2,1)S(1)}, u32[]{:S(2)}, u32[]{:S(2)}) collective-permute-start(bf16[256,2048]{1,0:T(8,128)(2,1)S(1)} %get-tuple-element.70.refs_4_.refs_2_.refs_3_.refs_0_), channel_id=1, source_target_pairs={{0,8},{8,0},{16,24},{24,16},{1,9},{9,1},{17,25},{25,17},{2,10},{10... | collective-permute-start | bytes 3145736 | tf_op jit(solution)/shard_map/ppermute | solution.py:505
  60.6 42.0 %collective-permute-start.7 = (bf16[256,2048]{1,0:T(8,128)(2,1)S(1)}, bf16[256,2048]{1,0:T(8,128)(2,1)S(1)}, u32[]{:S(2)}, u32[]{:S(2)}) collective-permute-start(bf16[256,2048]{1,0:T(8,128)(2,1)S(1)} %get-tuple-element.70.refs_4_.refs_2_.refs_3_.refs_0_), channel_id=1, source_target_pairs={{0,16},{8,24},{16,0},{24,8},{1,17},{9,25},{17,1},{25,9},{2,18},{10... | collective-permute-start | bytes 3145736 | tf_op jit(solution)/shard_map/ppermute | solution.py:505
  60.6 2.6 %collective-permute-start.10 = (f32[8,256]{1,0:T(8,128)S(1)}, f32[8,256]{1,0:T(8,128)S(1)}, u32[]{:S(2)}, u32[]{:S(2)}) collective-permute-start(f32[8,256]{1,0:T(8,128)S(1)} %sums_0.1.refs_3_.refs_0_), channel_id=1, source_target_pairs={{0,1},{1,0},{2,3},{3,2},{4,5},{5,4},{6,7},{7,6},{8,9},{9,8},{10,11... | collective-permute-start | bytes 24584 | tf_op jit(solution)/shard_map/ppermute | solution.py:537
  63.2 4.2 %collective-permute-start.11 = (f32[8,256]{1,0:T(8,128)S(1)}, f32[8,256]{1,0:T(8,128)S(1)}, u32[]{:S(2)}, u32[]{:S(2)}) collective-permute-start(f32[8,256]{1,0:T(8,128)S(1)} %sums_1.1.refs_2_.refs_0_), channel_id=1, source_target_pairs={{0,2},{1,3},{2,0},{3,1},{4,6},{5,7},{6,4},{7,5},{8,10},{9,11},{10,... | collective-permute-start | bytes 24584 | tf_op jit(solution)/shard_map/ppermute | solution.py:537
  67.4 4.6 %collective-permute-start.12 = (f32[8,256]{1,0:T(8,128)S(1)}, f32[8,256]{1,0:T(8,128)S(1)}, u32[]{:S(2)}, u32[]{:S(2)}) collective-permute-start(f32[8,256]{1,0:T(8,128)S(1)} %sums_2.1.refs_0_), channel_id=1, source_target_pairs={{0,4},{1,5},{2,6},{3,7},{4,0},{5,1},{6,2},{7,3},{8,12},{9,13},{10,... | collective-permute-start | bytes 24584 | tf_op jit(solution)/shard_map/ppermute | solution.py:537
  72.1 16.2 %collective-permute-start.15 = (bf16[1,128,2048]{2,1,0:T(8,128)(2,1)S(1)}, bf16[1,128,2048]{2,1,0:T(8,128)(2,1)S(1)}, u32[]{:S(2)}, u32[]{:S(2)}) collective-permute-start(bf16[1,128,2048]{2,1,0:T(8,128)(2,1)S(1)} %get-tuple-element.73.refs_5_.refs_4_.refs_2_), channel_id=1, source_target_pairs={{0,1},{1,0},{2,3},{3,2},{4,5},{5,4},{6,7},{7,6},{8,9},{9,8},{10,11... | collective-permute-start | bytes 1572872 | tf_op jit(solution)/shard_map/ppermute | solution.py:504
  72.1 15.7 %copy-start.1 = (f32[8,256]{1,0:T(8,128)}, f32[8,256]{1,0:T(8,128)S(1)}, u32[]{:S(2)}) copy-start(f32[8,256]{1,0:T(8,128)S(1)} %sums_4.1.refs_3_.refs_2_) | copy-start | bytes 24580
  87.7 2.0 %collective-permute-start.13 = (bf16[1,128,2048]{2,1,0:T(8,128)(2,1)S(1)}, bf16[1,128,2048]{2,1,0:T(8,128)(2,1)S(1)}, u32[]{:S(2)}, u32[]{:S(2)}) collective-permute-start(bf16[1,128,2048]{2,1,0:T(8,128)(2,1)S(1)} %get-tuple-element.77), channel_id=1, source_target_pairs={{0,1},{1,0},{2,3},{3,2},{4,5},{5,4},{6,7},{7,6},{8,9},{9,8},{10,11... | collective-permute-start | bytes 1572872 | tf_op jit(solution)/shard_map/ppermute | solution.py:504
  87.8 2.6 %collective-permute-start.14 = (bf16[1,128,2048]{2,1,0:T(8,128)(2,1)S(1)}, bf16[1,128,2048]{2,1,0:T(8,128)(2,1)S(1)}, u32[]{:S(2)}, u32[]{:S(2)}) collective-permute-start(bf16[1,128,2048]{2,1,0:T(8,128)(2,1)S(1)} %get-tuple-element.78), channel_id=1, source_target_pairs={{0,1},{1,0},{2,3},{3,2},{4,5},{5,4},{6,7},{7,6},{8,9},{9,8},{10,11... | collective-permute-start | bytes 1572872 | tf_op jit(solution)/shard_map/ppermute | solution.py:504
  88.3 25.2 %collective-permute-start.18 = (bf16[1,128,2048]{2,1,0:T(8,128)(2,1)S(1)}, bf16[1,128,2048]{2,1,0:T(8,128)(2,1)S(1)}, u32[]{:S(2)}, u32[]{:S(2)}) collective-permute-start(bf16[1,128,2048]{2,1,0:T(8,128)(2,1)S(1)} %get-tuple-element.75.refs_6_.refs_8_.refs_10_.refs_9_), channel_id=1, source_target_pairs={{0,1},{1,0},{2,3},{3,2},{4,5},{5,4},{6,7},{7,6},{8,9},{9,8},{10,11... | collective-permute-start | bytes 1572872 | tf_op jit(solution)/shard_map/ppermute | solution.py:504
  90.8 22.8 %collective-permute-start.19 = (bf16[128,2048]{1,0:T(8,128)(2,1)S(1)}, bf16[128,2048]{1,0:T(8,128)(2,1)S(1)}, u32[]{:S(2)}, u32[]{:S(2)}) collective-permute-start(bf16[128,2048]{1,0:T(8,128)(2,1)S(1)} %get-tuple-element.82.refs_3_.refs_7_.refs_6_.refs_9_.refs_8_.refs_5_.refs_4_.refs_2_.refs_0_), channel_id=1, source_target_pairs={{0,2},{1,3},{6,4},{7,5},{10,8},{11,9},{14,12},{15,13},{12,14},{13,... | collective-permute-start | bytes 1572872 | tf_op jit(solution)/shard_map/ppermute | solution.py:533
  102.5 11.9 %collective-permute-start.16 = (bf16[128,2048]{1,0:T(8,128)(2,1)S(1)}, bf16[128,2048]{1,0:T(8,128)(2,1)S(1)}, u32[]{:S(2)}, u32[]{:S(2)}) collective-permute-start(bf16[128,2048]{1,0:T(8,128)(2,1)S(1)} %get-tuple-element.83.refs_3_), channel_id=1, source_target_pairs={{0,16},{8,24},{16,0},{24,8},{1,17},{9,25},{17,1},{25,9},{2,18},{10... | collective-permute-start | bytes 1572872 | tf_op jit(solution)/shard_map/ppermute | solution.py:505
  104.3 10.1 %collective-permute-start.17 = (bf16[128,2048]{1,0:T(8,128)(2,1)S(1)}, bf16[128,2048]{1,0:T(8,128)(2,1)S(1)}, u32[]{:S(2)}, u32[]{:S(2)}) collective-permute-start(bf16[128,2048]{1,0:T(8,128)(2,1)S(1)} %get-tuple-element.84), channel_id=1, source_target_pairs={{0,8},{8,0},{16,24},{24,16},{1,9},{9,1},{17,25},{25,17},{2,10},{10... | collective-permute-start | bytes 1572872 | tf_op jit(solution)/shard_map/ppermute | solution.py:505
  104.7 12.3 %collective-permute-start.20 = (bf16[128,2048]{1,0:T(8,128)(2,1)S(1)}, bf16[128,2048]{1,0:T(8,128)(2,1)S(1)}, u32[]{:S(2)}, u32[]{:S(2)}) collective-permute-start(bf16[128,2048]{1,0:T(8,128)(2,1)S(1)} %pick_0.1.refs_3_), channel_id=1, source_target_pairs={{0,2},{1,3},{6,4},{7,5},{8,10},{9,11},{14,12},{15,13},{16,18},{17,... | collective-permute-start | bytes 1572872 | tf_op jit(solution)/shard_map/ppermute | solution.py:533
  113.5 3.5 %collective-permute-start.21 = (bf16[2,128,2048]{2,1,0:T(8,128)(2,1)S(1)}, bf16[2,128,2048]{2,1,0:T(8,128)(2,1)S(1)}, u32[]{:S(2)}, u32[]{:S(2)}) collective-permute-start(bf16[2,128,2048]{2,1,0:T(8,128)(2,1)S(1)} %get-tuple-element.89), channel_id=1, source_target_pairs={{0,1},{1,0},{2,3},{3,2},{4,5},{5,4},{6,7},{7,6},{8,9},{9,8},{10,11... | collective-permute-start | bytes 3145736 | tf_op jit(solution)/shard_map/ppermute | solution.py:504
  113.7 15.6 %collective-permute-start.27 = (bf16[128,2048]{1,0:T(8,128)(2,1)S(1)}, bf16[128,2048]{1,0:T(8,128)(2,1)S(1)}, u32[]{:S(2)}, u32[]{:S(2)}) collective-permute-start(bf16[128,2048]{1,0:T(8,128)(2,1)S(1)} %add_next_0.1.refs_9_.refs_10_.refs_12_.refs_11_.refs_8_.refs_6_.refs_5_.refs_3_.refs_4_.refs_1_), channel_id=1, source_target_pairs={{2,4},{3,5},{4,2},{5,3},{12,8},{13,9},{10,14},{11,15},{20,16},{21,... | collective-permute-start | bytes 1572872 | tf_op jit(solution)/shard_map/ppermute | solution.py:533
  114.4 14.5 %collective-permute-start.25 = (bf16[128,2048]{1,0:T(8,128)(2,1)S(1)}, bf16[128,2048]{1,0:T(8,128)(2,1)S(1)}, u32[]{:S(2)}, u32[]{:S(2)}) collective-permute-start(bf16[128,2048]{1,0:T(8,128)(2,1)S(1)} %get-tuple-element.88.refs_0_), channel_id=1, source_target_pairs={{0,16},{8,24},{16,0},{24,8},{1,17},{9,25},{17,1},{25,9},{2,18},{10... | collective-permute-start | bytes 1572872 | tf_op jit(solution)/shard_map/ppermute | solution.py:505
  115.1 14.2 %collective-permute-start.26 = (bf16[128,2048]{1,0:T(8,128)(2,1)S(1)}, bf16[128,2048]{1,0:T(8,128)(2,1)S(1)}, u32[]{:S(2)}, u32[]{:S(2)}) collective-permute-start(bf16[128,2048]{1,0:T(8,128)(2,1)S(1)} %get-tuple-element.97), channel_id=1, source_target_pairs={{0,8},{8,0},{16,24},{24,16},{1,9},{9,1},{17,25},{25,17},{2,10},{10... | collective-permute-start | bytes 1572872 | tf_op jit(solution)/shard_map/ppermute | solution.py:505
  119.7 1.6 collective-permute-start.22
  119.8 1.9 %collective-permute-start.23 = (bf16[1,128,1024]{2,1,0:T(8,128)(2,1)S(1)}, bf16[1,128,1024]{2,1,0:T(8,128)(2,1)S(1)}, u32[]{:S(2)}, u32[]{:S(2)}) collective-permute-start(bf16[1,128,1024]{2,1,0:T(8,128)(2,1)S(1)} %get-tuple-element.94), channel_id=1, source_target_pairs={{0,1},{1,0},{2,3},{3,2},{4,5},{5,4},{6,7},{7,6},{8,9},{9,8},{10,11... | collective-permute-start | bytes 786440 | tf_op jit(solution)/shard_map/ppermute | solution.py:504
  122.0 17.2 %collective-permute-start.30 = (bf16[128,2048]{1,0:T(8,128)(2,1)S(1)}, bf16[128,2048]{1,0:T(8,128)(2,1)S(1)}, u32[]{:S(2)}, u32[]{:S(2)}) collective-permute-start(bf16[128,2048]{1,0:T(8,128)(2,1)S(1)} %get-tuple-element.95.refs_0_.refs_11_.refs_13_.refs_10_.refs_8_.refs_9_.refs_3_), channel_id=1, source_target_pairs={{2,0},{3,1},{6,4},{7,5},{4,6},{5,7},{0,2},{1,3},{8,10},{9,11},{14,... | collective-permute-start | bytes 1572872 | tf_op jit(solution)/shard_map/ppermute | solution.py:533
  127.0 23.5 %collective-permute-start.24 = (bf16[128,2048]{1,0:T(8,128)(2,1)S(1)}, bf16[128,2048]{1,0:T(8,128)(2,1)S(1)}, u32[]{:S(2)}, u32[]{:S(2)}) collective-permute-start(bf16[128,2048]{1,0:T(8,128)(2,1)S(1)} %release_n1.1.refs_9_.refs_11_.refs_8_.refs_6_.refs_7_.refs_10_.refs_0_), channel_id=1, source_target_pairs={{0,2},{1,3},{6,4},{7,5},{10,8},{11,9},{14,12},{15,13},{12,14},{13,... | collective-permute-start | bytes 1572872 | tf_op jit(solution)/shard_map/ppermute | solution.py:533
  131.6 26.3 %copy-start.2 = (f32[8,256]{1,0:T(8,128)S(1)}, f32[8,256]{1,0:T(8,128)}, u32[]{:S(2)}) copy-start(f32[8,256]{1,0:T(8,128)} %copy-done.1) | copy-start | bytes 24580
  131.6 1.6 collective-permute-start.28
  131.7 1.9 %collective-permute-start.29 = (bf16[1,128,1024]{2,1,0:T(8,128)(2,1)S(1)}, bf16[1,128,1024]{2,1,0:T(8,128)(2,1)S(1)}, u32[]{:S(2)}, u32[]{:S(2)}) collective-permute-start(bf16[1,128,1024]{2,1,0:T(8,128)(2,1)S(1)} %get-tuple-element.100), channel_id=1, source_target_pairs={{0,1},{1,0},{2,3},{3,2},{4,5},{5,4},{6,7},{7,6},{8,9},{9,8},{10,11... | collective-permute-start | bytes 786440 | tf_op jit(solution)/shard_map/ppermute | solution.py:504
  133.9 28.7 %collective-permute-start.32 = (bf16[128,2048]{1,0:T(8,128)(2,1)S(1)}, bf16[128,2048]{1,0:T(8,128)(2,1)S(1)}, u32[]{:S(2)}, u32[]{:S(2)}) collective-permute-start(bf16[128,2048]{1,0:T(8,128)(2,1)S(1)} %get-tuple-element.102.refs_12_.refs_10_.refs_11_.refs_0_.refs_13_.refs_3_), channel_id=1, source_target_pairs={{2,0},{3,1},{6,4},{7,5},{4,6},{5,7},{0,2},{1,3},{8,10},{9,11},{14,... | collective-permute-start | bytes 1572872 | tf_op jit(solution)/shard_map/ppermute | solution.py:533
  139.4 23.3 %collective-permute-start.33 = (bf16[128,2048]{1,0:T(8,128)(2,1)S(1)}, bf16[128,2048]{1,0:T(8,128)(2,1)S(1)}, u32[]{:S(2)}, u32[]{:S(2)}) collective-permute-start(bf16[128,2048]{1,0:T(8,128)(2,1)S(1)} %add_opposite_0.1.refs_13_.refs_14_.refs_6_), channel_id=1, source_target_pairs={{4,0},{5,1},{2,6},{3,7},{10,12},{11,13},{12,10},{13,11},{18,20},{1... | collective-permute-start | bytes 1572872 | tf_op jit(solution)/shard_map/ppermute | solution.py:533
  150.6 13.5 %collective-permute-start.31 = (bf16[128,2048]{1,0:T(8,128)(2,1)S(1)}, bf16[128,2048]{1,0:T(8,128)(2,1)S(1)}, u32[]{:S(2)}, u32[]{:S(2)}) collective-permute-start(bf16[128,2048]{1,0:T(8,128)(2,1)S(1)} %add_next_1.1.refs_15_.refs_11_.refs_1_), channel_id=1, source_target_pairs={{2,4},{3,5},{4,2},{5,3},{12,8},{13,9},{10,14},{11,15},{20,16},{21,... | collective-permute-start | bytes 1572872 | tf_op jit(solution)/shard_map/ppermute | solution.py:533
  151.3 20.8 %collective-permute-start.35 = (bf16[128,2048]{1,0:T(8,128)(2,1)S(1)}, bf16[128,2048]{1,0:T(8,128)(2,1)S(1)}, u32[]{:S(2)}, u32[]{:S(2)}) collective-permute-start(bf16[128,2048]{1,0:T(8,128)(2,1)S(1)} %pick_1.1.refs_2_), channel_id=1, source_target_pairs={{0,2},{1,3},{6,4},{7,5},{8,10},{9,11},{14,12},{15,13},{16,18},{17,... | collective-permute-start | bytes 1572872 | tf_op jit(solution)/shard_map/ppermute | solution.py:533
  157.9 6.2 %collective-permute-start.36 = (f32[8,256]{1,0:T(8,128)S(1)}, f32[8,256]{1,0:T(8,128)S(1)}, u32[]{:S(2)}, u32[]{:S(2)}) collective-permute-start(f32[8,256]{1,0:T(8,128)S(1)} %release_sums.1), channel_id=1, source_target_pairs={{0,0},{1,1},{8,2},{9,3},{16,4},{17,5},{24,6},{25,7},{2,8},{3,9},{1... | collective-permute-start | bytes 24584 | tf_op jit(solution)/shard_map/ppermute | solution.py:600
  162.8 16.3 %collective-permute-start.34 = (bf16[128,2048]{1,0:T(8,128)(2,1)S(1)}, bf16[128,2048]{1,0:T(8,128)(2,1)S(1)}, u32[]{:S(2)}, u32[]{:S(2)}) collective-permute-start(bf16[128,2048]{1,0:T(8,128)(2,1)S(1)} %add_opposite_1.1.refs_16_.refs_6_), channel_id=1, source_target_pairs={{4,0},{5,1},{2,6},{3,7},{10,12},{11,13},{12,10},{13,11},{18,20},{1... | collective-permute-start | bytes 1572872 | tf_op jit(solution)/shard_map/ppermute | solution.py:533

commit v4 on v3

--- a/solution.py
+++ b/solution.py
@@ -125,6 +125,7 @@
     b_t = b_ref[0].astype(F32).T.astype(BF16)
     lane_head = lane_heads(head_size)
     row_id = lax.broadcasted_iota(jnp.int32, (EXTRA, LANES), 0)
+    wide = []
     for p in range(channels // LANES):
         cols = slice(p * LANES, (p + 1) * LANES)
         first = p * lane_head[1]
@@ -132,7 +133,11 @@
             if cut.start == cols.start:
                 fetch.wait()
         xw = (x_ref[0, :, cols].astype(F32) * spread(tail, lane_head, first)).astype(BF16)
-        msg_ref[:state, cols] = dot(b_t, xw).astype(BF16)
+        wide.append(xw)
+        for cut in cuts:
+            if cut.stop == cols.stop:
+                msg_ref[:state, cut] = dot(b_t, jnp.concatenate(wide, axis=1)).astype(BF16)
+                wide = []
         decay = spread(etot, lane_head, first)
         high = decay.astype(BF16).astype(F32)
         extra = jnp.where(row_id == 0, high, jnp.where(row_id == 1, decay - high, jnp.where(row_id == 2, last, 0.0)))

time: 181 us -> 181 us (level)
  no operation moved by 1% of the time
where the time goes in v4:
time: 181 us; the launch traced here: 180 us
  starting transfers between devices  67.6 us (37%)
  waiting for transfers between devices  61.1 us (34%)
  Pallas kernels  50.9 us (28%)
    pallas_call x34, Pallas kernels, call(): pl.pallas_call(body, name=name, in_specs=[IN_VMEM] * len(operands) + [ANY...  48.8 us
    ppermute x10, starting transfers between devices, turn(): return lax.ppermute(value, ('seq', 'head'), sends(kinds, i))  30.3 us
    ppermute x10, waiting for transfers between devices, turn(): return lax.ppermute(value, ('seq', 'head'), sends(kinds, i))  28.1 us
    ppermute x8, starting transfers between devices, fast(): beside = lambda a, k: lax.ppermute(a, 'seq', xor_pairs(n_seq, k))  21.1 us
    ppermute x8, waiting for transfers between devices, fast(): beside = lambda a, k: lax.ppermute(a, 'seq', xor_pairs(n_seq, k))  18.8 us
    ppermute x1, starting transfers between devices, fast(): near0 = lax.ppermute(msg0, 'seq', ring)  4.88 us
    ppermute x9, waiting for transfers between devices, fast(): across = lambda a: lax.ppermute(a, 'head', xor_pairs(n_head, 1))  4.87 us
    ppermute x1, waiting for transfers between devices, fast(): near1 = lax.ppermute(msg1, 'seq', ring)  4.36 us
  transfers between devices with their start and end apart: 37, of which 20 were waited for; matrix products, arithmetic and copies ran while one was open for 0% of the time, Pallas kernels for 25%

profile of v4, /device:TPU:0, one launch (start us, length us, event | category | flops | bytes accessed | tf_op | source)
XLA Modules:
  0.0 180.2 jit_solution(17618384272215178983)
XLA Ops:
  0.0 3.9 %prep_0.1 = (bf16[144,2048]{1,0:T(8,128)(2,1)S(1)}, f32[32,384]{1,0:T(8,128)S(1)}, f32[32,256]{1,0:T(8,128)S(1)}, f32[32,256]{1,0:T(8,128)S(1)}, f32[1,256]{1,0:T(1,128)S(1)}) custom-call(bf16[2,256,2048]{2,1,0:T(8,128)(2,1)} %refs_4_.7, bf16[2,256,128]{2,1,0:T(8,128)(2,1)} %refs_6_.3, f32[2,32,256]{2,1,0:T(8,128)} %bitcast.2, f32[2,32]{1,0:T(2,128)} %refs_3_.5, ...), custom_call_target="tpu_custom_call" | custom-call | flops 1 | bytes 1 | tf_op jit(solution)/shard_map/prep_0/pallas_call | solution.py:31
  3.9 4.9 %collective-permute-start = (bf16[144,2048]{1,0:T(8,128)(2,1)S(1)}, bf16[144,2048]{1,0:T(8,128)(2,1)S(1)}, u32[]{:S(2)}, u32[]{:S(2)}) collective-permute-start(bf16[144,2048]{1,0:T(8,128)(2,1)S(1)} %get-tuple-element.54.refs_7_.refs_8_.refs_0_), channel_id=1, source_target_pairs={{0,8},{16,24},{1,9},{17,25},{2,10},{18,26},{3,11},{19,27},{4,12},{... | collective-permute-start | bytes 1769480 | tf_op jit(solution)/shard_map/ppermute | solution.py:518
  8.8 3.9 %prep_1.1 = (bf16[144,2048]{1,0:T(8,128)(2,1)S(1)}, f32[32,384]{1,0:T(8,128)S(1)}, f32[32,256]{1,0:T(8,128)S(1)}, f32[32,256]{1,0:T(8,128)S(1)}, f32[1,256]{1,0:T(1,128)S(1)}) custom-call(bf16[2,256,2048]{2,1,0:T(8,128)(2,1)} %refs_4_.7, bf16[2,256,128]{2,1,0:T(8,128)(2,1)} %refs_6_.3, f32[2,32,256]{2,1,0:T(8,128)} %bitcast.3, f32[2,32]{1,0:T(2,128)} %refs_3_.5, ...), custom_call_target="tpu_custom_call" | custom-call | flops 1 | bytes 1 | tf_op jit(solution)/shard_map/prep_1/pallas_call | solution.py:31
  12.8 1.3 collective-permute-start.3
  14.1 5.4 %inside_0.1 = (bf16[256,2048]{1,0:T(8,128)(2,1)S(1)}, bf16[256,2048]{1,0:T(8,128)(2,1)S(1)}) custom-call(f32[32,384]{1,0:T(8,128)S(1)} %get-tuple-element.55.refs_8_.refs_0_, f32[32,256]{1,0:T(8,128)S(1)} %get-tuple-element.56.refs_9_.refs_1_, f32[32,256]{1,0:T(8,128)S(1)} %get-tuple-element.57.refs_10_.refs_2_, ...), custom_call_target="tpu_custom_call" | custom-call | flops 1 | bytes 1 | tf_op jit(solution)/shard_map/inside_0/pallas_call | solution.py:31
  19.5 3.0 %collective-permute-done.refs_1_.refs_11_.refs_4_.refs_2_.refs_0_ = bf16[144,2048]{1,0:T(8,128)(2,1)S(1)} collective-permute-done((bf16[144,2048]{1,0:T(8,128)(2,1)S(1)}, bf16[144,2048]{1,0:T(8,128)(2,1)S(1)}, u32[]{:S(2)}, u32[]{:S(2)}) %collective-permute-start) | collective-permute-done | bytes 589856 | tf_op jit(solution)/shard_map/ppermute | solution.py:518
  22.7 0.7 collective-permute-start.1
  23.4 0.9 collective-permute-start.2
  24.3 5.4 %inside_1.1 = (bf16[256,2048]{1,0:T(8,128)(2,1)S(1)}, bf16[256,2048]{1,0:T(8,128)(2,1)S(1)}) custom-call(f32[32,384]{1,0:T(8,128)S(1)} %get-tuple-element.60.refs_10_.refs_6_.refs_0_, f32[32,256]{1,0:T(8,128)S(1)} %get-tuple-element.61.refs_11_.refs_7_.refs_1_, f32[32,256]{1,0:T(8,128)S(1)} %get-tuple-element.62.refs_12_.refs_8_.refs_2_, ...), custom_call_target="tpu_custom_call" | custom-call | flops 1 | bytes 1 | tf_op jit(solution)/shard_map/inside_1/pallas_call | solution.py:31
  29.6 4.4 %collective-permute-done.3.refs_1_.refs_8_.refs_11_.refs_0_ = bf16[144,2048]{1,0:T(8,128)(2,1)S(1)} collective-permute-done((bf16[144,2048]{1,0:T(8,128)(2,1)S(1)}, bf16[144,2048]{1,0:T(8,128)(2,1)S(1)}, u32[]{:S(2)}, u32[]{:S(2)}) %collective-permute-start.3) | collective-permute-done | bytes 589856 | tf_op jit(solution)/shard_map/ppermute | solution.py:520
  34.2 0.8 collective-permute-start.4
  35.0 0.7 collective-permute-start.5
  35.7 5.8 %load.1.refs_8_.refs_2_.refs_1_.refs_3_.refs_5_.refs_7_.refs_6_.refs_4_ = bf16[2,2048,2048]{2,1,0:T(8,128)(2,1)S(1)} custom-call(bf16[2,2048,2048]{2,1,0:T(8,128)(2,1)} %refs_0_.5, bf16[144,2048]{1,0:T(8,128)(2,1)S(1)} %join_1.1.refs_1_, bf16[144,2048]{1,0:T(8,128)(2,1)S(1)} %collective-permute-done.refs_1_.refs_11_.refs_4_.refs_2_.refs_0_, ...), custom_call_target="tpu_custom_call" | custom-call | flops 1 | bytes 1 | tf_op jit(solution)/shard_map/load/pallas_call | solution.py:31
  41.6 1.1 gated_0.1
  42.7 13.5 %collective-permute-start.8 = (bf16[256,2048]{1,0:T(8,128)(2,1)S(1)}, bf16[256,2048]{1,0:T(8,128)(2,1)S(1)}, u32[]{:S(2)}, u32[]{:S(2)}) collective-permute-start(bf16[256,2048]{1,0:T(8,128)(2,1)S(1)} %get-tuple-element.68.refs_9_.refs_3_.refs_0_), channel_id=1, source_target_pairs={{0,8},{8,0},{16,24},{24,16},{1,9},{9,1},{17,25},{25,17},{2,10},{10... | collective-permute-start | bytes 3145736 | tf_op jit(solution)/shard_map/ppermute | solution.py:510
  56.2 2.5 %collective-permute-start.9 = (bf16[256,2048]{1,0:T(8,128)(2,1)S(1)}, bf16[256,2048]{1,0:T(8,128)(2,1)S(1)}, u32[]{:S(2)}, u32[]{:S(2)}) collective-permute-start(bf16[256,2048]{1,0:T(8,128)(2,1)S(1)} %get-tuple-element.68.refs_9_.refs_3_.refs_0_), channel_id=1, source_target_pairs={{0,16},{8,24},{16,0},{24,8},{1,17},{9,25},{17,1},{25,9},{2,18},{10... | collective-permute-start | bytes 3145736 | tf_op jit(solution)/shard_map/ppermute | solution.py:510
  58.7 1.1 gated_1.1
  59.9 0.7 collective-permute-start.6
  60.5 2.6 %own_0.1 = (bf16[1,128,2048]{2,1,0:T(8,128)(2,1)S(1)}, bf16[1,128,2048]{2,1,0:T(8,128)(2,1)S(1)}) custom-call(bf16[256,2048]{1,0:T(8,128)(2,1)S(1)} %get-tuple-element.68.refs_9_.refs_3_.refs_0_, bf16[2,2048,2048]{2,1,0:T(8,128)(2,1)S(1)} %load.1.refs_8_.refs_2_.refs_1_.refs_3_.refs_5_.refs_7_.refs_6_.refs_4_, ...), custom_call_target="tpu_custom_call" | custom-call | flops 1 | bytes 1 | tf_op jit(solution)/shard_map/own_0/pallas_call | solution.py:31
  63.2 1.7 collective-permute-start.11
  64.8 2.6 %own_1.1 = (bf16[1,128,2048]{2,1,0:T(8,128)(2,1)S(1)}, bf16[1,128,2048]{2,1,0:T(8,128)(2,1)S(1)}) custom-call(bf16[256,2048]{1,0:T(8,128)(2,1)S(1)} %get-tuple-element.70.refs_4_.refs_2_.refs_3_.refs_0_, bf16[2,2048,2048]{2,1,0:T(8,128)(2,1)S(1)} %load.1.refs_8_.refs_2_.refs_1_.refs_3_.refs_5_.refs_7_.refs_6_.refs_4_, f32[8,256]{1,0:T(8,128)S(1)} %sums_1.1.refs_2_.refs_0_, ...), custom_call_target="tpu_custom_call" | custom-call | flops 1 | bytes 1 | tf_op jit(solution)/shard_map/own_1/pallas_call | solution.py:31
  67.4 2.7 %collective-permute-start.12 = (f32[8,256]{1,0:T(8,128)S(1)}, f32[8,256]{1,0:T(8,128)S(1)}, u32[]{:S(2)}, u32[]{:S(2)}) collective-permute-start(f32[8,256]{1,0:T(8,128)S(1)} %sums_2.1.refs_0_), channel_id=1, source_target_pairs={{0,4},{1,5},{2,6},{3,7},{4,0},{5,1},{6,2},{7,3},{8,12},{9,13},{10,... | collective-permute-start | bytes 24584 | tf_op jit(solution)/shard_map/ppermute | solution.py:542
  70.1 2.0 %collective-permute-done.12.refs_1_ = f32[8,256]{1,0:T(8,128)S(1)} collective-permute-done((f32[8,256]{1,0:T(8,128)S(1)}, f32[8,256]{1,0:T(8,128)S(1)}, u32[]{:S(2)}, u32[]{:S(2)}) %collective-permute-start.12) | collective-permute-done | bytes 8224 | tf_op jit(solution)/shard_map/ppermute | solution.py:542
  72.0 8.3 %collective-permute-done.8.refs_0_ = bf16[256,2048]{1,0:T(8,128)(2,1)S(1)} collective-permute-done((bf16[256,2048]{1,0:T(8,128)(2,1)S(1)}, bf16[256,2048]{1,0:T(8,128)(2,1)S(1)}, u32[]{:S(2)}, u32[]{:S(2)}) %collective-permute-start.8) | collective-permute-done | bytes 1048608 | tf_op jit(solution)/shard_map/ppermute | solution.py:510
  80.3 2.5 %collective-permute-done.9.refs_1_ = bf16[256,2048]{1,0:T(8,128)(2,1)S(1)} collective-permute-done((bf16[256,2048]{1,0:T(8,128)(2,1)S(1)}, bf16[256,2048]{1,0:T(8,128)(2,1)S(1)}, u32[]{:S(2)}, u32[]{:S(2)}) %collective-permute-start.9) | collective-permute-done | bytes 1048608 | tf_op jit(solution)/shard_map/ppermute | solution.py:510
  82.8 4.9 %next_0.1 = (bf16[2,128,2048]{2,1,0:T(8,128)(2,1)S(1)}, bf16[1,128,2048]{2,1,0:T(8,128)(2,1)S(1)}, bf16[1,128,2048]{2,1,0:T(8,128)(2,1)S(1)}, bf16[128,2048]{1,0:T(8,128)(2,1)S(1)}, bf16[128,2048]{1,0:T(8,128)(2,1)S(1)}) custom-call(bf16[256,2048]{1,0:T(8,128)(2,1)S(1)} %collective-permute-done.8.refs_0_, ...), custom_call_target="tpu_custom_call" | custom-call | flops 1 | bytes 1 | tf_op jit(solution)/shard_map/next_0/pallas_call | solution.py:31
  87.8 0.5 collective-permute-start.14
  88.4 1.3 collective-permute-done.13.refs_2_
  89.7 0.7 collective-permute-done.14.refs_3_
  90.4 0.3 sum_next_0.1
  90.8 3.7 %collective-permute-start.19 = (bf16[128,2048]{1,0:T(8,128)(2,1)S(1)}, bf16[128,2048]{1,0:T(8,128)(2,1)S(1)}, u32[]{:S(2)}, u32[]{:S(2)}) collective-permute-start(bf16[128,2048]{1,0:T(8,128)(2,1)S(1)} %get-tuple-element.82.refs_3_.refs_7_.refs_6_.refs_9_.refs_8_.refs_5_.refs_4_.refs_2_.refs_0_), channel_id=1, source_target_pairs={{0,2},{1,3},{6,4},{7,5},{10,8},{11,9},{14,12},{15,13},{12,14},{13,... | collective-permute-start | bytes 1572872 | tf_op jit(solution)/shard_map/ppermute | solution.py:538
  94.7 4.1 %collective-permute-done.6.refs_0_ = bf16[256,2048]{1,0:T(8,128)(2,1)S(1)} collective-permute-done((bf16[256,2048]{1,0:T(8,128)(2,1)S(1)}, bf16[256,2048]{1,0:T(8,128)(2,1)S(1)}, u32[]{:S(2)}, u32[]{:S(2)}) %collective-permute-start.6) | collective-permute-done | bytes 1048608 | tf_op jit(solution)/shard_map/ppermute | solution.py:510
  98.8 3.7 %collective-permute-done.7.refs_1_ = bf16[256,2048]{1,0:T(8,128)(2,1)S(1)} collective-permute-done((bf16[256,2048]{1,0:T(8,128)(2,1)S(1)}, bf16[256,2048]{1,0:T(8,128)(2,1)S(1)}, u32[]{:S(2)}, u32[]{:S(2)}) %collective-permute-start.7) | collective-permute-done | bytes 1048608 | tf_op jit(solution)/shard_map/ppermute | solution.py:510
  102.5 1.7 collective-permute-start.16
  104.2 0.4 collective-permute-start.17
  104.6 3.9 %collective-permute-start.20 = (bf16[128,2048]{1,0:T(8,128)(2,1)S(1)}, bf16[128,2048]{1,0:T(8,128)(2,1)S(1)}, u32[]{:S(2)}, u32[]{:S(2)}) collective-permute-start(bf16[128,2048]{1,0:T(8,128)(2,1)S(1)} %pick_0.1.refs_3_), channel_id=1, source_target_pairs={{0,2},{1,3},{6,4},{7,5},{8,10},{9,11},{14,12},{15,13},{16,18},{17,... | collective-permute-start | bytes 1572872 | tf_op jit(solution)/shard_map/ppermute | solution.py:538
  108.5 4.9 %next_1.1 = (bf16[2,128,2048]{2,1,0:T(8,128)(2,1)S(1)}, bf16[2,128,2048]{2,1,0:T(8,128)(2,1)S(1)}, bf16[128,2048]{1,0:T(8,128)(2,1)S(1)}, bf16[128,2048]{1,0:T(8,128)(2,1)S(1)}) custom-call(bf16[256,2048]{1,0:T(8,128)(2,1)S(1)} %collective-permute-done.6.refs_0_, bf16[256,2048]{1,0:T(8,128)(2,1)S(1)} %collective-permute-done.7.refs_1_, ...), custom_call_target="tpu_custom_call" | custom-call | flops 1 | bytes 1 | tf_op jit(solution)/shard_map/next_1/pallas_call | solution.py:31
  113.7 0.7 collective-permute-start.27
  114.4 0.7 collective-permute-start.25
  115.1 1.6 collective-permute-start.26
  117.0 0.3 sum_next_1.1
  117.3 2.3 %opposite_0.1 = (bf16[1,128,2048]{2,1,0:T(8,128)(2,1)S(1)}, bf16[1,128,1024]{2,1,0:T(8,128)(2,1)S(1)}, bf16[1,128,1024]{2,1,0:T(8,128)(2,1)S(1)}) custom-call(bf16[128,2048]{1,0:T(8,128)(2,1)S(1)} %collective-permute-done.16.refs_0_.refs_2_.refs_4_, bf16[128,2048]{1,0:T(8,128)(2,1)S(1)} %collective-permute-done.17.refs_1_.refs_3_.refs_5_, ...), custom_call_target="tpu_custom_call" | custom-call | flops 1 | bytes 1 | tf_op jit(solution)/shard_map/opposite_0/pallas_call | solution.py:31
  119.7 0.5 collective-permute-start.23
  120.2 1.0 collective-permute-done.22.refs_3_
  121.2 0.4 collective-permute-done.23.refs_4_
  121.6 0.3 sum_opposite_0.1
  122.0 5.0 %collective-permute-start.30 = (bf16[128,2048]{1,0:T(8,128)(2,1)S(1)}, bf16[128,2048]{1,0:T(8,128)(2,1)S(1)}, u32[]{:S(2)}, u32[]{:S(2)}) collective-permute-start(bf16[128,2048]{1,0:T(8,128)(2,1)S(1)} %get-tuple-element.95.refs_0_.refs_11_.refs_13_.refs_10_.refs_8_.refs_9_.refs_3_), channel_id=1, source_target_pairs={{2,0},{3,1},{6,4},{7,5},{4,6},{5,7},{0,2},{1,3},{8,10},{9,11},{14,... | collective-permute-start | bytes 1572872 | tf_op jit(solution)/shard_map/ppermute | solution.py:538
  127.0 1.9 %collective-permute-start.24 = (bf16[128,2048]{1,0:T(8,128)(2,1)S(1)}, bf16[128,2048]{1,0:T(8,128)(2,1)S(1)}, u32[]{:S(2)}, u32[]{:S(2)}) collective-permute-start(bf16[128,2048]{1,0:T(8,128)(2,1)S(1)} %release_n1.1.refs_9_.refs_11_.refs_8_.refs_6_.refs_7_.refs_10_.refs_0_), channel_id=1, source_target_pairs={{0,2},{1,3},{6,4},{7,5},{10,8},{11,9},{14,12},{15,13},{12,14},{13,... | collective-permute-start | bytes 1572872 | tf_op jit(solution)/shard_map/ppermute | solution.py:538
  129.2 2.3 %opposite_1.1 = (bf16[1,128,2048]{2,1,0:T(8,128)(2,1)S(1)}, bf16[1,128,1024]{2,1,0:T(8,128)(2,1)S(1)}, bf16[1,128,1024]{2,1,0:T(8,128)(2,1)S(1)}) custom-call(bf16[128,2048]{1,0:T(8,128)(2,1)S(1)} %collective-permute-done.25.refs_0_, bf16[128,2048]{1,0:T(8,128)(2,1)S(1)} %collective-permute-done.26.refs_1_, ...), custom_call_target="tpu_custom_call" | custom-call | flops 99999997952 | bytes 1 | tf_op jit(solution)/shard_map/opposite_1/pallas_call | solution.py:31
  131.7 0.5 collective-permute-start.29
  132.2 1.0 collective-permute-done.28.refs_3_
  133.2 0.4 collective-permute-done.29.refs_4_
  133.9 5.2 %collective-permute-start.32 = (bf16[128,2048]{1,0:T(8,128)(2,1)S(1)}, bf16[128,2048]{1,0:T(8,128)(2,1)S(1)}, u32[]{:S(2)}, u32[]{:S(2)}) collective-permute-start(bf16[128,2048]{1,0:T(8,128)(2,1)S(1)} %get-tuple-element.102.refs_12_.refs_10_.refs_11_.refs_0_.refs_13_.refs_3_), channel_id=1, source_target_pairs={{2,0},{3,1},{6,4},{7,5},{4,6},{5,7},{0,2},{1,3},{8,10},{9,11},{14,... | collective-permute-start | bytes 1572872 | tf_op jit(solution)/shard_map/ppermute | solution.py:538
  139.4 1.3 collective-permute-start.33
  140.8 9.7 %collective-permute-done.24.refs_1_ = bf16[128,2048]{1,0:T(8,128)(2,1)S(1)} collective-permute-done((bf16[128,2048]{1,0:T(8,128)(2,1)S(1)}, bf16[128,2048]{1,0:T(8,128)(2,1)S(1)}, u32[]{:S(2)}, u32[]{:S(2)}) %collective-permute-start.24) | collective-permute-done | bytes 524320 | tf_op jit(solution)/shard_map/ppermute | solution.py:538
  150.6 0.7 collective-permute-start.31
  151.3 6.6 %collective-permute-start.35 = (bf16[128,2048]{1,0:T(8,128)(2,1)S(1)}, bf16[128,2048]{1,0:T(8,128)(2,1)S(1)}, u32[]{:S(2)}, u32[]{:S(2)}) collective-permute-start(bf16[128,2048]{1,0:T(8,128)(2,1)S(1)} %pick_1.1.refs_2_), channel_id=1, source_target_pairs={{0,2},{1,3},{6,4},{7,5},{8,10},{9,11},{14,12},{15,13},{16,18},{17,... | collective-permute-start | bytes 1572872 | tf_op jit(solution)/shard_map/ppermute | solution.py:538
  157.9 0.7 collective-permute-start.36
  158.6 4.0 %collective-permute-done.32.refs_1_.refs_15_.refs_5_ = bf16[128,2048]{1,0:T(8,128)(2,1)S(1)} collective-permute-done((bf16[128,2048]{1,0:T(8,128)(2,1)S(1)}, bf16[128,2048]{1,0:T(8,128)(2,1)S(1)}, u32[]{:S(2)}, u32[]{:S(2)}) %collective-permute-start.32) | collective-permute-done | bytes 524320 | tf_op jit(solution)/shard_map/ppermute | solution.py:538
  162.8 1.3 collective-permute-start.34
  164.1 8.1 %collective-permute-done.35.refs_17_.refs_8_ = bf16[128,2048]{1,0:T(8,128)(2,1)S(1)} collective-permute-done((bf16[128,2048]{1,0:T(8,128)(2,1)S(1)}, bf16[128,2048]{1,0:T(8,128)(2,1)S(1)}, u32[]{:S(2)}, u32[]{:S(2)}) %collective-permute-start.35) | collective-permute-done | bytes 524320 | tf_op jit(solution)/shard_map/ppermute | solution.py:538
  172.2 1.1 last_0.1.refs_10_
  173.2 5.8 %collective-permute-done.34.refs_7_ = bf16[128,2048]{1,0:T(8,128)(2,1)S(1)} collective-permute-done((bf16[128,2048]{1,0:T(8,128)(2,1)S(1)}, bf16[128,2048]{1,0:T(8,128)(2,1)S(1)}, u32[]{:S(2)}, u32[]{:S(2)}) %collective-permute-start.34) | collective-permute-done | bytes 524320 | tf_op jit(solution)/shard_map/ppermute | solution.py:538
  179.1 1.1 last_1.1
  (54 shorter events, 2.7 us)
Async XLA Ops:
  3.9 18.6 %collective-permute-start = (bf16[144,2048]{1,0:T(8,128)(2,1)S(1)}, bf16[144,2048]{1,0:T(8,128)(2,1)S(1)}, u32[]{:S(2)}, u32[]{:S(2)}) collective-permute-start(bf16[144,2048]{1,0:T(8,128)(2,1)S(1)} %get-tuple-element.54.refs_7_.refs_8_.refs_0_), channel_id=1, source_target_pairs={{0,8},{16,24},{1,9},{17,25},{2,10},{18,26},{3,11},{19,27},{4,12},{... | collective-permute-start | bytes 1769480 | tf_op jit(solution)/shard_map/ppermute | solution.py:518
  12.8 21.2 %collective-permute-start.3 = (bf16[144,2048]{1,0:T(8,128)(2,1)S(1)}, bf16[144,2048]{1,0:T(8,128)(2,1)S(1)}, u32[]{:S(2)}, u32[]{:S(2)}) collective-permute-start(bf16[144,2048]{1,0:T(8,128)(2,1)S(1)} %get-tuple-element.59.refs_9_.refs_4_.refs_12_.refs_0_), channel_id=1, source_target_pairs={{0,8},{16,24},{1,9},{17,25},{2,10},{18,26},{3,11},{19,27},{4,12},{... | collective-permute-start | bytes 1769480 | tf_op jit(solution)/shard_map/ppermute | solution.py:520
  22.7 11.3 %collective-permute-start.1 = (bf16[144,2048]{1,0:T(8,128)(2,1)S(1)}, bf16[144,2048]{1,0:T(8,128)(2,1)S(1)}, u32[]{:S(2)}, u32[]{:S(2)}) collective-permute-start(bf16[144,2048]{1,0:T(8,128)(2,1)S(1)} %join_0.1.refs_8_), channel_id=1, source_target_pairs={{8,16},{9,17},{10,18},{11,19},{12,20},{13,21},{14,22},{15,23}} | collective-permute-start | bytes 1769480 | tf_op jit(solution)/shard_map/ppermute | solution.py:523
  23.4 10.6 %collective-permute-start.2 = (bf16[144,2048]{1,0:T(8,128)(2,1)S(1)}, bf16[144,2048]{1,0:T(8,128)(2,1)S(1)}, u32[]{:S(2)}, u32[]{:S(2)}) collective-permute-start(bf16[144,2048]{1,0:T(8,128)(2,1)S(1)} %join_0.1.refs_8_), channel_id=1, source_target_pairs={{8,24},{9,25},{10,26},{11,27},{12,28},{13,29},{14,30},{15,31}} | collective-permute-start | bytes 1769480 | tf_op jit(solution)/shard_map/ppermute | solution.py:523
  34.2 7.4 %copy-start = (bf16[2,256,128]{2,1,0:T(8,128)(2,1)S(1)}, bf16[2,256,128]{2,1,0:T(8,128)(2,1)}, u32[]{:S(2)}) copy-start(bf16[2,256,128]{2,1,0:T(8,128)(2,1)} %refs_3_.7) | copy-start | bytes 393220
  34.2 7.4 %copy-start.3 = (f32[2,2048]{1,0:T(2,128)S(1)}, f32[2,2048]{1,0:T(2,128)}, u32[]{:S(2)}) copy-start(f32[2,2048]{1,0:T(2,128)} %refs_7_.7) | copy-start | bytes 49156
  34.2 7.3 %collective-permute-start.4 = (bf16[144,2048]{1,0:T(8,128)(2,1)S(1)}, bf16[144,2048]{1,0:T(8,128)(2,1)S(1)}, u32[]{:S(2)}, u32[]{:S(2)}) collective-permute-start(bf16[144,2048]{1,0:T(8,128)(2,1)S(1)} %join_1.1.refs_1_), channel_id=1, source_target_pairs={{8,16},{9,17},{10,18},{11,19},{12,20},{13,21},{14,22},{15,23}} | collective-permute-start | bytes 1769480 | tf_op jit(solution)/shard_map/ppermute | solution.py:526
  35.0 6.5 %collective-permute-start.5 = (bf16[144,2048]{1,0:T(8,128)(2,1)S(1)}, bf16[144,2048]{1,0:T(8,128)(2,1)S(1)}, u32[]{:S(2)}, u32[]{:S(2)}) collective-permute-start(bf16[144,2048]{1,0:T(8,128)(2,1)S(1)} %join_1.1.refs_1_), channel_id=1, source_target_pairs={{8,24},{9,25},{10,26},{11,27},{12,28},{13,29},{14,30},{15,31}} | collective-permute-start | bytes 1769480 | tf_op jit(solution)/shard_map/ppermute | solution.py:526
  42.7 37.6 %collective-permute-start.8 = (bf16[256,2048]{1,0:T(8,128)(2,1)S(1)}, bf16[256,2048]{1,0:T(8,128)(2,1)S(1)}, u32[]{:S(2)}, u32[]{:S(2)}) collective-permute-start(bf16[256,2048]{1,0:T(8,128)(2,1)S(1)} %get-tuple-element.68.refs_9_.refs_3_.refs_0_), channel_id=1, source_target_pairs={{0,8},{8,0},{16,24},{24,16},{1,9},{9,1},{17,25},{25,17},{2,10},{10... | collective-permute-start | bytes 3145736 | tf_op jit(solution)/shard_map/ppermute | solution.py:510
  56.2 26.6 %collective-permute-start.9 = (bf16[256,2048]{1,0:T(8,128)(2,1)S(1)}, bf16[256,2048]{1,0:T(8,128)(2,1)S(1)}, u32[]{:S(2)}, u32[]{:S(2)}) collective-permute-start(bf16[256,2048]{1,0:T(8,128)(2,1)S(1)} %get-tuple-element.68.refs_9_.refs_3_.refs_0_), channel_id=1, source_target_pairs={{0,16},{8,24},{16,0},{24,8},{1,17},{9,25},{17,1},{25,9},{2,18},{10... | collective-permute-start | bytes 3145736 | tf_op jit(solution)/shard_map/ppermute | solution.py:510
  59.9 38.9 %collective-permute-start.6 = (bf16[256,2048]{1,0:T(8,128)(2,1)S(1)}, bf16[256,2048]{1,0:T(8,128)(2,1)S(1)}, u32[]{:S(2)}, u32[]{:S(2)}) collective-permute-start(bf16[256,2048]{1,0:T(8,128)(2,1)S(1)} %get-tuple-element.70.refs_4_.refs_2_.refs_3_.refs_0_), channel_id=1, source_target_pairs={{0,8},{8,0},{16,24},{24,16},{1,9},{9,1},{17,25},{25,17},{2,10},{10... | collective-permute-start | bytes 3145736 | tf_op jit(solution)/shard_map/ppermute | solution.py:510
  60.5 41.9 %collective-permute-start.7 = (bf16[256,2048]{1,0:T(8,128)(2,1)S(1)}, bf16[256,2048]{1,0:T(8,128)(2,1)S(1)}, u32[]{:S(2)}, u32[]{:S(2)}) collective-permute-start(bf16[256,2048]{1,0:T(8,128)(2,1)S(1)} %get-tuple-element.70.refs_4_.refs_2_.refs_3_.refs_0_), channel_id=1, source_target_pairs={{0,16},{8,24},{16,0},{24,8},{1,17},{9,25},{17,1},{25,9},{2,18},{10... | collective-permute-start | bytes 3145736 | tf_op jit(solution)/shard_map/ppermute | solution.py:510
  60.5 2.6 %collective-permute-start.10 = (f32[8,256]{1,0:T(8,128)S(1)}, f32[8,256]{1,0:T(8,128)S(1)}, u32[]{:S(2)}, u32[]{:S(2)}) collective-permute-start(f32[8,256]{1,0:T(8,128)S(1)} %sums_0.1.refs_3_.refs_0_), channel_id=1, source_target_pairs={{0,1},{1,0},{2,3},{3,2},{4,5},{5,4},{6,7},{7,6},{8,9},{9,8},{10,11... | collective-permute-start | bytes 24584 | tf_op jit(solution)/shard_map/ppermute | solution.py:542
  63.2 4.2 %collective-permute-start.11 = (f32[8,256]{1,0:T(8,128)S(1)}, f32[8,256]{1,0:T(8,128)S(1)}, u32[]{:S(2)}, u32[]{:S(2)}) collective-permute-start(f32[8,256]{1,0:T(8,128)S(1)} %sums_1.1.refs_2_.refs_0_), channel_id=1, source_target_pairs={{0,2},{1,3},{2,0},{3,1},{4,6},{5,7},{6,4},{7,5},{8,10},{9,11},{10,... | collective-permute-start | bytes 24584 | tf_op jit(solution)/shard_map/ppermute | solution.py:542
  67.4 4.6 %collective-permute-start.12 = (f32[8,256]{1,0:T(8,128)S(1)}, f32[8,256]{1,0:T(8,128)S(1)}, u32[]{:S(2)}, u32[]{:S(2)}) collective-permute-start(f32[8,256]{1,0:T(8,128)S(1)} %sums_2.1.refs_0_), channel_id=1, source_target_pairs={{0,4},{1,5},{2,6},{3,7},{4,0},{5,1},{6,2},{7,3},{8,12},{9,13},{10,... | collective-permute-start | bytes 24584 | tf_op jit(solution)/shard_map/ppermute | solution.py:542
  72.0 16.2 %collective-permute-start.15 = (bf16[1,128,2048]{2,1,0:T(8,128)(2,1)S(1)}, bf16[1,128,2048]{2,1,0:T(8,128)(2,1)S(1)}, u32[]{:S(2)}, u32[]{:S(2)}) collective-permute-start(bf16[1,128,2048]{2,1,0:T(8,128)(2,1)S(1)} %get-tuple-element.73.refs_5_.refs_4_.refs_2_), channel_id=1, source_target_pairs={{0,1},{1,0},{2,3},{3,2},{4,5},{5,4},{6,7},{7,6},{8,9},{9,8},{10,11... | collective-permute-start | bytes 1572872 | tf_op jit(solution)/shard_map/ppermute | solution.py:509
  72.0 15.6 %copy-start.1 = (f32[8,256]{1,0:T(8,128)}, f32[8,256]{1,0:T(8,128)S(1)}, u32[]{:S(2)}) copy-start(f32[8,256]{1,0:T(8,128)S(1)} %sums_4.1.refs_3_.refs_2_) | copy-start | bytes 24580
  87.7 2.0 %collective-permute-start.13 = (bf16[1,128,2048]{2,1,0:T(8,128)(2,1)S(1)}, bf16[1,128,2048]{2,1,0:T(8,128)(2,1)S(1)}, u32[]{:S(2)}, u32[]{:S(2)}) collective-permute-start(bf16[1,128,2048]{2,1,0:T(8,128)(2,1)S(1)} %get-tuple-element.77), channel_id=1, source_target_pairs={{0,1},{1,0},{2,3},{3,2},{4,5},{5,4},{6,7},{7,6},{8,9},{9,8},{10,11... | collective-permute-start | bytes 1572872 | tf_op jit(solution)/shard_map/ppermute | solution.py:509
  87.8 2.6 %collective-permute-start.14 = (bf16[1,128,2048]{2,1,0:T(8,128)(2,1)S(1)}, bf16[1,128,2048]{2,1,0:T(8,128)(2,1)S(1)}, u32[]{:S(2)}, u32[]{:S(2)}) collective-permute-start(bf16[1,128,2048]{2,1,0:T(8,128)(2,1)S(1)} %get-tuple-element.78), channel_id=1, source_target_pairs={{0,1},{1,0},{2,3},{3,2},{4,5},{5,4},{6,7},{7,6},{8,9},{9,8},{10,11... | collective-permute-start | bytes 1572872 | tf_op jit(solution)/shard_map/ppermute | solution.py:509
  88.3 25.2 %collective-permute-start.18 = (bf16[1,128,2048]{2,1,0:T(8,128)(2,1)S(1)}, bf16[1,128,2048]{2,1,0:T(8,128)(2,1)S(1)}, u32[]{:S(2)}, u32[]{:S(2)}) collective-permute-start(bf16[1,128,2048]{2,1,0:T(8,128)(2,1)S(1)} %get-tuple-element.75.refs_6_.refs_8_.refs_10_.refs_9_), channel_id=1, source_target_pairs={{0,1},{1,0},{2,3},{3,2},{4,5},{5,4},{6,7},{7,6},{8,9},{9,8},{10,11... | collective-permute-start | bytes 1572872 | tf_op jit(solution)/shard_map/ppermute | solution.py:509
  90.8 22.8 %collective-permute-start.19 = (bf16[128,2048]{1,0:T(8,128)(2,1)S(1)}, bf16[128,2048]{1,0:T(8,128)(2,1)S(1)}, u32[]{:S(2)}, u32[]{:S(2)}) collective-permute-start(bf16[128,2048]{1,0:T(8,128)(2,1)S(1)} %get-tuple-element.82.refs_3_.refs_7_.refs_6_.refs_9_.refs_8_.refs_5_.refs_4_.refs_2_.refs_0_), channel_id=1, source_target_pairs={{0,2},{1,3},{6,4},{7,5},{10,8},{11,9},{14,12},{15,13},{12,14},{13,... | collective-permute-start | bytes 1572872 | tf_op jit(solution)/shard_map/ppermute | solution.py:538
  102.5 11.9 %collective-permute-start.16 = (bf16[128,2048]{1,0:T(8,128)(2,1)S(1)}, bf16[128,2048]{1,0:T(8,128)(2,1)S(1)}, u32[]{:S(2)}, u32[]{:S(2)}) collective-permute-start(bf16[128,2048]{1,0:T(8,128)(2,1)S(1)} %get-tuple-element.83.refs_3_), channel_id=1, source_target_pairs={{0,16},{8,24},{16,0},{24,8},{1,17},{9,25},{17,1},{25,9},{2,18},{10... | collective-permute-start | bytes 1572872 | tf_op jit(solution)/shard_map/ppermute | solution.py:510
  104.2 10.2 %collective-permute-start.17 = (bf16[128,2048]{1,0:T(8,128)(2,1)S(1)}, bf16[128,2048]{1,0:T(8,128)(2,1)S(1)}, u32[]{:S(2)}, u32[]{:S(2)}) collective-permute-start(bf16[128,2048]{1,0:T(8,128)(2,1)S(1)} %get-tuple-element.84), channel_id=1, source_target_pairs={{0,8},{8,0},{16,24},{24,16},{1,9},{9,1},{17,25},{25,17},{2,10},{10... | collective-permute-start | bytes 1572872 | tf_op jit(solution)/shard_map/ppermute | solution.py:510
  104.6 12.3 %collective-permute-start.20 = (bf16[128,2048]{1,0:T(8,128)(2,1)S(1)}, bf16[128,2048]{1,0:T(8,128)(2,1)S(1)}, u32[]{:S(2)}, u32[]{:S(2)}) collective-permute-start(bf16[128,2048]{1,0:T(8,128)(2,1)S(1)} %pick_0.1.refs_3_), channel_id=1, source_target_pairs={{0,2},{1,3},{6,4},{7,5},{8,10},{9,11},{14,12},{15,13},{16,18},{17,... | collective-permute-start | bytes 1572872 | tf_op jit(solution)/shard_map/ppermute | solution.py:538
  113.4 3.5 %collective-permute-start.21 = (bf16[2,128,2048]{2,1,0:T(8,128)(2,1)S(1)}, bf16[2,128,2048]{2,1,0:T(8,128)(2,1)S(1)}, u32[]{:S(2)}, u32[]{:S(2)}) collective-permute-start(bf16[2,128,2048]{2,1,0:T(8,128)(2,1)S(1)} %get-tuple-element.89), channel_id=1, source_target_pairs={{0,1},{1,0},{2,3},{3,2},{4,5},{5,4},{6,7},{7,6},{8,9},{9,8},{10,11... | collective-permute-start | bytes 3145736 | tf_op jit(solution)/shard_map/ppermute | solution.py:509
  113.7 15.6 %collective-permute-start.27 = (bf16[128,2048]{1,0:T(8,128)(2,1)S(1)}, bf16[128,2048]{1,0:T(8,128)(2,1)S(1)}, u32[]{:S(2)}, u32[]{:S(2)}) collective-permute-start(bf16[128,2048]{1,0:T(8,128)(2,1)S(1)} %add_next_0.1.refs_9_.refs_10_.refs_12_.refs_11_.refs_8_.refs_6_.refs_5_.refs_3_.refs_4_.refs_1_), channel_id=1, source_target_pairs={{2,4},{3,5},{4,2},{5,3},{12,8},{13,9},{10,14},{11,15},{20,16},{21,... | collective-permute-start | bytes 1572872 | tf_op jit(solution)/shard_map/ppermute | solution.py:538
  114.4 14.6 %collective-permute-start.25 = (bf16[128,2048]{1,0:T(8,128)(2,1)S(1)}, bf16[128,2048]{1,0:T(8,128)(2,1)S(1)}, u32[]{:S(2)}, u32[]{:S(2)}) collective-permute-start(bf16[128,2048]{1,0:T(8,128)(2,1)S(1)} %get-tuple-element.88.refs_0_), channel_id=1, source_target_pairs={{0,16},{8,24},{16,0},{24,8},{1,17},{9,25},{17,1},{25,9},{2,18},{10... | collective-permute-start | bytes 1572872 | tf_op jit(solution)/shard_map/ppermute | solution.py:510
  115.1 14.2 %collective-permute-start.26 = (bf16[128,2048]{1,0:T(8,128)(2,1)S(1)}, bf16[128,2048]{1,0:T(8,128)(2,1)S(1)}, u32[]{:S(2)}, u32[]{:S(2)}) collective-permute-start(bf16[128,2048]{1,0:T(8,128)(2,1)S(1)} %get-tuple-element.97), channel_id=1, source_target_pairs={{0,8},{8,0},{16,24},{24,16},{1,9},{9,1},{17,25},{25,17},{2,10},{10... | collective-permute-start | bytes 1572872 | tf_op jit(solution)/shard_map/ppermute | solution.py:510
  119.6 1.6 collective-permute-start.22
  119.7 1.9 %collective-permute-start.23 = (bf16[1,128,1024]{2,1,0:T(8,128)(2,1)S(1)}, bf16[1,128,1024]{2,1,0:T(8,128)(2,1)S(1)}, u32[]{:S(2)}, u32[]{:S(2)}) collective-permute-start(bf16[1,128,1024]{2,1,0:T(8,128)(2,1)S(1)} %get-tuple-element.94), channel_id=1, source_target_pairs={{0,1},{1,0},{2,3},{3,2},{4,5},{5,4},{6,7},{7,6},{8,9},{9,8},{10,11... | collective-permute-start | bytes 786440 | tf_op jit(solution)/shard_map/ppermute | solution.py:509
  122.0 17.3 %collective-permute-start.30 = (bf16[128,2048]{1,0:T(8,128)(2,1)S(1)}, bf16[128,2048]{1,0:T(8,128)(2,1)S(1)}, u32[]{:S(2)}, u32[]{:S(2)}) collective-permute-start(bf16[128,2048]{1,0:T(8,128)(2,1)S(1)} %get-tuple-element.95.refs_0_.refs_11_.refs_13_.refs_10_.refs_8_.refs_9_.refs_3_), channel_id=1, source_target_pairs={{2,0},{3,1},{6,4},{7,5},{4,6},{5,7},{0,2},{1,3},{8,10},{9,11},{14,... | collective-permute-start | bytes 1572872 | tf_op jit(solution)/shard_map/ppermute | solution.py:538
  127.0 23.5 %collective-permute-start.24 = (bf16[128,2048]{1,0:T(8,128)(2,1)S(1)}, bf16[128,2048]{1,0:T(8,128)(2,1)S(1)}, u32[]{:S(2)}, u32[]{:S(2)}) collective-permute-start(bf16[128,2048]{1,0:T(8,128)(2,1)S(1)} %release_n1.1.refs_9_.refs_11_.refs_8_.refs_6_.refs_7_.refs_10_.refs_0_), channel_id=1, source_target_pairs={{0,2},{1,3},{6,4},{7,5},{10,8},{11,9},{14,12},{15,13},{12,14},{13,... | collective-permute-start | bytes 1572872 | tf_op jit(solution)/shard_map/ppermute | solution.py:538
  131.6 26.3 %copy-start.2 = (f32[8,256]{1,0:T(8,128)S(1)}, f32[8,256]{1,0:T(8,128)}, u32[]{:S(2)}) copy-start(f32[8,256]{1,0:T(8,128)} %copy-done.1) | copy-start | bytes 24580
  131.6 1.6 collective-permute-start.28
  131.7 1.9 %collective-permute-start.29 = (bf16[1,128,1024]{2,1,0:T(8,128)(2,1)S(1)}, bf16[1,128,1024]{2,1,0:T(8,128)(2,1)S(1)}, u32[]{:S(2)}, u32[]{:S(2)}) collective-permute-start(bf16[1,128,1024]{2,1,0:T(8,128)(2,1)S(1)} %get-tuple-element.100), channel_id=1, source_target_pairs={{0,1},{1,0},{2,3},{3,2},{4,5},{5,4},{6,7},{7,6},{8,9},{9,8},{10,11... | collective-permute-start | bytes 786440 | tf_op jit(solution)/shard_map/ppermute | solution.py:509
  133.9 28.7 %collective-permute-start.32 = (bf16[128,2048]{1,0:T(8,128)(2,1)S(1)}, bf16[128,2048]{1,0:T(8,128)(2,1)S(1)}, u32[]{:S(2)}, u32[]{:S(2)}) collective-permute-start(bf16[128,2048]{1,0:T(8,128)(2,1)S(1)} %get-tuple-element.102.refs_12_.refs_10_.refs_11_.refs_0_.refs_13_.refs_3_), channel_id=1, source_target_pairs={{2,0},{3,1},{6,4},{7,5},{4,6},{5,7},{0,2},{1,3},{8,10},{9,11},{14,... | collective-permute-start | bytes 1572872 | tf_op jit(solution)/shard_map/ppermute | solution.py:538
  139.4 23.2 %collective-permute-start.33 = (bf16[128,2048]{1,0:T(8,128)(2,1)S(1)}, bf16[128,2048]{1,0:T(8,128)(2,1)S(1)}, u32[]{:S(2)}, u32[]{:S(2)}) collective-permute-start(bf16[128,2048]{1,0:T(8,128)(2,1)S(1)} %add_opposite_0.1.refs_13_.refs_14_.refs_6_), channel_id=1, source_target_pairs={{4,0},{5,1},{2,6},{3,7},{10,12},{11,13},{12,10},{13,11},{18,20},{1... | collective-permute-start | bytes 1572872 | tf_op jit(solution)/shard_map/ppermute | solution.py:538
  150.6 13.4 %collective-permute-start.31 = (bf16[128,2048]{1,0:T(8,128)(2,1)S(1)}, bf16[128,2048]{1,0:T(8,128)(2,1)S(1)}, u32[]{:S(2)}, u32[]{:S(2)}) collective-permute-start(bf16[128,2048]{1,0:T(8,128)(2,1)S(1)} %add_next_1.1.refs_15_.refs_11_.refs_1_), channel_id=1, source_target_pairs={{2,4},{3,5},{4,2},{5,3},{12,8},{13,9},{10,14},{11,15},{20,16},{21,... | collective-permute-start | bytes 1572872 | tf_op jit(solution)/shard_map/ppermute | solution.py:538
  151.3 20.8 %collective-permute-start.35 = (bf16[128,2048]{1,0:T(8,128)(2,1)S(1)}, bf16[128,2048]{1,0:T(8,128)(2,1)S(1)}, u32[]{:S(2)}, u32[]{:S(2)}) collective-permute-start(bf16[128,2048]{1,0:T(8,128)(2,1)S(1)} %pick_1.1.refs_2_), channel_id=1, source_target_pairs={{0,2},{1,3},{6,4},{7,5},{8,10},{9,11},{14,12},{15,13},{16,18},{17,... | collective-permute-start | bytes 1572872 | tf_op jit(solution)/shard_map/ppermute | solution.py:538
  157.9 6.1 %collective-permute-start.36 = (f32[8,256]{1,0:T(8,128)S(1)}, f32[8,256]{1,0:T(8,128)S(1)}, u32[]{:S(2)}, u32[]{:S(2)}) collective-permute-start(f32[8,256]{1,0:T(8,128)S(1)} %release_sums.1), channel_id=1, source_target_pairs={{0,0},{1,1},{8,2},{9,3},{16,4},{17,5},{24,6},{25,7},{2,8},{3,9},{1... | collective-permute-start | bytes 24584 | tf_op jit(solution)/shard_map/ppermute | solution.py:605
  162.8 16.3 %collective-permute-start.34 = (bf16[128,2048]{1,0:T(8,128)(2,1)S(1)}, bf16[128,2048]{1,0:T(8,128)(2,1)S(1)}, u32[]{:S(2)}, u32[]{:S(2)}) collective-permute-start(bf16[128,2048]{1,0:T(8,128)(2,1)S(1)} %add_opposite_1.1.refs_16_.refs_6_), channel_id=1, source_target_pairs={{4,0},{5,1},{2,6},{3,7},{10,12},{11,13},{12,10},{13,11},{18,20},{1... | collective-permute-start | bytes 1572872 | tf_op jit(solution)/shard_map/ppermute | solution.py:538
